TPU v7x, 128 devices: a whole 4x4x4 slice. The times are simulated.
128 devices in a mesh: dp: 4 (over y), expert: 8 (over x, z_lo), tensor: 4 (over z_hi, core).
Axes of the slice: x: 4, y: 4, z: 4 (z_hi: 2, z_lo: 2; z = z_hi * 2 + z_lo), core: 2. Of those that a mesh axis runs over, the one named last changes fastest.
Arguments:
- tokens: bfloat16 [4, 1024, 2048], P('dp', 'expert'), may hold values from -6 to 6
- cotangent: bfloat16 [4, 1024, 2048], P('dp', 'expert'), may hold values from -6 to 6
- doc_lengths: int32 [4, 8], P('dp'), may hold values from 1 to 897, as said below
- att_routes: int32 [4, 1024, 2], P('dp', 'expert'), may hold values from 0 to 7, all different within a row; in each aligned block of 128 rows (0 to 127, 128 to 255, ..., all dimensions but the last counted through in order) at most 40 rows name the same one
- att_gates: float32 [4, 1024, 2], P('dp', 'expert'), may hold values from 0.25 to 0.75
- ffn_routes: int32 [4, 1024, 2], P('dp', 'expert'), may hold values from 0 to 7, all different within a row; in each aligned block of 128 rows (0 to 127, 128 to 255, ..., all dimensions but the last counted through in order) at most 40 rows name the same one
- ffn_gates: float32 [4, 1024, 2], P('dp', 'expert'), may hold values from 0.25 to 0.75
- kv_weight: bfloat16 [2048, 2, 2048], P(('dp', 'expert'), None, 'tensor'), may hold values from -0.125 to 0.125
- query_weight: bfloat16 [8, 2048, 2048], P(None, ('dp', 'expert'), 'tensor'), may hold values from -0.125 to 0.125
- out_weight: bfloat16 [8, 2048, 2048], P(None, 'tensor', ('dp', 'expert')), may hold values from -0.75 to 0.75
- attn_gain: bfloat16 [2048], P(('dp', 'expert')), may hold values from 0.5 to 1.5
- ffn_gain: bfloat16 [2048], P(('dp', 'expert')), may hold values from 0.5 to 1.5
- gate_weight: bfloat16 [8, 2048, 5632], P('expert', 'dp', 'tensor'), may hold values from -0.125 to 0.125
- up_weight: bfloat16 [8, 2048, 5632], P('expert', 'dp', 'tensor'), may hold values from -0.125 to 0.125
- down_weight: bfloat16 [8, 5632, 2048], P('expert', 'tensor', 'dp'), may hold values from -0.078125 to 0.078125
Outputs:
- output: bfloat16 [4, 1024, 2048], P('dp', 'expert')
- input_grad: float32 [4, 1024, 2048], P('dp', 'expert')
- kv_weight_grad: float32 [2048, 2, 2048], P(('dp', 'expert'), None, 'tensor')
- query_weight_grad: float32 [8, 2048, 2048], P(None, ('dp', 'expert'), 'tensor')
- out_weight_grad: float32 [8, 2048, 2048], P(None, 'tensor', ('dp', 'expert'))
- attn_gain_grad: float32 [2048], P(('dp', 'expert'))
- ffn_gain_grad: float32 [2048], P(('dp', 'expert'))
- gate_weight_grad: float32 [8, 2048, 5632], P('expert', 'dp', 'tensor')
- up_weight_grad: float32 [8, 2048, 5632], P('expert', 'dp', 'tensor')
- down_weight_grad: float32 [8, 5632, 2048], P('expert', 'tensor', 'dp')
Inputs may be any that keep to these rules, and one draw needn't show every extreme that they name: `doc_lengths`: the 8 document lengths of a sequence are positive and sum to 1024; one of them is exactly 1024 - 1024 // 8 + 1. `att_routes`: each token names 2 different maps; in each aligned block of 128 positions of a sequence no map is named by more than 40 tokens, a bound that some block reaches. `ffn_routes`: each token names 2 different experts; in each aligned block of 128 positions of a sequence no expert is named by more than 40 tokens, a bound that some block reaches.
All inputs are finite; a program needn't handle non-finite values.
Results may differ from a plain program's by a relative error of at most 0.028.
Values may be sent and summed in bfloat16 or wider, within the bound.
A program may use at most 256 MiB of HBM per device.

v0:
```python
import jax
import jax.numpy as jnp
from jax import lax
from jax.sharding import PartitionSpec as P

HD = 128
ATT_EXP = 8
TOPK = 2
EXP_DEV = 1


EPSILON = 1e-06


def rope_tables(positions):
    half_dim = HD // 2
    freqs = 10000.0 ** (-(jnp.arange(half_dim).astype(jnp.float32) * 2.0 / HD))
    angles = positions[:, None] * freqs[None, :]
    return (jnp.cos(angles), jnp.sin(angles))


def rotate(values, cos_tab, sin_tab):
    half_dim = values.shape[-1] // 2
    first_half = values[..., :half_dim]
    second_half = values[..., half_dim:]
    return jnp.concatenate(
        [
            first_half * cos_tab - second_half * sin_tab,
            second_half * cos_tab + first_half * sin_tab,
        ],
        -1,
    )


def segment_ids(lengths, length_all):
    ends = jnp.cumsum(lengths, -1, dtype=jnp.int32)
    places = jnp.arange(length_all, dtype=jnp.int32)
    return jnp.sum((ends[..., None, :] <= places[:, None]).astype(jnp.int32), -1)


def slot_maps(routes, expert_count, capacity):
    blocks, block_len, choices = routes.shape
    row_len = block_len * choices
    flat_routes = routes.reshape(blocks, row_len)
    onehot = (
        flat_routes[:, :, None] == jnp.arange(expert_count, dtype=jnp.int32)[None, None, :]
    ).astype(jnp.int32)
    position = jnp.sum((jnp.cumsum(onehot, axis=1, dtype=jnp.int32) - 1) * onehot, -1)
    block_base = (jnp.arange(blocks, dtype=jnp.int32) * capacity)[:, None]
    flat_slot = (flat_routes * (blocks * capacity) + block_base + position).reshape(-1)
    source = jnp.full((expert_count * blocks * capacity,), blocks * row_len, jnp.int32)
    source = source.at[flat_slot].set(jnp.arange(blocks * row_len, dtype=jnp.int32))
    return (flat_slot, source)


def take_rows(rows, source):
    padded = jnp.concatenate([rows, jnp.zeros((1,) + rows.shape[1:], rows.dtype)], 0)
    return padded[source]


def regroup(received, owners, local_count):
    tail = received.shape[2:]
    return (
        received.reshape((owners, local_count, -1) + tail)
        .swapaxes(0, 1)
        .reshape((local_count, -1) + tail)
    )


def ungroup(results, owners, local_count):
    tail = results.shape[2:]
    return (
        results.reshape((local_count, owners, -1) + tail)
        .swapaxes(0, 1)
        .reshape((owners, -1) + tail)
    )


def per_device(
    tokens,
    cotangent,
    doc_lengths,
    att_routes,
    att_gates,
    ffn_routes,
    ffn_gates,
    kv_weight,
    query_weight,
    out_weight,
    attn_gain,
    ffn_gain,
    gate_weight,
    up_weight,
    down_weight,
):
    seq_count, group_len, model_width = tokens.shape
    token_count = seq_count * group_len
    row_count = token_count * TOPK
    owners = lax.axis_size("expert")
    expert_count = EXP_DEV * owners
    att_cap = min(group_len, group_len * TOPK * 5 // (4 * ATT_EXP))
    ffn_cap = min(group_len, group_len * TOPK * 5 // (4 * expert_count))
    kv_full, query_full, out_full, gain_one, gain_two = (
        lax.all_gather(kv_weight, ("dp", "expert"), axis=0, tiled=True),
        lax.all_gather(query_weight, ("dp", "expert"), axis=1, tiled=True),
        lax.all_gather(out_weight, ("dp", "expert"), axis=2, tiled=True),
        lax.all_gather(attn_gain, ("dp", "expert"), axis=0, tiled=True),
        lax.all_gather(ffn_gain, ("dp", "expert"), axis=0, tiled=True),
    )
    gate_full, up_full, down_full = (
        lax.all_gather(gate_weight, "dp", axis=1, tiled=True),
        lax.all_gather(up_weight, "dp", axis=1, tiled=True),
        lax.all_gather(down_weight, "dp", axis=2, tiled=True),
    )
    head_width = kv_full.shape[2]
    local_heads = head_width // HD
    gain_one = gain_one.astype(jnp.float32)
    gain_two = gain_two.astype(jnp.float32)
    inputs = tokens.reshape(token_count, model_width).astype(jnp.float32)
    inv_one = lax.rsqrt(jnp.mean(inputs * inputs, -1, keepdims=True) + EPSILON)
    normed = (inputs * inv_one * gain_one).astype(jnp.bfloat16)
    projected = jnp.einsum("td,dcf->tcf", normed, kv_full, preferred_element_type=jnp.float32)
    first_pos = lax.axis_index("expert") * group_len
    query_pos = first_pos + jnp.arange(group_len, dtype=jnp.int32)
    cos_tab, sin_tab = rope_tables(query_pos.astype(jnp.float32))
    key_own = rotate(
        projected[:, 0].reshape(seq_count, group_len, local_heads, HD),
        cos_tab[None, :, None],
        sin_tab[None, :, None],
    )
    pair_own = jnp.stack(
        [
            key_own.reshape(seq_count, group_len, head_width),
            projected[:, 1].reshape(seq_count, group_len, head_width),
        ],
        2,
    ).astype(jnp.bfloat16)
    pair_all = lax.all_gather(pair_own, "expert", axis=1, tiled=True)
    seq_len = pair_all.shape[1]
    key_all = pair_all[:, :, 0].reshape(seq_count, seq_len, local_heads, HD)
    value_all = pair_all[:, :, 1].reshape(seq_count, seq_len, local_heads, HD)
    seg_all = segment_ids(doc_lengths, seq_len)
    seg_own = lax.dynamic_slice_in_dim(seg_all, first_pos, group_len, 1)
    key_pos = jnp.arange(seq_len, dtype=jnp.int32)
    visible = (seg_own[:, :, None] == seg_all[:, None, :]) & (
        key_pos[None, None, :] <= query_pos[None, :, None]
    )
    visible = visible[:, None, None]
    att_slot, att_source = slot_maps(att_routes, ATT_EXP, att_cap)
    att_token = jnp.where(att_source < row_count, att_source // TOPK, token_count)
    x_buffer = take_rows(normed, att_token).reshape(ATT_EXP, -1, model_width)
    q_buffer = jnp.einsum("acd,adh->ach", x_buffer, query_full, preferred_element_type=jnp.float32)
    queries = q_buffer.reshape(-1, head_width)[att_slot].reshape(
        seq_count, group_len, TOPK, local_heads, HD
    )
    queries = rotate(queries, cos_tab[None, :, None, None], sin_tab[None, :, None, None]).astype(
        jnp.bfloat16
    )
    scale = HD ** (-0.5)
    scores = (
        jnp.einsum("stjhd,skhd->shjtk", queries, key_all, preferred_element_type=jnp.float32)
        * scale
    )
    scores = jnp.where(visible, scores, -1e30)
    row_top = jnp.max(scores, -1, keepdims=True)
    shifted = jnp.exp(scores - row_top)
    row_total = jnp.sum(shifted, -1, keepdims=True)
    weights = (shifted / row_total).astype(jnp.bfloat16)
    log_sum = row_top + jnp.log(row_total)
    mixed = jnp.einsum("shjtk,skhd->stjhd", weights, value_all, preferred_element_type=jnp.float32)
    mixed = mixed.astype(jnp.bfloat16).reshape(row_count, head_width)
    o_buffer = take_rows(mixed, att_source).reshape(ATT_EXP, -1, head_width)
    z_buffer = jnp.einsum("ach,ahd->acd", o_buffer, out_full, preferred_element_type=jnp.float32)
    att_gate = att_gates.reshape(token_count, TOPK)
    branch = z_buffer.reshape(-1, model_width)[att_slot].reshape(token_count, TOPK, model_width)
    attention = lax.psum(jnp.sum(branch * att_gate[:, :, None], 1), "tensor")
    state = inputs + attention
    inv_two = lax.rsqrt(jnp.mean(state * state, -1, keepdims=True) + EPSILON)
    normed_two = (state * inv_two * gain_two).astype(jnp.bfloat16)
    ffn_slot, ffn_source = slot_maps(ffn_routes, expert_count, ffn_cap)
    ffn_token = jnp.where(ffn_source < row_count, ffn_source // TOPK, token_count)
    ffn_gate = ffn_gates.reshape(token_count, TOPK)
    upstream = cotangent.reshape(token_count, model_width).astype(jnp.float32)
    grad_rows = (
        (upstream[:, None, :] * ffn_gate[:, :, None])
        .astype(jnp.bfloat16)
        .reshape(row_count, model_width)
    )
    send_rows = take_rows(normed_two, ffn_token).reshape(owners, -1, model_width)
    send_grads = take_rows(grad_rows, ffn_source).reshape(owners, -1, model_width)
    got_rows, got_grads = (
        lax.all_to_all(send_rows, "expert", split_axis=0, concat_axis=0, tiled=True),
        lax.all_to_all(send_grads, "expert", split_axis=0, concat_axis=0, tiled=True),
    )
    expert_in = regroup(got_rows, owners, EXP_DEV)
    expert_grad = regroup(got_grads, owners, EXP_DEV)
    gate_act = jnp.einsum("ecd,edf->ecf", expert_in, gate_full, preferred_element_type=jnp.float32)
    up_act = jnp.einsum("ecd,edf->ecf", expert_in, up_full, preferred_element_type=jnp.float32)
    hidden = (jax.nn.silu(gate_act) * up_act).astype(jnp.bfloat16)
    expert_out = jnp.einsum("ecf,efd->ecd", hidden, down_full, preferred_element_type=jnp.float32)
    returned = lax.all_to_all(
        ungroup(expert_out, owners, EXP_DEV).astype(jnp.bfloat16),
        "expert",
        split_axis=0,
        concat_axis=0,
        tiled=True,
    ).astype(jnp.float32)
    ffn_rows = returned.reshape(-1, model_width)[ffn_slot].reshape(token_count, TOPK, model_width)
    ffn_part = jnp.sum(ffn_rows * ffn_gate[:, :, None], 1)
    sigma = jax.nn.sigmoid(gate_act)
    d_down = jnp.einsum("ecf,ecd->efd", hidden, expert_grad, preferred_element_type=jnp.float32)
    d_hidden = jnp.einsum(
        "ecd,efd->ecf", expert_grad, down_full, preferred_element_type=jnp.float32
    )
    d_gate = (d_hidden * up_act * sigma * (1.0 + gate_act * (1.0 - sigma))).astype(jnp.bfloat16)
    d_up = (d_hidden * gate_act * sigma).astype(jnp.bfloat16)
    d_gate_w = jnp.einsum("ecd,ecf->edf", expert_in, d_gate, preferred_element_type=jnp.float32)
    d_up_w = jnp.einsum("ecd,ecf->edf", expert_in, d_up, preferred_element_type=jnp.float32)
    d_expert_in = jnp.einsum("ecf,edf->ecd", d_gate, gate_full, preferred_element_type=jnp.float32)
    d_expert_in = d_expert_in + jnp.einsum(
        "ecf,edf->ecd", d_up, up_full, preferred_element_type=jnp.float32
    )
    grad_back = lax.all_to_all(
        ungroup(d_expert_in, owners, EXP_DEV), "expert", split_axis=0, concat_axis=0, tiled=True
    )
    grad_norm_rows = grad_back.reshape(-1, model_width)[ffn_slot].reshape(
        token_count, TOPK, model_width
    )
    ffn_total, d_normed_two = lax.psum((ffn_part, jnp.sum(grad_norm_rows, 1)), "tensor")
    output = (state + ffn_total).astype(jnp.bfloat16).reshape(seq_count, group_len, model_width)
    gate_grad, up_grad, down_grad = (
        lax.psum_scatter(
            d_gate_w.astype(jnp.bfloat16), "dp", scatter_dimension=1, tiled=True
        ).astype(jnp.float32),
        lax.psum_scatter(d_up_w.astype(jnp.bfloat16), "dp", scatter_dimension=1, tiled=True).astype(
            jnp.float32
        ),
        lax.psum_scatter(d_down.astype(jnp.bfloat16), "dp", scatter_dimension=2, tiled=True).astype(
            jnp.float32
        ),
    )
    scaled_two = gain_two * d_normed_two
    d_gain_two = jnp.sum(d_normed_two * state * inv_two, 0)
    d_state = (
        upstream
        + inv_two * scaled_two
        - state * inv_two**3 * jnp.mean(state * scaled_two, -1, keepdims=True)
    )
    d_branch = (
        (d_state[:, None, :] * att_gate[:, :, None])
        .astype(jnp.bfloat16)
        .reshape(row_count, model_width)
    )
    dz_buffer = take_rows(d_branch, att_source).reshape(ATT_EXP, -1, model_width)
    do_buffer = jnp.einsum("acd,ahd->ach", dz_buffer, out_full, preferred_element_type=jnp.float32)
    d_mixed = (
        do_buffer.reshape(-1, head_width)[att_slot]
        .astype(jnp.bfloat16)
        .reshape(seq_count, group_len, TOPK, local_heads, HD)
    )
    scores = (
        jnp.einsum("stjhd,skhd->shjtk", queries, key_all, preferred_element_type=jnp.float32)
        * scale
    )
    probs = jnp.where(visible, jnp.exp(scores - log_sum), 0.0)
    d_probs = jnp.einsum(
        "stjhd,skhd->shjtk", d_mixed, value_all, preferred_element_type=jnp.float32
    )
    delta = jnp.sum(probs * d_probs, -1, keepdims=True)
    d_scores = (probs * (d_probs - delta)).astype(jnp.bfloat16)
    d_queries = (
        jnp.einsum("shjtk,skhd->stjhd", d_scores, key_all, preferred_element_type=jnp.float32)
        * scale
    )
    d_keys = (
        jnp.einsum("shjtk,stjhd->skhd", d_scores, queries, preferred_element_type=jnp.float32)
        * scale
    )
    d_values = jnp.einsum(
        "shjtk,stjhd->skhd", probs.astype(jnp.bfloat16), d_mixed, preferred_element_type=jnp.float32
    )
    d_pair = jnp.stack(
        [
            d_keys.reshape(seq_count, seq_len, head_width),
            d_values.reshape(seq_count, seq_len, head_width),
        ],
        2,
    )
    d_pair_own = lax.psum_scatter(d_pair, "expert", scatter_dimension=1, tiled=True)
    d_key_own = rotate(
        d_pair_own[:, :, 0].reshape(seq_count, group_len, local_heads, HD),
        cos_tab[None, :, None],
        -sin_tab[None, :, None],
    )
    d_proj = jnp.stack(
        [
            d_key_own.reshape(token_count, head_width),
            d_pair_own[:, :, 1].reshape(token_count, head_width),
        ],
        1,
    ).astype(jnp.bfloat16)
    d_norm_kv = jnp.einsum("tcf,dcf->td", d_proj, kv_full, preferred_element_type=jnp.float32)
    d_query_raw = (
        rotate(d_queries, cos_tab[None, :, None, None], -sin_tab[None, :, None, None])
        .astype(jnp.bfloat16)
        .reshape(row_count, head_width)
    )
    dq_buffer = take_rows(d_query_raw, att_source).reshape(ATT_EXP, -1, head_width)
    dx_buffer = jnp.einsum(
        "ach,adh->acd", dq_buffer, query_full, preferred_element_type=jnp.float32
    )
    d_norm_q = jnp.sum(
        dx_buffer.reshape(-1, model_width)[att_slot].reshape(token_count, TOPK, model_width), 1
    )
    d_normed_one = lax.psum((d_norm_kv + d_norm_q).astype(jnp.bfloat16), "tensor").astype(
        jnp.float32
    )
    scaled_one = gain_one * d_normed_one
    d_gain_one = jnp.sum(d_normed_one * inputs * inv_one, 0)
    input_grad = (
        d_state
        + inv_one * scaled_one
        - inputs * inv_one**3 * jnp.mean(inputs * scaled_one, -1, keepdims=True)
    )
    input_grad = input_grad.reshape(seq_count, group_len, model_width)
    d_out_w = jnp.einsum("ach,acd->ahd", o_buffer, dz_buffer, preferred_element_type=jnp.float32)
    d_query_w = jnp.einsum("acd,ach->adh", x_buffer, dq_buffer, preferred_element_type=jnp.float32)
    d_kv_w = jnp.einsum("td,tcf->dcf", normed, d_proj, preferred_element_type=jnp.float32)
    kv_grad, query_grad, out_grad, gain_one_grad, gain_two_grad = (
        lax.psum_scatter(
            d_kv_w.astype(jnp.bfloat16), ("dp", "expert"), scatter_dimension=0, tiled=True
        ).astype(jnp.float32),
        lax.psum_scatter(
            d_query_w.astype(jnp.bfloat16), ("dp", "expert"), scatter_dimension=1, tiled=True
        ).astype(jnp.float32),
        lax.psum_scatter(
            d_out_w.astype(jnp.bfloat16), ("dp", "expert"), scatter_dimension=2, tiled=True
        ).astype(jnp.float32),
        lax.psum_scatter(
            d_gain_one.astype(jnp.bfloat16), ("dp", "expert"), scatter_dimension=0, tiled=True
        ).astype(jnp.float32),
        lax.psum_scatter(
            d_gain_two.astype(jnp.bfloat16), ("dp", "expert"), scatter_dimension=0, tiled=True
        ).astype(jnp.float32),
    )
    return (
        output,
        input_grad,
        kv_grad,
        query_grad,
        out_grad,
        gain_one_grad,
        gain_two_grad,
        gate_grad,
        up_grad,
        down_grad,
    )


def solution(mesh):
    in_specs = (
        P("dp", "expert", None),
        P("dp", "expert", None),
        P("dp", None),
        P("dp", "expert", None),
        P("dp", "expert", None),
        P("dp", "expert", None),
        P("dp", "expert", None),
        P(("dp", "expert"), None, "tensor"),
        P(None, ("dp", "expert"), "tensor"),
        P(None, "tensor", ("dp", "expert")),
        P(("dp", "expert")),
        P(("dp", "expert")),
        P("expert", "dp", "tensor"),
        P("expert", "dp", "tensor"),
        P("expert", "tensor", "dp"),
    )
    out_specs = (
        P("dp", "expert", None),
        P("dp", "expert", None),
        P(("dp", "expert"), None, "tensor"),
        P(None, ("dp", "expert"), "tensor"),
        P(None, "tensor", ("dp", "expert")),
        P(("dp", "expert")),
        P(("dp", "expert")),
        P("expert", "dp", "tensor"),
        P("expert", "dp", "tensor"),
        P("expert", "tensor", "dp"),
    )
    return jax.shard_map(
        per_device, mesh=mesh, in_specs=in_specs, out_specs=out_specs, check_vma=False
    )
```

profile of v0, /device:TPU:1, one launch (start us, length us, event | category | flops | bytes accessed | tf_op | source)
XLA Modules:
  0.0 2587.9 jit_solution(9728092506507985602)
XLA Ops:
  13.4 74.0 %all-reduce.12 = (bf16[2048]{0:T(1024)(128)(2,1)S(1)}, bf16[2048]{0:T(1024)(128)(2,1)}) all-reduce(bf16[2048]{0:T(1024)(128)(2,1)S(1)} %dynamic-update-slice, bf16[2048]{0:T(1024)(128)(2,1)S(1)} %dynamic-update-slice.1), channel_id=1, replica_groups=mesh['dp'=4,'expert'=8,'tensor'=4] {'dp','expert'}, use_global_device_ids=true, to_apply=%add.6 | all-reduce | flops 4096 | bytes 16384
  91.5 63.6 %all-gather.8.cloned.1.call-done = bf16[2048,2,512]{2,0,1:T(8,128)(2,1)} async-done(((bf16[64,2,512]{2,0,1:T(8,128)(2,1)}), bf16[2048,2,512]{2,0,1:T(8,128)(2,1)}) %all-gather.8.cloned.1.call-update) | async-done | bytes 4194320 | tf_op jit(solution)/shard_map/all_gather | solution.py:104
  168.2 58.7 %all-gather.10.cloned.1.call-done = bf16[1,1024,2,512]{3,1,2,0:T(8,128)(2,1)} async-done(((bf16[1,128,2,512]{3,1,2,0:T(8,128)(2,1)}), bf16[1,1024,2,512]{3,1,2,0:T(8,128)(2,1)}) %all-gather.10.cloned.1.call-update) | async-done | bytes 2097168 | tf_op jit(solution)/shard_map/all_gather | solution.py:138
  234.8 356.5 %all-gather.12.cloned.1.call-done = bf16[8,2048,512]{2,1,0:T(8,128)(2,1)} async-done(((bf16[8,64,512]{2,1,0:T(8,128)(2,1)}), bf16[8,2048,512]{2,1,0:T(8,128)(2,1)}) %all-gather.12.cloned.1.call-update) | async-done | bytes 16777232 | tf_op jit(solution)/shard_map/all_gather | solution.py:105
  591.2 8.7 fusion.100
  608.4 347.4 %all-gather.14.cloned.1.call-done = bf16[8,512,2048]{1,2,0:T(8,128)(2,1)} async-done(((bf16[8,512,64]{1,2,0:T(8,128)(2,1)}), bf16[8,512,2048]{1,2,0:T(8,128)(2,1)}) %all-gather.14.cloned.1.call-update) | async-done | bytes 16777232 | tf_op jit(solution)/shard_map/all_gather | solution.py:106
  955.8 10.7 fusion.101
  995.1 42.1 %all-reduce.17.cloned.1.call-done = f32[128,2048]{1,0:T(8,128)} async-done(((f32[128,2048]{1,0:T(8,128)}), f32[128,2048]{1,0:T(8,128)}) %all-reduce.17.cloned.1.call-update) | async-done | bytes 1048592 | tf_op jit(solution)/shard_map/psum | solution.py:176
  1053.8 51.6 %all-gather.16.cloned.1.call-done = bf16[1,2048,1408]{2,1,0:T(8,128)(2,1)} async-done(((bf16[1,512,1408]{2,1,0:T(8,128)(2,1)}), bf16[1,2048,1408]{2,1,0:T(8,128)(2,1)}) %all-gather.16.cloned.1.call-update) | async-done | bytes 5767184 | tf_op jit(solution)/shard_map/all_gather | solution.py:111
  1105.4 6.6 fusion.13
  1112.0 56.8 %all-gather.18.cloned.1.call-done = bf16[1,2048,1408]{2,1,0:T(8,128)(2,1)} async-done(((bf16[1,512,1408]{2,1,0:T(8,128)(2,1)}), bf16[1,2048,1408]{2,1,0:T(8,128)(2,1)}) %all-gather.18.cloned.1.call-update) | async-done | bytes 5767184 | tf_op jit(solution)/shard_map/all_gather | solution.py:112
  1168.8 7.5 multiply_convert_fusion.4
  1193.2 6.4 fusion.22
  1199.6 7.7 all-to-all-done.1
  1231.5 17.5 all-to-all-done.3
  1261.4 57.7 %all-reduce.21.cloned.1.call-done = (f32[128,2048]{1,0:T(8,128)}, f32[128,2048]{1,0:T(8,128)}) async-done(((f32[128,2048]{1,0:T(8,128)}, f32[128,2048]{1,0:T(8,128)}), (f32[128,2048]{1,0:T(8,128)}, f32[128,2048]{1,0:T(8,128)})) %all-reduce.21.cloned.1.call-update) | async-done | bytes 2097168 | tf_op jit(solution)/shard_map/psum | solution.py:229
  1333.9 9.1 fusion.102
  1364.5 7.4 fusion
  1372.0 7.5 fusion.1
  1379.5 7.3 fusion.2
  1392.1 10.8 fusion.103
  1412.1 41.6 %reduce-scatter.8.cloned.1.call-done = f32[1,128,2,512]{3,1,2,0:T(8,128)} async-done(((f32[1,1024,2,512]{3,1,2,0:T(8,128)}), f32[1,128,2,512]{3,1,2,0:T(8,128)}) %reduce-scatter.8.cloned.1.call-update) | async-done | bytes 524304 | tf_op jit(solution)/shard_map/reduce_scatter | solution.py:289
  1465.6 8.1 convolution_convert_fusion
  1475.1 8.2 convolution_convert_fusion.1
  1484.0 32.7 %reduce-scatter.16.cloned.1.call-done = bf16[1,512,1408]{2,1,0:T(8,128)(2,1)} async-done(((bf16[1,2048,1408]{2,1,0:T(8,128)(2,1)}), bf16[1,512,1408]{2,1,0:T(8,128)(2,1)}) %reduce-scatter.16.cloned.1.call-update) | async-done | bytes 1441808 | tf_op jit(solution)/shard_map/reduce_scatter | solution.py:232
  1519.9 58.7 %reduce-scatter.18.cloned.1.call-done = bf16[1,512,1408]{2,1,0:T(8,128)(2,1)} async-done(((bf16[1,2048,1408]{2,1,0:T(8,128)(2,1)}), bf16[1,512,1408]{2,1,0:T(8,128)(2,1)}) %reduce-scatter.18.cloned.1.call-update) | async-done | bytes 1441808 | tf_op jit(solution)/shard_map/reduce_scatter | solution.py:235
  1581.8 58.5 %reduce-scatter.20.cloned.1.call-done = bf16[1,1408,512]{2,1,0:T(8,128)(2,1)} async-done(((bf16[1,1408,2048]{2,1,0:T(8,128)(2,1)}), bf16[1,1408,512]{2,1,0:T(8,128)(2,1)}) %reduce-scatter.20.cloned.1.call-update) | async-done | bytes 1441808 | tf_op jit(solution)/shard_map/reduce_scatter | solution.py:238
  1643.6 42.1 %all-reduce.19.cloned.1.call-done = bf16[128,2048]{1,0:T(8,128)(2,1)} async-done(((bf16[128,2048]{1,0:T(8,128)(2,1)}), bf16[128,2048]{1,0:T(8,128)(2,1)}) %all-reduce.19.cloned.1.call-update) | async-done | bytes 524304 | tf_op jit(solution)/shard_map/psum | solution.py:315
  1687.1 71.0 %all-reduce.11 = (bf16[2048]{0:T(1024)(128)(2,1)S(1)}, bf16[2048]{0:T(1024)(128)(2,1)S(1)}) all-reduce(bf16[2048]{0:T(1024)(128)(2,1)S(1)} %get-tuple-element.52, bf16[2048]{0:T(1024)(128)(2,1)S(1)} %copy-done.38), channel_id=6, replica_groups=mesh['dp'=4,'expert'=8,'tensor'=4] {'dp','expert'}, use_global_device_ids=true, to_apply=%region_30.31.clone | all-reduce | flops 4096 | bytes 16384
  1761.6 71.3 %reduce-scatter.10.cloned.1.call-done = bf16[64,2,512]{2,0,1:T(8,128)(2,1)} async-done(((bf16[2048,2,512]{2,0,1:T(8,128)(2,1)}), bf16[64,2,512]{2,0,1:T(8,128)(2,1)}) %reduce-scatter.10.cloned.1.call-update) | async-done | bytes 131088 | tf_op jit(solution)/shard_map/reduce_scatter | solution.py:330
  1834.6 380.4 %reduce-scatter.14.cloned.1.call-done = bf16[8,512,64]{1,2,0:T(8,128)(2,1)} async-done(((bf16[8,512,2048]{1,2,0:T(8,128)(2,1)}), bf16[8,512,64]{1,2,0:T(8,128)(2,1)}) %reduce-scatter.14.cloned.1.call-update) | async-done | bytes 524304 | tf_op jit(solution)/shard_map/reduce_scatter | solution.py:336
  2217.1 361.1 %reduce-scatter.12.cloned.1.call-done = bf16[8,64,512]{2,1,0:T(8,128)(2,1)} async-done(((bf16[8,2048,512]{2,1,0:T(8,128)(2,1)}), bf16[8,64,512]{2,1,0:T(8,128)(2,1)}) %reduce-scatter.12.cloned.1.call-update) | async-done | bytes 524304 | tf_op jit(solution)/shard_map/reduce_scatter | solution.py:333
  (316 shorter events, 220.5 us)
Async XLA Ops:
  8.0 147.1 %all-gather.8.cloned.1.call-start = ((), (), s32[]{:S(2)}) async-start(), calls=%async_computation.11 | async-start | bytes 4325376 | tf_op jit(solution)/shard_map/all_gather | solution.py:104
  9.7 217.2 %all-gather.10.cloned.1.call-start = ((), (), s32[]{:S(2)}) async-start(), calls=%async_computation.12 | async-start | bytes 2359296 | tf_op jit(solution)/shard_map/all_gather | solution.py:138
  90.2 511.2 %copy-start.25 = (f32[128,64]{1,0:T(8,128)}, f32[128,64]{1,0:T(8,128)S(1)}, u32[]{:S(2)}) copy-start(f32[128,64]{1,0:T(8,128)S(1)} %get-tuple-element.85) | copy-start | bytes 98308
  159.5 431.7 %all-gather.12.cloned.1.call-start = ((), (), s32[]{:S(2)}) async-start(), calls=%async_computation.13 | async-start | bytes 17301504 | tf_op jit(solution)/shard_map/all_gather | solution.py:105
  160.2 795.6 %all-gather.14.cloned.1.call-start = ((), (), s32[]{:S(2)}) async-start(), calls=%async_computation.14 | async-start | bytes 17301504 | tf_op jit(solution)/shard_map/all_gather | solution.py:106
  160.8 876.3 %all-reduce.17.cloned.1.call-start = ((), (), s32[]{:S(2)}) async-start(), calls=%async_computation.15 | async-start | bytes 2097152 | tf_op jit(solution)/shard_map/psum | solution.py:176
  164.8 441.5 %copy-start.34 = (s32[1024]{0:T(1024)}, s32[1024]{0:T(1024)S(1)}, u32[]{:S(2)}) copy-start(s32[1024]{0:T(1024)S(1)} %get-tuple-element.98) | copy-start | bytes 12292
  167.8 423.4 %copy-start.5 = (bf16[320,2048]{1,0:T(8,128)(2,1)}, bf16[320,2048]{1,0:T(8,128)(2,1)S(1)}, u32[]{:S(2)}) copy-start(bf16[320,2048]{1,0:T(8,128)(2,1)S(1)} %gather_fusion) | copy-start | bytes 3932164
  168.0 798.6 %copy-start.36 = (s32[1024]{0:T(1024)}, s32[1024]{0:T(1024)S(1)}, u32[]{:S(2)}) copy-start(s32[1024]{0:T(1024)S(1)} %pad_clamp_fusion.4) | copy-start | bytes 12292
  232.2 369.4 %copy-start.9 = (bf16[1024,4,128,1]{0,2,3,1:T(8,128)(2,1)}, bf16[1024,4,128,1]{0,2,3,1:T(8,128)(2,1)S(1)}, u32[]{:S(2)}) copy-start(bf16[1024,4,128,1]{0,2,3,1:T(8,128)(2,1)S(1)} %copy.140) | copy-start | bytes 3145732
  608.4 358.2 %copy-start.19 = (bf16[320,512]{1,0:T(8,128)(2,1)}, bf16[320,512]{1,0:T(8,128)(2,1)S(1)}, u32[]{:S(2)}) copy-start(bf16[320,512]{1,0:T(8,128)(2,1)S(1)} %gather_fusion.2) | copy-start | bytes 983044
  976.0 71.7 %all-gather.20.cloned.1.call-start = ((), (), s32[]{:S(2)}) async-start(), calls=%async_computation.18 | async-start | bytes 7208960 | tf_op jit(solution)/shard_map/all_gather | solution.py:113
  976.6 128.8 %all-gather.16.cloned.1.call-start = ((), (), s32[]{:S(2)}) async-start(), calls=%async_computation.16 | async-start | bytes 7208960 | tf_op jit(solution)/shard_map/all_gather | solution.py:111
  977.2 191.6 %all-gather.18.cloned.1.call-start = ((), (), s32[]{:S(2)}) async-start(), calls=%async_computation.17 | async-start | bytes 7208960 | tf_op jit(solution)/shard_map/all_gather | solution.py:112
  989.6 53.2 %all-to-all-start.2 = ((bf16[8,40,2048]{2,1,0:T(8,128)(2,1)}), bf16[8,40,2048]{2,1,0:T(8,128)(2,1)S(1)}, u32[]{:S(2)}, u32[]{:S(2)}) async-start(bf16[8,40,2048]{2,1,0:T(8,128)(2,1)} %bitcast.48), calls=%async_computation.2 | async-start | bytes 2621440 | tf_op jit(solution)/shard_map/all_to_all | solution.py:193
  1042.8 62.6 %all-to-all-start = ((bf16[8,40,2048]{2,1,0:T(8,128)(2,1)}), bf16[8,40,2048]{2,1,0:T(8,128)(2,1)}, u32[]{:S(2)}, u32[]{:S(2)}) async-start(bf16[8,40,2048]{2,1,0:T(8,128)(2,1)} %bitcast.36), calls=%async_computation | async-start | bytes 2621440 | tf_op jit(solution)/shard_map/all_to_all | solution.py:192
  1183.1 24.2 all-to-all-start.1
  1208.4 40.6 %all-to-all-start.3 = ((f32[8,40,2048]{2,1,0:T(8,128)}), f32[8,40,2048]{2,1,0:T(8,128)S(1)}, u32[]{:S(2)}, u32[]{:S(2)}) async-start(f32[8,40,2048]{2,1,0:T(8,128)} %bitcast.295), calls=%async_computation.3 | async-start | bytes 5242880 | tf_op jit(solution)/shard_map/all_to_all | solution.py:223
  1212.0 107.2 %all-reduce.21.cloned.1.call-start = ((), (), s32[]{:S(2)}) async-start(), calls=%async_computation.27 | async-start | bytes 4194304 | tf_op jit(solution)/shard_map/psum | solution.py:229
  1260.3 193.3 %reduce-scatter.8.cloned.1.call-start = ((), (), s32[]{:S(2)}) async-start(), calls=%async_computation.19 | async-start | bytes 4718592 | tf_op jit(solution)/shard_map/reduce_scatter | solution.py:289
  1364.3 152.5 %reduce-scatter.16.cloned.1.call-start = ((), (), s32[]{:S(2)}) async-start(), calls=%async_computation.24 | async-start | bytes 7208960 | tf_op jit(solution)/shard_map/reduce_scatter | solution.py:232
  1371.9 206.7 %reduce-scatter.18.cloned.1.call-start = ((), (), s32[]{:S(2)}) async-start(), calls=%async_computation.25 | async-start | bytes 7208960 | tf_op jit(solution)/shard_map/reduce_scatter | solution.py:235
  1379.5 260.8 %reduce-scatter.20.cloned.1.call-start = ((), (), s32[]{:S(2)}) async-start(), calls=%async_computation.26 | async-start | bytes 7208960 | tf_op jit(solution)/shard_map/reduce_scatter | solution.py:238
  1386.8 298.9 %all-reduce.19.cloned.1.call-start = ((), (), s32[]{:S(2)}) async-start(), calls=%async_computation.20 | async-start | bytes 1048576 | tf_op jit(solution)/shard_map/psum | solution.py:315
  1460.8 372.1 %reduce-scatter.10.cloned.1.call-start = ((), (), s32[]{:S(2)}) async-start(), calls=%async_computation.21 | async-start | bytes 4325376 | tf_op jit(solution)/shard_map/reduce_scatter | solution.py:330
  1464.2 750.7 %reduce-scatter.14.cloned.1.call-start = ((), (), s32[]{:S(2)}) async-start(), calls=%async_computation.23 | async-start | bytes 17301504 | tf_op jit(solution)/shard_map/reduce_scatter | solution.py:336
  1473.7 1104.4 %reduce-scatter.12.cloned.1.call-start = ((), (), s32[]{:S(2)}) async-start(), calls=%async_computation.22 | async-start | bytes 17301504 | tf_op jit(solution)/shard_map/reduce_scatter | solution.py:333
  1581.7 104.0 %copy-start.33 = (f32[2048]{0:T(1024)S(1)}, f32[2048]{0:T(1024)}, u32[]{:S(2)}) copy-start(f32[2048]{0:T(1024)} %copy-done.32) | copy-start | bytes 24580
  1581.7 104.0 %copy-start.42 = (f32[128]{0:T(128)S(1)}, f32[128]{0:T(128)}, u32[]{:S(2)}) copy-start(f32[128]{0:T(128)} %copy-done.41) | copy-start | bytes 1540
  1581.7 105.4 %copy-start.38 = (bf16[2048]{0:T(1024)(128)(2,1)S(1)}, bf16[2048]{0:T(1024)(128)(2,1)}, u32[]{:S(2)}) copy-start(bf16[2048]{0:T(1024)(128)(2,1)} %get-tuple-element.50) | copy-start | bytes 12292
  1581.7 177.5 %copy-start.11 = (f32[128,2048]{1,0:T(8,128)S(1)}, f32[128,2048]{1,0:T(8,128)}, u32[]{:S(2)}) copy-start(f32[128,2048]{1,0:T(8,128)} %copy-done.10) | copy-start | bytes 3145732
  1581.7 177.5 %copy-start.54 = (f32[128]{0:T(128)S(1)}, f32[128]{0:T(128)}, u32[]{:S(2)}) copy-start(f32[128]{0:T(128)} %get-tuple-element.88) | copy-start | bytes 1540
  (49 other events, 735.6 us)
Sparse Core Ops, SparseCore 0:
  11.1 143.9 all-gather.7
  159.6 67.2 all-gather.9
  228.5 362.6 all-gather.11
  592.7 363.0 all-gather.13
  976.1 61.0 all-reduce.16
  1260.5 58.6 all-reduce.20
  1364.4 89.1 reduce-scatter.7
  1456.1 60.6 reduce-scatter.15
  1519.2 59.3 reduce-scatter.17
  1580.9 59.3 reduce-scatter.19
  1643.4 42.2 all-reduce.18
  1687.9 144.8 reduce-scatter.9
  1835.3 379.6 reduce-scatter.13
  2217.2 360.8 reduce-scatter.11
Sparse Core Ops, SparseCore 1:
  978.2 63.7 all-gather.19
  1043.6 61.7 all-gather.15
  1107.1 61.7 all-gather.17
where the time goes:
time: 2590 us
  waiting for transfers between devices  2110 us (81%)
  blocking collectives  145 us (6%)
  matrix products  139 us (5%)
  local copies, waits for them, and re-layouts  91.4 us (4%)
  other arithmetic  64.7 us (2%)
    reduce_scatter x1, waiting for transfers between devices, per_device(): lax.psum_scatter(d_out_w.astype(jnp.bfloat16), ('dp', 'expert'), scatter_...  380 us
    reduce_scatter x1, waiting for transfers between devices, per_device(): lax.psum_scatter(d_query_w.astype(jnp.bfloat16), ('dp', 'expert'), scatte...  361 us
    all_gather x1, waiting for transfers between devices, per_device(): lax.all_gather(query_weight, ('dp', 'expert'), axis=1, tiled=True)  356 us
    all_gather x1, waiting for transfers between devices, per_device(): lax.all_gather(out_weight, ('dp', 'expert'), axis=2, tiled=True)  347 us
    unnamed x2, blocking collectives  145 us
    reduce_scatter x1, waiting for transfers between devices, per_device(): lax.psum_scatter(d_kv_w.astype(jnp.bfloat16), ('dp', 'expert'), scatter_d...  71.3 us
    all_gather x1, waiting for transfers between devices, per_device(): lax.all_gather(kv_weight, ('dp', 'expert'), axis=0, tiled=True)  63.6 us
    reduce_scatter x1, waiting for transfers between devices, per_device(): lax.psum_scatter(d_up_w.astype(jnp.bfloat16), 'dp', scatter_dimension=1,...  58.7 us
  transfers between devices with their start and end apart: 21, of which 18 were waited for; matrix products, arithmetic and copies ran while one was open for 7% of the time, Pallas kernels for 0%

commit v1 on v0

v1 whole, which is shorter than its diff:
```python
import jax
import jax.numpy as jnp
from jax import lax
from jax.sharding import PartitionSpec as P

HD = 128
ATT_EXP = 8
TOPK = 2
EPSILON = 1e-06
BF = jnp.bfloat16
F32 = jnp.float32


def dot(spec, left, right):
    return jnp.einsum(spec, left, right, preferred_element_type=F32)


def swap(blocks, axes):
    return lax.all_to_all(blocks, axes, split_axis=0, concat_axis=0, tiled=True)


def spread(block, axis):
    count = lax.axis_size(axis)
    return swap(jnp.broadcast_to(block[None], (count,) + block.shape), axis)


def rope_tables(positions):
    half_dim = HD // 2
    freqs = 10000.0 ** (-(jnp.arange(half_dim).astype(F32) * 2.0 / HD))
    angles = positions[..., None].astype(F32) * freqs
    return (jnp.cos(angles), jnp.sin(angles))


def rotate(values, cos_tab, sin_tab):
    half_dim = values.shape[-1] // 2
    first_half = values[..., :half_dim]
    second_half = values[..., half_dim:]
    return jnp.concatenate(
        [
            first_half * cos_tab - second_half * sin_tab,
            second_half * cos_tab + first_half * sin_tab,
        ],
        -1,
    )


def slot_places(routes, expert_count, capacity):
    length = routes.shape[-2]
    names = jnp.arange(expert_count, dtype=jnp.int32)[:, None]
    member = jnp.any(jnp.swapaxes(routes, -1, -2)[..., None, :] == names, -3)
    order = jnp.arange(length)
    before = (order[:, None] < order[None, :]).astype(BF)
    rank = dot("...et,tu->...eu", member.astype(BF), before)
    slots = jnp.arange(capacity, dtype=F32)[:, None]
    return (member[..., None, :] & (rank[..., None, :] == slots)).astype(BF)


def per_device(
    tokens,
    cotangent,
    doc_lengths,
    att_routes,
    att_gates,
    ffn_routes,
    ffn_gates,
    kv_weight,
    query_weight,
    out_weight,
    attn_gain,
    ffn_gain,
    gate_weight,
    up_weight,
    down_weight,
):
    _, group, width = tokens.shape
    owners = lax.axis_size("expert")
    shares = lax.axis_size("tensor")
    dps = lax.axis_size("dp")
    own = lax.axis_index("expert")
    share = lax.axis_index("tensor")
    columns = owners // 2
    column_half = own % 2
    att_cap = min(group, group * TOPK * 5 // (4 * ATT_EXP))
    ffn_cap = min(group, group * TOPK * 5 // (4 * owners))
    rows = owners * att_cap
    seq_len = owners * group
    piece = width // shares
    local = kv_weight.shape[0]
    head_width = kv_weight.shape[2]

    kv_parts = jnp.transpose(kv_weight.reshape(local, 2, columns, HD), (2, 0, 1, 3))
    kv_parts = jnp.repeat(kv_parts.reshape(columns, local, 2 * HD), 2, axis=0)
    gains = jnp.pad(jnp.stack([attn_gain, ffn_gain], 1), ((0, 0), (0, HD - 2)))
    gains = jnp.broadcast_to(gains[None], (owners, local, HD))
    first_pack = swap(jnp.concatenate([kv_parts, gains, query_weight], 2), "expert")
    second_pack = swap(jnp.swapaxes(out_weight, 1, 2), "expert")
    first_full = lax.all_gather(first_pack.reshape(owners * local, -1), "dp", axis=0, tiled=True)
    out_full = lax.all_gather(second_pack.reshape(owners * local, -1), "dp", axis=0, tiled=True)
    key_value = first_full[:, : 2 * HD]
    gain_one = first_full[:, 2 * HD].astype(F32)
    gain_two = first_full[:, 2 * HD + 1].astype(F32)
    query_full = first_full[:, 3 * HD :]
    gate_full = lax.all_gather(gate_weight[0], "dp", axis=0, tiled=True)
    up_full = lax.all_gather(up_weight[0], "dp", axis=0, tiled=True)
    down_full = lax.all_gather(down_weight[0], "dp", axis=0, tiled=False)

    marks = jnp.pad(att_routes[0].astype(BF), ((0, 0), (0, HD - TOPK)))
    gathered = spread(jnp.concatenate([tokens[0], marks], 1), "expert")
    routes_all = gathered[:, :, width : width + TOPK].astype(jnp.int32)
    inputs_all = gathered[:, :, :width].astype(F32)
    inv_all = lax.rsqrt(jnp.mean(inputs_all * inputs_all, -1, keepdims=True) + EPSILON)
    normed = (inputs_all * inv_all * gain_one).astype(BF)
    places = slot_places(routes_all, ATT_EXP, att_cap)
    token_names = jnp.arange(group, dtype=F32)
    block_starts = (jnp.arange(owners) * group).astype(F32)
    slot_pos = jnp.sum(places.astype(F32) * token_names, -1) + block_starts[:, None, None]
    place_owned = lax.dynamic_index_in_dim(places, own, 1, False)
    pos_owned = lax.dynamic_index_in_dim(slot_pos, own, 1, False)
    pos_half = lax.dynamic_slice_in_dim(slot_pos, column_half * columns, columns, 0)
    row_pos = jnp.swapaxes(pos_half, 0, 1).reshape(rows * columns)
    ends = jnp.cumsum(doc_lengths[0], dtype=jnp.int32).astype(F32)
    key_pos = jnp.arange(seq_len).astype(F32)
    row_seg = jnp.sum((ends[None, :] <= row_pos[:, None]).astype(jnp.int32), -1)
    key_seg = jnp.sum((ends[None, :] <= key_pos[:, None]).astype(jnp.int32), -1)
    visible = (row_seg[:, None] == key_seg[None, :]) & (key_pos[None, :] <= row_pos[:, None])

    def to_heads(values):
        values = values.astype(BF).reshape(2, columns, att_cap, columns, HD)
        values = jnp.transpose(values, (3, 0, 1, 2, 4)).reshape(owners, columns * att_cap, HD)
        return swap(values, "expert").reshape(rows * columns, HD)

    def to_maps(values):
        values = swap(values.astype(BF).reshape(owners, columns * att_cap, HD), "expert")
        values = values.reshape(columns, 2, columns, att_cap, HD)
        return jnp.transpose(values, (1, 2, 3, 0, 4)).reshape(rows, head_width)

    chosen = dot("bst,btd->bsd", place_owned, normed).astype(BF).reshape(rows, width)
    cos_slot, sin_slot = rope_tables(pos_owned)
    query_rows = dot("cd,dh->ch", chosen, query_full).reshape(owners, att_cap, -1, HD)
    query_rows = rotate(query_rows, cos_slot[:, :, None], sin_slot[:, :, None])
    queries = to_heads(query_rows)
    normed = normed.reshape(seq_len, width)
    projected = dot("td,df->tf", normed, key_value)
    cos_key, sin_key = rope_tables(key_pos)
    keys = rotate(projected[:, :HD], cos_key, sin_key).astype(BF)
    values = projected[:, HD:].astype(BF)

    scale = HD ** (-0.5)
    scores = jnp.where(visible, dot("qd,kd->qk", queries, keys) * scale, -1e30)
    row_top = jnp.max(scores, -1, keepdims=True)
    shifted = jnp.exp(scores - row_top)
    row_total = jnp.sum(shifted, -1, keepdims=True)
    probs = shifted / row_total
    log_sum = row_top + jnp.log(row_total)
    mixed = to_maps(dot("qk,kd->qd", probs.astype(BF), values))

    def to_blocks(parts):
        parts = parts.astype(BF).reshape(shares, owners, -1, piece)
        parts = jnp.swapaxes(parts, 0, 1).reshape(owners * shares, -1, piece)
        return swap(parts, ("expert", "tensor"))

    def choice_places(places_here, routes):
        names = jnp.arange(places_here.shape[0], dtype=jnp.int32)
        picks = (routes[:, :, None] == names).astype(BF)
        return jnp.einsum("mst,tjm->jtms", places_here, picks)

    def from_slots(selection, parts):
        selection = jnp.broadcast_to(
            selection[..., None, :], selection.shape[:-1] + (shares, selection.shape[-1])
        )
        selection = selection.reshape(selection.shape[:-3] + (-1,))
        return dot("...tk,kd->...td", selection, parts.reshape(-1, piece))

    def join(part):
        return jnp.swapaxes(spread(part, "tensor"), 0, 1).reshape(group, -1)

    place_att = slot_places(att_routes[0], ATT_EXP, att_cap)
    pick_att = choice_places(place_att, att_routes[0])
    att_gate = att_gates[0]
    out_rows = jnp.einsum(
        "ch,kdh->kcd", mixed, out_full.reshape(shares, piece, head_width), preferred_element_type=F32
    )
    branch = from_slots(pick_att, to_blocks(out_rows))
    attention = jnp.einsum("jtd,tj->td", branch, att_gate, precision=lax.Precision.HIGHEST)
    inputs = tokens[0].astype(F32)
    state = inputs + join(attention.astype(BF)).astype(F32)
    inv_two = lax.rsqrt(jnp.mean(state * state, -1, keepdims=True) + EPSILON)
    normed_two = (state * inv_two * gain_two).astype(BF)

    place_ffn = slot_places(ffn_routes[0], owners, ffn_cap)
    pick_ffn = choice_places(place_ffn, ffn_routes[0])
    ffn_gate = ffn_gates[0]
    gate_slot = jnp.einsum("jtms,tj->ms", pick_ffn, ffn_gate, precision=lax.Precision.HIGHEST)
    upstream = cotangent[0]
    grad_rows = (dot("mst,td->msd", place_ffn, upstream) * gate_slot[:, :, None]).astype(BF)
    expert_grad = swap(grad_rows, "expert").reshape(-1, width)
    send_rows = dot("mst,td->msd", place_ffn, normed_two).astype(BF)
    expert_in = swap(send_rows, "expert").reshape(-1, width)
    gate_act = dot("cd,df->cf", expert_in, gate_full)
    up_act = dot("cd,df->cf", expert_in, up_full)
    sigma = jax.nn.sigmoid(gate_act)
    hidden = (gate_act * sigma * up_act).astype(BF)
    expert_out = dot("cf,kfd->kcd", hidden, down_full)
    ffn_rows = from_slots(pick_ffn, to_blocks(expert_out))
    ffn_part = jnp.einsum("jtd,tj->td", ffn_rows, ffn_gate, precision=lax.Precision.HIGHEST)
    state_part = lax.dynamic_slice_in_dim(state, share * piece, piece, 1)
    output_part = (state_part + ffn_part).astype(BF)

    split_grad = expert_grad.reshape(-1, shares, piece)
    d_hidden = dot("ckd,kfd->cf", split_grad, down_full)
    d_gate = (d_hidden * up_act * sigma * (1.0 + gate_act * (1.0 - sigma))).astype(BF)
    d_up = (d_hidden * gate_act * sigma).astype(BF)
    d_expert_in = dot("cf,df->cd", d_gate, gate_full) + dot("cf,df->cd", d_up, up_full)
    d_expert_in = jnp.swapaxes(d_expert_in.reshape(-1, shares, piece), 0, 1)
    d_norm_rows = to_blocks(d_expert_in)
    d_normed_two = join(
        from_slots(jnp.transpose(place_ffn, (2, 0, 1)), d_norm_rows).astype(BF)
    ).astype(F32)

    def scatter(grad):
        return lax.psum_scatter(grad.astype(BF), "dp", scatter_dimension=0, tiled=True)

    down_grad = scatter(dot("cf,ckd->kfd", hidden, split_grad)).astype(F32)
    gate_grad = scatter(dot("cd,cf->df", expert_in, d_gate)).astype(F32)[None]
    up_grad = scatter(dot("cd,cf->df", expert_in, d_up)).astype(F32)[None]

    upstream = upstream.astype(F32)
    scaled_two = gain_two * d_normed_two
    d_gain_two = jnp.sum(d_normed_two * state * inv_two, 0)
    d_state = (
        upstream
        + inv_two * scaled_two
        - state * inv_two**3 * jnp.mean(state * scaled_two, -1, keepdims=True)
    )
    d_branch = (att_gate.T[:, :, None] * d_state[None]).astype(BF)
    branch_rows = dot("jtms,jtd->msd", pick_att, d_branch).astype(BF)
    d_rows = swap(branch_rows, "expert").reshape(rows, width)
    d_mixed = to_heads(dot("cd,dh->ch", d_rows, out_full))
    out_grad = scatter(dot("cd,ch->dh", d_rows, mixed)).reshape(owners, local, head_width)
    out_grad = jnp.swapaxes(swap(out_grad, "expert"), 1, 2).astype(F32)

    scores = dot("qd,kd->qk", queries, keys) * scale
    probs = jnp.where(visible, jnp.exp(scores - log_sum), 0.0)
    d_probs = dot("qd,kd->qk", d_mixed, values)
    delta = jnp.sum(probs * d_probs, -1, keepdims=True)
    d_scores = (probs * (d_probs - delta)).astype(BF)
    d_queries = dot("qk,kd->qd", d_scores, keys) * scale
    d_keys = dot("qk,qd->kd", d_scores, queries) * scale
    d_values = dot("qk,qd->kd", probs.astype(BF), d_mixed)
    cos_row, sin_row = rope_tables(row_pos)
    d_query_rows = to_maps(rotate(d_queries, cos_row, -sin_row))
    first = column_half == 0
    pairs = [(i, i + 1 - 2 * (i % 2)) for i in range(owners)]
    d_other = lax.ppermute(jnp.where(first, d_values, d_keys).astype(BF), "expert", pairs)
    d_own = jnp.where(first, d_keys, d_values) + d_other.astype(F32)
    d_own = jnp.where(first, rotate(d_own, cos_key, -sin_key), d_own).astype(BF)
    own_weight = jnp.where(first, key_value[:, :HD], key_value[:, HD:])

    d_query_tokens = dot(
        "bst,bsh->bth", place_owned, d_query_rows.reshape(owners, att_cap, head_width)
    )
    d_proj = jnp.concatenate([d_query_tokens.astype(BF).reshape(seq_len, -1), d_own], 1)
    weight_cat = jnp.concatenate([query_full, own_weight], 1).reshape(shares, piece, -1)
    d_normed = dot("th,kdh->ktd", d_proj, weight_cat)
    d_parts = to_blocks(d_normed)
    d_normed_one = jnp.sum(d_parts.astype(F32), 0).astype(BF)
    both = spread(jnp.concatenate([d_normed_one, output_part], 1), "tensor")
    d_normed_one = jnp.swapaxes(both[:, :, :piece], 0, 1).reshape(group, width).astype(F32)
    output = jnp.swapaxes(both[:, :, piece:], 0, 1).reshape(1, group, width)
    scaled_one = gain_one * d_normed_one
    inv_one = lax.rsqrt(jnp.mean(inputs * inputs, -1, keepdims=True) + EPSILON)
    d_gain_one = jnp.sum(d_normed_one * inputs * inv_one, 0)
    input_grad = (
        d_state
        + inv_one * scaled_one
        - inputs * inv_one**3 * jnp.mean(inputs * scaled_one, -1, keepdims=True)
    )[None]

    map_grad = scatter(dot("td,th->dh", normed, d_proj)).reshape(owners, local, -1)
    map_grad = swap(map_grad, "expert").astype(F32)
    query_grad = map_grad[:, :, :head_width]
    kv_grad = jnp.transpose(
        map_grad[:, :, head_width:].reshape(columns, 2, local, HD), (2, 1, 0, 3)
    ).reshape(local, 2, head_width)
    gain_grads = jnp.stack([d_gain_one, d_gain_two]).reshape(2, dps * owners, local)
    gain_grads = jnp.sum(swap(jnp.swapaxes(gain_grads, 0, 1), ("dp", "expert")), 0)
    return (
        output,
        input_grad,
        kv_grad,
        query_grad,
        out_grad,
        gain_grads[0],
        gain_grads[1],
        gate_grad,
        up_grad,
        down_grad,
    )


def solution(mesh):
    in_specs = (
        P("dp", "expert", None),
        P("dp", "expert", None),
        P("dp", None),
        P("dp", "expert", None),
        P("dp", "expert", None),
        P("dp", "expert", None),
        P("dp", "expert", None),
        P(("dp", "expert"), None, "tensor"),
        P(None, ("dp", "expert"), "tensor"),
        P(None, "tensor", ("dp", "expert")),
        P(("dp", "expert")),
        P(("dp", "expert")),
        P("expert", "dp", "tensor"),
        P("expert", "dp", "tensor"),
        P("expert", "tensor", "dp"),
    )
    out_specs = (
        P("dp", "expert", None),
        P("dp", "expert", None),
        P(("dp", "expert"), None, "tensor"),
        P(None, ("dp", "expert"), "tensor"),
        P(None, "tensor", ("dp", "expert")),
        P(("dp", "expert")),
        P(("dp", "expert")),
        P("expert", "dp", "tensor"),
        P("expert", "dp", "tensor"),
        P("expert", "tensor", "dp"),
    )
    return jax.shard_map(
        per_device, mesh=mesh, in_specs=in_specs, out_specs=out_specs, check_vma=False
    )
```

time: 2590 us -> 699 us (0.27)
  waiting for transfers between devices: 2110 us -> 280 us
  blocking collectives: 145 us -> 29.6 us
  starting transfers between devices: 21.1 us -> 99.2 us
    reduce_scatter x7 -> x5, waiting for transfers between devices: 1000 us -> 25 us  [scatter(): lax.psum_scatter(grad.astype(BF), 'dp', scatter_dimension=0, tiled=True)]
    all_gather x7 -> x5, waiting for transfers between devices: 935 us -> 31 us  [the longest x1 31 us: per_device(): down_full = lax.all_gather(down_weight[0], 'dp', axis=0, tiled=False)]
    all_to_all x4 -> x18, waiting for transfers between devices: 25.2 us -> 223 us  [swap(): return lax.all_to_all(blocks, axes, split_axis=0, concat_axis=0, tiled=True)]
    unnamed x2 -> x0, blocking collectives: 145 us -> none
    psum x3 -> x0, waiting for transfers between devices: 142 us -> none  [the longest x1 57.7 us: per_device(): lax.psum((ffn_part, jnp.sum(grad_norm_rows, 1)), 'tensor')]
    all_to_all x4 -> x18, starting transfers between devices: 19 us -> 97 us  [swap(): return lax.all_to_all(blocks, axes, split_axis=0, concat_axis=0, tiled=True)]
    gather x12 -> x0, local copies, waits for them, and re-layouts: 31 us -> none  [the longest x6 15.5 us: take_rows(): return padded[source]]
    all_to_all x0 -> x2, blocking collectives: none -> 29.6 us  [swap(): return lax.all_to_all(blocks, axes, split_axis=0, concat_axis=0, tiled=True)]
  transfers between devices with their start and end apart: 21 -> 29, of which waited for: 18 -> 17; matrix products, arithmetic and copies ran while one was open for 7% -> 31% of each run, Pallas kernels for 0% -> 0%
where the time goes in v1:
time: 699 us; the launch traced here: 690 us
  waiting for transfers between devices  280 us (40%)
  matrix products  119 us (17%)
  starting transfers between devices  99.2 us (14%)
  local copies, waits for them, and re-layouts  84 us (12%)
  other arithmetic  62.5 us (9%)
  blocking collectives  29.6 us (4%)
  between operations  15.8 us (2%)
    all_to_all x18, waiting for transfers between devices, swap(): return lax.all_to_all(blocks, axes, split_axis=0, concat_axis=0, tiled=True)  223 us
    dot_general x31, matrix products, dot(): return jnp.einsum(spec, left, right, preferred_element_type=F32)  111 us
    all_to_all x18, starting transfers between devices, swap(): return lax.all_to_all(blocks, axes, split_axis=0, concat_axis=0, tiled=True)  97 us
    all_gather x1, waiting for transfers between devices, per_device(): down_full = lax.all_gather(down_weight[0], 'dp', axis=0, tiled=False)  31 us
    all_to_all x2, blocking collectives, swap(): return lax.all_to_all(blocks, axes, split_axis=0, concat_axis=0, tiled=True)  29.6 us
    reduce_scatter x5, waiting for transfers between devices, scatter(): lax.psum_scatter(grad.astype(BF), 'dp', scatter_dimension=0, tiled=True)  25 us
    unnamed x122, local copies, waits for them, and re-layouts  22.6 us
  transfers between devices with their start and end apart: 29, of which 17 were waited for; matrix products, arithmetic and copies ran while one was open for 31% of the time, Pallas kernels for 0%

profile of v1, /device:TPU:1, one launch (start us, length us, event | category | flops | bytes accessed | tf_op | source)
XLA Modules:
  0.0 690.1 jit_solution(10395411021296999171)
XLA Ops:
  9.5 19.0 %all_to_all.100 = bf16[8,64,896]{2,1,0:T(8,128)(2,1)S(1)} all-to-all(bf16[8,64,896]{2,1,0:T(8,128)(2,1)S(1)} %pad_maximum_fusion.2), channel_id=1, replica_groups=mesh['dp'=4,'expert'=8,'tensor'=4] {'expert'}, dimensions={0} | all-to-all | bytes 1835008 | tf_op jit(solution)/shard_map/all_to_all | solution.py:19
  29.9 10.6 %all_to_all.101 = bf16[8,64,512]{2,1,0:T(8,128)(2,1)} all-to-all(bf16[8,64,512]{2,1,0:T(8,128)(2,1)S(1)} %bitcast.384), channel_id=1, replica_groups=mesh['dp'=4,'expert'=8,'tensor'=4] {'expert'}, dimensions={0} | all-to-all | bytes 1048576 | tf_op jit(solution)/shard_map/all_to_all | solution.py:19
  51.6 59.1 %all-to-all-done.1 = bf16[8,128,2176]{2,1,0:T(8,128)(2,1)} async-done(((bf16[8,128,2176]{2,1,0:T(8,128)(2,1)}), bf16[8,128,2176]{2,1,0:T(8,128)(2,1)}, u32[]{:S(2)}, u32[]{:S(2)}) %all-to-all-start.1) | async-done | bytes 4456480 | tf_op jit(solution)/shard_map/all_to_all | solution.py:19
  150.9 6.0 all-to-all-done.3
  161.1 10.3 %all-to-all-start.5 = ((bf16[32,40,512]{2,1,0:T(8,128)(2,1)}), bf16[32,40,512]{2,1,0:T(8,128)(2,1)S(1)}, u32[]{:S(2)}, u32[]{:S(2)}) async-start(bf16[32,40,512]{2,1,0:T(8,128)(2,1)} %bitcast.351), calls=%async_computation.5 | async-start | bytes 2621440 | tf_op jit(solution)/shard_map/all_to_all | solution.py:19
  177.0 13.8 %all-to-all-done.5 = bf16[32,40,512]{2,1,0:T(8,128)(2,1)S(1)} async-done(((bf16[32,40,512]{2,1,0:T(8,128)(2,1)}), bf16[32,40,512]{2,1,0:T(8,128)(2,1)S(1)}, u32[]{:S(2)}, u32[]{:S(2)}) %all-to-all-start.5) | async-done | bytes 1310752 | tf_op jit(solution)/shard_map/all_to_all | solution.py:19
  200.9 7.5 %all-to-all-done.6 = bf16[4,128,512]{2,1,0:T(8,128)(2,1)S(1)} async-done(((bf16[4,128,512]{2,1,0:T(8,128)(2,1)}), bf16[4,128,512]{2,1,0:T(8,128)(2,1)S(1)}, u32[]{:S(2)}, u32[]{:S(2)}) %all-to-all-start.6) | async-done | bytes 524320 | tf_op jit(solution)/shard_map/all_to_all | solution.py:19
  220.5 11.7 %all-to-all-done.7 = bf16[8,40,2048]{2,1,0:T(8,128)(2,1)} async-done(((bf16[8,40,2048]{2,1,0:T(8,128)(2,1)}), bf16[8,40,2048]{2,1,0:T(8,128)(2,1)}, u32[]{:S(2)}, u32[]{:S(2)}) %all-to-all-start.7) | async-done | bytes 1310752 | tf_op jit(solution)/shard_map/all_to_all | solution.py:19
  240.7 14.0 %all-to-all-done.8 = bf16[8,40,2048]{2,1,0:T(8,128)(2,1)} async-done(((bf16[8,40,2048]{2,1,0:T(8,128)(2,1)}), bf16[8,40,2048]{2,1,0:T(8,128)(2,1)}, u32[]{:S(2)}, u32[]{:S(2)}) %all-to-all-start.8) | async-done | bytes 1310752 | tf_op jit(solution)/shard_map/all_to_all | solution.py:19
  254.7 6.5 fusion.5
  261.2 6.5 fusion.9
  267.7 31.0 %all-gather.12.cloned.1.call-done = bf16[4,1408,512]{2,1,0:T(8,128)(2,1)} async-done(((bf16[1,1408,512]{2,1,0:T(8,128)(2,1)}), bf16[4,1408,512]{2,1,0:T(8,128)(2,1)}) %all-gather.12.cloned.1.call-update) | async-done | bytes 5767184 | tf_op jit(solution)/shard_map/all_gather | solution.py:105
  298.7 7.7 %multiply_convert_fusion.3 = (bf16[320,1408]{1,0:T(8,128)(2,1)S(1)}, bf16[320,1408]{1,0:T(8,128)(2,1)S(1)}, bf16[320,1408]{1,0:T(8,128)(2,1)}) fusion(f32[320,1408]{1,0:T(8,128)} %fusion.5, f32[320,1408]{1,0:T(8,128)} %fusion.9, bf16[4,1408,512]{2,1,0:T(8,128)(2,1)} %all-gather.12.cloned.1.call-done, bf16[320,4,512]{2,1,0:T(4,128)(2,1)} %reshape_reshape.6), kind=kOutput, calls=%fused_computation.45 | convolution fusion | flops 1852702720 | bytes 13385728 | tf_op jit(solution)/shard_map/ckd,kfd->cf/dot_general | solution.py:15
  306.4 5.6 fusion.3
  315.5 7.8 %all-to-all-start.9 = ((bf16[32,40,512]{2,1,0:T(8,128)(2,1)}), bf16[32,40,512]{2,1,0:T(8,128)(2,1)}, u32[]{:S(2)}, u32[]{:S(2)}) async-start(bf16[32,40,512]{2,1,0:T(8,128)(2,1)} %bitcast.352), calls=%async_computation.9 | async-start | bytes 2621440 | tf_op jit(solution)/shard_map/all_to_all | solution.py:19
  323.3 19.5 %all-to-all-done.9 = bf16[32,40,512]{2,1,0:T(8,128)(2,1)} async-done(((bf16[32,40,512]{2,1,0:T(8,128)(2,1)}), bf16[32,40,512]{2,1,0:T(8,128)(2,1)}, u32[]{:S(2)}, u32[]{:S(2)}) %all-to-all-start.9) | async-done | bytes 1310752 | tf_op jit(solution)/shard_map/all_to_all | solution.py:19
  354.1 5.2 all-to-all-done.10
  380.2 19.4 %all-to-all-done.11 = bf16[8,40,2048]{2,1,0:T(8,128)(2,1)} async-done(((bf16[8,40,2048]{2,1,0:T(8,128)(2,1)}), bf16[8,40,2048]{2,1,0:T(8,128)(2,1)}, u32[]{:S(2)}, u32[]{:S(2)}) %all-to-all-start.11) | async-done | bytes 1310752 | tf_op jit(solution)/shard_map/all_to_all | solution.py:19
  451.8 7.2 %convolution_convert_fusion.2 = bf16[2048,640]{1,0:T(8,128)(2,1)} fusion(bf16[1024,2048]{1,0:T(8,128)(2,1)} %bitcast.335, bf16[1024,128]{1,0:T(8,128)(2,1)} %copy.238, bf16[1024,512]{1,0:T(8,128)(2,1)S(1)} %bitcast.376), kind=kOutput, calls=%fused_computation.24 | convolution fusion | flops 2688286720 | bytes 8126464 | tf_op jit(solution)/shard_map/td,th->dh/dot_general | solution.py:15
  459.1 7.4 %convert_bitcast_fusion = bf16[4,1408,512]{1,2,0:T(8,128)(2,1)} fusion(bf16[320,4,512]{2,1,0:T(4,128)(2,1)} %reshape_reshape.6, bf16[320,1408]{1,0:T(8,128)(2,1)} %get-tuple-element.90), kind=kOutput, calls=%fused_computation.15 | convolution fusion | flops 1848377344 | bytes 7979008 | tf_op jit(solution)/shard_map/cf,ckd->kfd/dot_general | solution.py:15
  466.6 7.4 %convolution_convert_fusion = bf16[2048,1408]{1,0:T(8,128)(2,1)} fusion(bf16[320,2048]{1,0:T(8,128)(2,1)} %bitcast.68, bf16[320,1408]{1,0:T(8,128)(2,1)} %copy-done.52), kind=kOutput, calls=%fused_computation.5 | convolution fusion | flops 1848377344 | bytes 7979008 | tf_op jit(solution)/shard_map/cd,cf->df/dot_general | solution.py:15
  474.2 7.4 %convolution_convert_fusion.1 = bf16[2048,1408]{1,0:T(8,128)(2,1)} fusion(bf16[320,2048]{1,0:T(8,128)(2,1)} %bitcast.68, bf16[320,1408]{1,0:T(8,128)(2,1)} %copy-done.51), kind=kOutput, calls=%fused_computation.6 | convolution fusion | flops 1848377344 | bytes 7979008 | tf_op jit(solution)/shard_map/cd,cf->df/dot_general | solution.py:15
  481.7 5.2 convolution_convert_fusion.7
  488.1 8.1 %all-to-all-start.15 = ((bf16[32,40,512]{2,1,0:T(8,128)(2,1)}), bf16[32,40,512]{2,1,0:T(8,128)(2,1)}, u32[]{:S(2)}, u32[]{:S(2)}) async-start(bf16[32,40,512]{2,1,0:T(8,128)(2,1)} %bitcast.350), calls=%async_computation.15 | async-start | bytes 2621440 | tf_op jit(solution)/shard_map/all_to_all | solution.py:19
  503.8 6.0 convolution_convert_fusion.6
  513.0 7.6 %copy.239 = bf16[4,8,128,512]{3,2,0,1:T(8,128)(2,1)} copy(bf16[4,8,128,512]{2,1,3,0:T(8,128)(2,1)} %bitcast.337) | data formatting | bytes 8388608 | tf_op jit(solution)/shard_map/reshape | solution.py:158
  520.6 8.0 %all-to-all-start.14 = ((bf16[32,128,512]{2,1,0:T(8,128)(2,1)}), bf16[32,128,512]{2,1,0:T(8,128)(2,1)}, u32[]{:S(2)}, u32[]{:S(2)}) async-start(bf16[32,128,512]{2,1,0:T(8,128)(2,1)} %bitcast.336), calls=%async_computation.14 | async-start | bytes 8388608 | tf_op jit(solution)/shard_map/all_to_all | solution.py:19
  533.9 46.6 %all-to-all-done.14 = bf16[32,128,512]{2,1,0:T(8,128)(2,1)} async-done(((bf16[32,128,512]{2,1,0:T(8,128)(2,1)}), bf16[32,128,512]{2,1,0:T(8,128)(2,1)}, u32[]{:S(2)}, u32[]{:S(2)}) %all-to-all-start.14) | async-done | bytes 4194336 | tf_op jit(solution)/shard_map/all_to_all | solution.py:19
  589.1 15.1 %all-to-all-done.16 = bf16[4,128,1024]{2,1,0:T(8,128)(2,1)S(1)} async-done(((bf16[4,128,1024]{2,1,0:T(8,128)(2,1)}), bf16[4,128,1024]{2,1,0:T(8,128)(2,1)S(1)}, u32[]{:S(2)}, u32[]{:S(2)}) %all-to-all-start.16) | async-done | bytes 1048608 | tf_op jit(solution)/shard_map/all_to_all | solution.py:19
  604.2 5.2 all-to-all-start.18
  618.3 6.6 all-to-all-start.19
  654.6 25.0 %reduce-scatter.10.cloned.1.call-done = bf16[512,1408]{1,0:T(8,128)(2,1)} async-done(((bf16[2048,1408]{1,0:T(8,128)(2,1)}), bf16[512,1408]{1,0:T(8,128)(2,1)}) %reduce-scatter.10.cloned.1.call-update) | async-done | bytes 1441808 | tf_op jit(solution)/shard_map/reduce_scatter | solution.py:221
  (317 shorter events, 250.2 us)
Async XLA Ops:
  7.2 109.7 %all-gather.8.cloned.1.call-start = ((), (), s32[]{:S(2)}) async-start(), calls=%async_computation.25 | async-start | bytes 4587520 | tf_op jit(solution)/shard_map/all_gather | solution.py:97
  29.8 127.5 %all-gather.10.cloned.1.call-start = ((), (), s32[]{:S(2)}) async-start(), calls=%async_computation.26 | async-start | bytes 2621440 | tf_op jit(solution)/shard_map/all_gather | solution.py:98
  40.5 200.1 %all-gather.16.cloned.1.call-start = ((), (), s32[]{:S(2)}) async-start(), calls=%async_computation.34 | async-start | bytes 7208960 | tf_op jit(solution)/shard_map/all_gather | solution.py:103
  41.3 219.9 %all-gather.14.cloned.1.call-start = ((), (), s32[]{:S(2)}) async-start(), calls=%async_computation.33 | async-start | bytes 7208960 | tf_op jit(solution)/shard_map/all_gather | solution.py:104
  44.7 66.0 %all-to-all-start.1 = ((bf16[8,128,2176]{2,1,0:T(8,128)(2,1)}), bf16[8,128,2176]{2,1,0:T(8,128)(2,1)}, u32[]{:S(2)}, u32[]{:S(2)}) async-start(bf16[8,128,2176]{2,1,0:T(8,128)(2,1)} %broadcast_in_dim.37), calls=%async_computation.1 | async-start | bytes 8912896 | tf_op jit(solution)/shard_map/all_to_all | solution.py:19
  49.4 249.2 %all-gather.12.cloned.1.call-start = ((), (), s32[]{:S(2)}) async-start(), calls=%async_computation.27 | async-start | bytes 7208960 | tf_op jit(solution)/shard_map/all_gather | solution.py:105
  51.5 85.3 %copy-start.33 = (f32[64]{0:T(128)}, f32[64]{0:T(128)S(1)}, u32[]{:S(2)}) copy-start(f32[64]{0:T(128)S(1)} %negate_power_fusion) | copy-start | bytes 772
  129.3 9.6 %all-to-all-start.2 = ((bf16[8,160,128]{2,1,0:T(8,128)(2,1)}), bf16[8,160,128]{2,1,0:T(8,128)(2,1)S(1)}, u32[]{:S(2)}, u32[]{:S(2)}) async-start(bf16[8,160,128]{2,1,0:T(8,128)(2,1)} %bitcast.24), calls=%async_computation.2 | async-start | bytes 655360 | tf_op jit(solution)/shard_map/all_to_all | solution.py:19
  145.7 11.2 %all-to-all-start.3 = ((bf16[8,160,128]{2,1,0:T(8,128)(2,1)}), bf16[8,160,128]{2,1,0:T(8,128)(2,1)S(1)}, u32[]{:S(2)}, u32[]{:S(2)}) async-start(bf16[8,160,128]{2,1,0:T(8,128)(2,1)} %bitcast.34), calls=%async_computation.3 | async-start | bytes 655360 | tf_op jit(solution)/shard_map/all_to_all | solution.py:19
  161.1 29.8 %all-to-all-start.5 = ((bf16[32,40,512]{2,1,0:T(8,128)(2,1)}), bf16[32,40,512]{2,1,0:T(8,128)(2,1)S(1)}, u32[]{:S(2)}, u32[]{:S(2)}) async-start(bf16[32,40,512]{2,1,0:T(8,128)(2,1)} %bitcast.351), calls=%async_computation.5 | async-start | bytes 2621440 | tf_op jit(solution)/shard_map/all_to_all | solution.py:19
  195.5 12.9 %all-to-all-start.6 = ((bf16[4,128,512]{2,1,0:T(8,128)(2,1)}), bf16[4,128,512]{2,1,0:T(8,128)(2,1)S(1)}, u32[]{:S(2)}, u32[]{:S(2)}) async-start(bf16[4,128,512]{2,1,0:T(8,128)(2,1)} %broadcast_in_dim.41), calls=%async_computation.6 | async-start | bytes 1048576 | tf_op jit(solution)/shard_map/all_to_all | solution.py:19
  208.4 23.9 %all-to-all-start.7 = ((bf16[8,40,2048]{2,1,0:T(8,128)(2,1)}), bf16[8,40,2048]{2,1,0:T(8,128)(2,1)}, u32[]{:S(2)}, u32[]{:S(2)}) async-start(bf16[8,40,2048]{2,1,0:T(8,128)(2,1)} %fusion.18), calls=%async_computation.7 | async-start | bytes 2621440 | tf_op jit(solution)/shard_map/all_to_all | solution.py:19
  217.9 149.9 %copy-start.35 = (f32[128]{0:T(128)}, f32[128]{0:T(128)S(1)}, u32[]{:S(2)}) copy-start(f32[128]{0:T(128)S(1)} %get-tuple-element.110) | copy-start | bytes 1540
  217.9 149.9 %copy-start.42 = (f32[128]{0:T(128)}, f32[128]{0:T(128)S(1)}, u32[]{:S(2)}) copy-start(f32[128]{0:T(128)S(1)} %get-tuple-element.109) | copy-start | bytes 1540
  232.3 22.4 %all-to-all-start.8 = ((bf16[8,40,2048]{2,1,0:T(8,128)(2,1)}), bf16[8,40,2048]{2,1,0:T(8,128)(2,1)}, u32[]{:S(2)}, u32[]{:S(2)}) async-start(bf16[8,40,2048]{2,1,0:T(8,128)(2,1)} %convolution_convert_fusion.4), calls=%async_computation.8 | async-start | bytes 2621440 | tf_op jit(solution)/shard_map/all_to_all | solution.py:19
  315.5 27.3 %all-to-all-start.9 = ((bf16[32,40,512]{2,1,0:T(8,128)(2,1)}), bf16[32,40,512]{2,1,0:T(8,128)(2,1)}, u32[]{:S(2)}, u32[]{:S(2)}) async-start(bf16[32,40,512]{2,1,0:T(8,128)(2,1)} %bitcast.352), calls=%async_computation.9 | async-start | bytes 2621440 | tf_op jit(solution)/shard_map/all_to_all | solution.py:19
  345.4 13.9 %all-to-all-start.10 = ((bf16[4,128,512]{2,1,0:T(8,128)(2,1)}), bf16[4,128,512]{2,1,0:T(8,128)(2,1)}, u32[]{:S(2)}, u32[]{:S(2)}) async-start(bf16[4,128,512]{2,1,0:T(8,128)(2,1)} %broadcast_in_dim.43), calls=%async_computation.10 | async-start | bytes 1048576 | tf_op jit(solution)/shard_map/all_to_all | solution.py:19
  375.9 23.7 %all-to-all-start.11 = ((bf16[8,40,2048]{2,1,0:T(8,128)(2,1)}), bf16[8,40,2048]{2,1,0:T(8,128)(2,1)}, u32[]{:S(2)}, u32[]{:S(2)}) async-start(bf16[8,40,2048]{2,1,0:T(8,128)(2,1)} %fusion.19), calls=%async_computation.11 | async-start | bytes 2621440 | tf_op jit(solution)/shard_map/all_to_all | solution.py:19
  406.7 10.2 %all-to-all-start.12 = ((bf16[8,160,128]{2,1,0:T(8,128)(2,1)}), bf16[8,160,128]{2,1,0:T(8,128)(2,1)}, u32[]{:S(2)}, u32[]{:S(2)}) async-start(bf16[8,160,128]{2,1,0:T(8,128)(2,1)} %bitcast.368), calls=%async_computation.12 | async-start | bytes 655360 | tf_op jit(solution)/shard_map/all_to_all | solution.py:19
  410.7 178.4 %reduce-scatter.8.cloned.1.call-start = ((), (), s32[]{:S(2)}) async-start(), calls=%async_computation.29 | async-start | bytes 2621440 | tf_op jit(solution)/shard_map/reduce_scatter | solution.py:221
  429.3 12.4 %collective-permute-start = (bf16[1024,128]{0,1:T(8,128)(2,1)}, bf16[1024,128]{0,1:T(8,128)(2,1)}, u32[]{:S(2)}, u32[]{:S(2)}) collective-permute-start(bf16[1024,128]{0,1:T(8,128)(2,1)} %get-tuple-element.115), channel_id=1, source_target_pairs={{0,4},{4,0},{8,12},{12,8},{16,20},{20,16},{24,28},{28,24},{1,5},{5... | collective-permute-start | bytes 786440 | tf_op jit(solution)/shard_map/ppermute | solution.py:254
  438.0 9.5 %all-to-all-start.13 = ((bf16[8,160,128]{2,1,0:T(8,128)(2,1)}), bf16[8,160,128]{2,1,0:T(8,128)(2,1)S(1)}, u32[]{:S(2)}, u32[]{:S(2)}) async-start(bf16[8,160,128]{2,1,0:T(8,128)(2,1)} %pad_maximum_fusion.6), calls=%async_computation.13 | async-start | bytes 655360 | tf_op jit(solution)/shard_map/all_to_all | solution.py:19
  441.5 190.5 %reduce-scatter.6.cloned.1.call-start = ((), (), s32[]{:S(2)}) async-start(), calls=%async_computation.28 | async-start | bytes 3276800 | tf_op jit(solution)/shard_map/reduce_scatter | solution.py:221
  459.1 189.3 %reduce-scatter.14.cloned.1.call-start = ((), (), s32[]{:S(2)}) async-start(), calls=%async_computation.32 | async-start | bytes 7208960 | tf_op jit(solution)/shard_map/reduce_scatter | solution.py:221
  466.5 184.9 %reduce-scatter.12.cloned.1.call-start = ((), (), s32[]{:S(2)}) async-start(), calls=%async_computation.31 | async-start | bytes 7208960 | tf_op jit(solution)/shard_map/reduce_scatter | solution.py:221
  474.0 205.7 %reduce-scatter.10.cloned.1.call-start = ((), (), s32[]{:S(2)}) async-start(), calls=%async_computation.30 | async-start | bytes 7208960 | tf_op jit(solution)/shard_map/reduce_scatter | solution.py:221
  488.1 32.5 %all-to-all-start.15 = ((bf16[32,40,512]{2,1,0:T(8,128)(2,1)}), bf16[32,40,512]{2,1,0:T(8,128)(2,1)}, u32[]{:S(2)}, u32[]{:S(2)}) async-start(bf16[32,40,512]{2,1,0:T(8,128)(2,1)} %bitcast.350), calls=%async_computation.15 | async-start | bytes 2621440 | tf_op jit(solution)/shard_map/all_to_all | solution.py:19
  520.6 59.8 %all-to-all-start.14 = ((bf16[32,128,512]{2,1,0:T(8,128)(2,1)}), bf16[32,128,512]{2,1,0:T(8,128)(2,1)}, u32[]{:S(2)}, u32[]{:S(2)}) async-start(bf16[32,128,512]{2,1,0:T(8,128)(2,1)} %bitcast.336), calls=%async_computation.14 | async-start | bytes 8388608 | tf_op jit(solution)/shard_map/all_to_all | solution.py:19
  584.4 19.9 %all-to-all-start.16 = ((bf16[4,128,1024]{2,1,0:T(8,128)(2,1)}), bf16[4,128,1024]{2,1,0:T(8,128)(2,1)S(1)}, u32[]{:S(2)}, u32[]{:S(2)}) async-start(bf16[4,128,1024]{2,1,0:T(8,128)(2,1)} %broadcast_in_dim.45), calls=%async_computation.16 | async-start | bytes 2097152 | tf_op jit(solution)/shard_map/all_to_all | solution.py:19
  604.2 14.1 %all-to-all-start.18 = ((bf16[8,64,512]{2,1,0:T(8,128)(2,1)}), bf16[8,64,512]{2,1,0:T(8,128)(2,1)}, u32[]{:S(2)}, u32[]{:S(2)}) async-start(bf16[8,64,512]{2,1,0:T(8,128)(2,1)} %bitcast.385), calls=%async_computation.20 | async-start | bytes 1048576 | tf_op jit(solution)/shard_map/all_to_all | solution.py:19
  618.3 13.7 %all-to-all-start.19 = ((f32[32,1,128]{2,1,0:T(1,128)}), f32[32,1,128]{2,1,0:T(1,128)S(1)}, u32[]{:S(2)}, u32[]{:S(2)}) async-start(f32[32,1,128]{2,1,0:T(1,128)} %reshape.608), calls=%async_computation.21 | async-start | bytes 32768 | tf_op jit(solution)/shard_map/all_to_all | solution.py:19
  632.0 12.3 %all-to-all-start.17 = ((bf16[8,64,640]{2,1,0:T(8,128)(2,1)}), bf16[8,64,640]{2,1,0:T(8,128)(2,1)}, u32[]{:S(2)}, u32[]{:S(2)}) async-start(bf16[8,64,640]{2,1,0:T(8,128)(2,1)} %bitcast.382), calls=%async_computation.18 | async-start | bytes 1310720 | tf_op jit(solution)/shard_map/all_to_all | solution.py:19
  (52 other events, 365.8 us)
Sparse Core Ops, SparseCore 0:
  30.0 45.8 all-gather.7
  77.5 31.1 all-gather.9
  110.4 61.3 all-gather.15
  173.3 61.8 all-gather.13
  236.7 61.8 all-gather.11
  414.9 29.8 reduce-scatter.7
  459.2 34.5 reduce-scatter.5
  496.3 59.4 reduce-scatter.13
  558.3 59.3 reduce-scatter.11
  620.1 59.4 reduce-scatter.9

commit v2 on v1

--- a/solution.py
+++ b/solution.py
@@ -1,6 +1,8 @@
 import jax
 import jax.numpy as jnp
 from jax import lax
+from jax.experimental import pallas as pl
+from jax.experimental.pallas import tpu as pltpu
 from jax.sharding import PartitionSpec as P
 
 HD = 128
@@ -53,6 +55,378 @@
     rank = dot("...et,tu->...eu", member.astype(BF), before)
     slots = jnp.arange(capacity, dtype=F32)[:, None]
     return (member[..., None, :] & (rank[..., None, :] == slots)).astype(BF)
+
+
+def remote(src, dst, send, recv, device):
+    return pltpu.make_async_remote_copy(
+        src_ref=src,
+        dst_ref=dst,
+        send_sem=send,
+        recv_sem=recv,
+        device_id=device,
+        device_id_type=pl.DeviceIdType.MESH,
+    )
+
+
+def each(count, body, start=1):
+    def step(index, carry):
+        body(index)
+        return carry
+
+    lax.fori_loop(start, count, step, 0)
+
+
+def mm(left, right, left_dim=1, right_dim=0):
+    return lax.dot_general(
+        left, right, (((left_dim,), (right_dim,)), ((), ())), preferred_element_type=F32
+    )
+
+
+def enter(own, half, core, owners):
+    semaphore = pltpu.get_barrier_semaphore()
+
+    def hello(expert, tensor):
+        pl.semaphore_signal(
+            semaphore,
+            inc=1,
+            device_id={"expert": expert, "tensor": tensor},
+            device_id_type=pl.DeviceIdType.MESH,
+        )
+
+    def column(step):
+        hello(
+            lax.rem(own + lax.div(step, 2), owners),
+            2 * lax.rem(half + lax.rem(step, 2), 2) + core,
+        )
+
+    each(2 * owners, column)
+    hello(own, 2 * half + 1 - core)
+    hello(own, 2 * (1 - half) + 1 - core)
+    pl.semaphore_wait(semaphore, 2 * owners + 1)
+
+
+def send_home(merged, landing, sends, recvs, own, half, core, owners):
+    def outgoing(step):
+        to, side = lax.rem(own + lax.div(step, 2), owners), lax.rem(half + lax.rem(step, 2), 2)
+        return remote(
+            merged.at[side, to],
+            landing.at[half, own],
+            sends.at[step],
+            recvs.at[step],
+            {"expert": to, "tensor": 2 * side + core},
+        )
+
+    each(2 * owners, lambda step: outgoing(step).start())
+    landing[half, own] = merged[half, own]
+    return outgoing
+
+
+def wait_home(outgoing, owners):
+    each(2 * owners, lambda step: outgoing(step).wait())
+
+
+def share_slices(slices, sends, recvs, own, share, shares):
+    def copy(step):
+        return remote(
+            slices.at[share],
+            slices.at[share],
+            sends.at[step],
+            recvs.at[step],
+            {"expert": own, "tensor": lax.rem(share + step, shares)},
+        )
+
+    each(shares, lambda step: copy(step).start())
+    each(shares, lambda step: copy(step).wait())
+
+
+def middle_kernel(
+    parts,
+    sel_ffn,
+    state,
+    inv_two,
+    upstream,
+    gain_two,
+    sel_att,
+    att_gate,
+    out_full,
+    queries,
+    keys,
+    values,
+    log_sum,
+    row_pos,
+    row_seg,
+    key_pos,
+    key_seg,
+    cos_row,
+    sin_row,
+    cos_key,
+    sin_key,
+    place_back,
+    d_state,
+    gain_grad,
+    d_rows,
+    d_proj,
+    sibling,
+    merged,
+    landing,
+    slices,
+    rows_out,
+    heads_out,
+    heads_in,
+    queries_out,
+    queries_in,
+    pair_out,
+    pair_in,
+    d_keys,
+    d_values,
+    one_send,
+    one_recv,
+    home_send,
+    home_recv,
+    slice_send,
+    slice_recv,
+    row_send,
+    row_recv,
+    head_send,
+    head_recv,
+    back_send,
+    back_recv,
+):
+    own, share = lax.axis_index("expert"), lax.axis_index("tensor")
+    owners, shares = heads_out.shape[0], slices.shape[0]
+    half, core = lax.div(share, 2), lax.rem(share, 2)
+    piece, width = slices.shape[2], state.shape[1]
+    slots = merged.shape[2]
+    rows = owners * slots
+    wide = width // 2
+    head_rows = heads_out.shape[1]
+    columns = owners // 2
+    other = {"expert": own, "tensor": 2 * half + 1 - core}
+    enter(own, half, core, owners)
+
+    across = remote(parts.at[1 - core], sibling, one_send.at[0], one_recv.at[0], other)
+    across.start()
+    across.wait()
+    for side in range(2):
+        merged[side] = (parts[core, side].astype(F32) + sibling[side].astype(F32)).astype(BF)
+    outgoing = send_home(merged, landing, home_send, home_recv, own, half, core, owners)
+    wait_home(outgoing, owners)
+    total = mm(sel_ffn[...], landing[0].reshape(rows, piece))
+    total = total + mm(sel_ffn[...], landing[1].reshape(rows, piece))
+    slices[share] = total.astype(BF)
+    share_slices(slices, slice_send, slice_recv, own, share, shares)
+
+    inv = inv_two[...]
+    mean = jnp.zeros_like(inv)
+    for index in range(shares):
+        cut = slice(index * piece, (index + 1) * piece)
+        grad, value = slices[index].astype(F32), state[:, cut]
+        mean = mean + jnp.sum(value * gain_two[:, cut] * grad, 1, keepdims=True)
+        gain_grad[:, cut] = jnp.sum(grad * value * inv, 0, keepdims=True)
+    mean = mean * (inv * inv * inv / width)
+    for index in range(shares):
+        cut = slice(index * piece, (index + 1) * piece)
+        grad = gain_two[:, cut] * slices[index].astype(F32)
+        d_state[:, cut] = upstream[:, cut].astype(F32) + inv * grad - state[:, cut] * mean
+
+    for index in range(2):
+        start = pl.multiple_of(core * wide + index * piece, piece)
+        grad = d_state[:, pl.ds(start, piece)]
+        both = jnp.concatenate(
+            [(att_gate[0] * grad).astype(BF), (att_gate[1] * grad).astype(BF)], 0
+        )
+        picked = mm(sel_att[...], both).astype(BF).reshape(owners, slots, piece)
+        rows_out[:, :, index * piece : (index + 1) * piece] = picked
+
+    def row_copy(step):
+        to = lax.rem(own + step, owners)
+        return remote(
+            rows_out.at[to],
+            d_rows.at[core, own],
+            row_send.at[step],
+            row_recv.at[step],
+            {"expert": to, "tensor": share},
+        )
+
+    each(owners, lambda step: row_copy(step).start())
+    d_rows[core, own] = rows_out[own]
+    each(owners, lambda step: row_copy(step).wait())
+    across = remote(d_rows.at[core], d_rows.at[core], one_send.at[1], one_recv.at[1], other)
+    across.start()
+    start = pl.multiple_of(core * wide, wide)
+    d_mixed = mm(d_rows[core].reshape(rows, wide), out_full[pl.ds(start, wide), :])
+    across.wait()
+    start = pl.multiple_of((1 - core) * wide, wide)
+    d_mixed = d_mixed + mm(d_rows[1 - core].reshape(rows, wide), out_full[pl.ds(start, wide), :])
+    d_mixed = d_mixed.astype(BF)
+    for column in range(columns):
+        for part in range(2):
+            heads_out[2 * column + part] = d_mixed[
+                part * head_rows : (part + 1) * head_rows, column * HD : (column + 1) * HD
+            ]
+
+    def head_copy(step):
+        to = lax.rem(own + step, owners)
+        return remote(
+            heads_out.at[to],
+            heads_in.at[own],
+            head_send.at[step],
+            head_recv.at[step],
+            {"expert": to, "tensor": share},
+        )
+
+    each(owners, lambda step: head_copy(step).start())
+    heads_in[own] = heads_out[own]
+
+    scale = HD ** (-0.5)
+    d_keys[...] = jnp.zeros_like(d_keys)
+    d_values[...] = jnp.zeros_like(d_values)
+
+    def attend(index):
+        span = pl.ds(pl.multiple_of(index * head_rows, head_rows), head_rows)
+        query, key, value, grad = queries[span, :], keys[...], values[...], heads_in[index]
+        scores = mm(query, key, 1, 1) * scale
+        visible = (row_seg[span, :] == key_seg[...]) & (key_pos[...] <= row_pos[span, :])
+        probs = jnp.where(visible, jnp.exp(scores - log_sum[span, :]), 0.0)
+        d_probs = mm(grad, value, 1, 1)
+        delta = jnp.sum(probs * d_probs, 1, keepdims=True)
+        d_scores = (probs * (d_probs - delta)).astype(BF)
+        d_query = mm(d_scores, key) * scale
+        d_query = d_query * cos_row[span, :] + pltpu.roll(d_query, HD // 2, 1) * sin_row[span, :]
+        queries_out[index] = d_query.astype(BF)
+        d_keys[...] += mm(d_scores, query, 0, 0)
+        d_values[...] += mm(probs.astype(BF), grad, 0, 0)
+
+    def query_copy(step):
+        to = lax.rem(own + owners - step, owners)
+        return remote(
+            queries_out.at[to],
+            queries_in.at[own],
+            back_send.at[step],
+            back_recv.at[step],
+            {"expert": to, "tensor": share},
+        )
+
+    def attend_other(step):
+        head_copy(step).wait()
+        attend(lax.rem(own + owners - step, owners))
+        query_copy(step).start()
+
+    attend(own)
+    queries_in[own] = queries_out[own]
+    each(owners, attend_other)
+
+    first = lax.rem(own, 2) == 0
+    pair_out[...] = jnp.where(first, d_values[...], d_keys[...] * scale).astype(BF)
+    pair = {"expert": own + 1 - 2 * lax.rem(own, 2), "tensor": share}
+    across = remote(pair_out, pair_in, one_send.at[2], one_recv.at[2], pair)
+    across.start()
+    each(owners, lambda step: query_copy(step).wait())
+    group = place_back.shape[1]
+    for part in range(2):
+        for index in range(columns):
+            block = part * columns + index
+            cut = slice(index * slots, (index + 1) * slots)
+            picked = jnp.concatenate(
+                [queries_in[2 * column + part, cut, :] for column in range(columns)], 1
+            )
+            d_proj[block * group : (block + 1) * group, : columns * HD] = mm(
+                place_back[block], picked
+            ).astype(BF)
+    across.wait()
+    mine = jnp.where(first, d_keys[...] * scale, d_values[...]) + pair_in[...].astype(F32)
+    turned = mine * cos_key[...] + pltpu.roll(mine, HD // 2, 1) * sin_key[...]
+    d_proj[:, columns * HD :] = jnp.where(first, turned, mine).astype(BF)
+
+
+def last_kernel(
+    d_proj,
+    weights,
+    output_part,
+    tokens,
+    inv_one,
+    gain_one,
+    d_state,
+    output,
+    input_grad,
+    gain_grad,
+    far,
+    near,
+    sibling,
+    landing,
+    slices,
+    one_send,
+    one_recv,
+    home_send,
+    home_recv,
+    slice_send,
+    slice_recv,
+):
+    own, share = lax.axis_index("expert"), lax.axis_index("tensor")
+    owners, shares = near.shape[1], slices.shape[0]
+    half, core = lax.div(share, 2), lax.rem(share, 2)
+    group, piece = near.shape[2], near.shape[3]
+    width = shares * piece
+    head_width = d_proj.shape[1] - HD
+    other = {"expert": own, "tensor": 2 * half + 1 - core}
+    enter(own, half, core, owners)
+    part = lax.rem(own, 2)
+
+    def product(index):
+        span = pl.ds(pl.multiple_of(index * piece, piece), piece)
+        queries = mm(d_proj[:, :head_width], weights[span, 3 * HD :], 1, 1)
+        side = weights[span, pl.ds(pl.multiple_of(part * HD, HD), HD)]
+        return (queries + mm(d_proj[:, head_width:], side, 1, 1)).reshape(owners, group, piece)
+
+    def across(side):
+        return remote(far.at[side], sibling.at[side], one_send.at[side], one_recv.at[side], other)
+
+    for side in range(2):
+        far[side] = product(2 * side + 1 - core).astype(BF)
+        across(side).start()
+    for side in range(2):
+        near[side] = product(2 * side + core).astype(BF)
+    for side in range(2):
+        across(side).wait()
+        near[side] = (near[side].astype(F32) + sibling[side].astype(F32)).astype(BF)
+    outgoing = send_home(near, landing, home_send, home_recv, own, half, core, owners)
+    wait_home(outgoing, owners)
+    total = jnp.zeros((group, piece), F32)
+    for side in range(2):
+        for index in range(owners):
+            total = total + landing[side, index].astype(F32)
+    slices[share, 0] = total.astype(BF)
+    slices[share, 1] = output_part[...]
+    share_slices(slices, slice_send, slice_recv, own, share, shares)
+    inv = inv_one[...]
+    mean = jnp.zeros_like(inv)
+    for index in range(shares):
+        cut = slice(index * piece, (index + 1) * piece)
+        grad, value = slices[index, 0].astype(F32), tokens[:, cut].astype(F32)
+        output[:, cut] = slices[index, 1]
+        mean = mean + jnp.sum(value * gain_one[:, cut] * grad, 1, keepdims=True)
+        gain_grad[:, cut] = jnp.sum(grad * value * inv, 0, keepdims=True)
+    mean = mean * (inv * inv * inv / width)
+    for index in range(shares):
+        cut = slice(index * piece, (index + 1) * piece)
+        grad = gain_one[:, cut] * slices[index, 0].astype(F32)
+        value = tokens[:, cut].astype(F32)
+        input_grad[:, cut] = d_state[:, cut] + inv * grad - value * mean
+
+
+def call_kernel(kernel, collective_id, outs, scratch, semaphores, args):
+    vmem = pl.BlockSpec(memory_space=pltpu.VMEM)
+    return pl.pallas_call(
+        kernel,
+        out_shape=[jax.ShapeDtypeStruct(shape, dtype) for shape, dtype in outs],
+        in_specs=[vmem] * len(args),
+        out_specs=[vmem] * len(outs),
+        scratch_shapes=[pltpu.VMEM(shape, dtype) for shape, dtype in scratch]
+        + [pltpu.SemaphoreType.DMA((count,)) for count in semaphores],
+        compiler_params=pltpu.CompilerParams(
+            collective_id=collective_id, has_side_effects=True, vmem_limit_bytes=56 * 2**20
+        ),
+    )(*args)
 
 
 def per_device(
@@ -80,34 +454,64 @@
     share = lax.axis_index("tensor")
     columns = owners // 2
     column_half = own % 2
-    att_cap = min(group, group * TOPK * 5 // (4 * ATT_EXP))
-    ffn_cap = min(group, group * TOPK * 5 // (4 * owners))
+    att_cap = -(-min(group, group * TOPK * 5 // (4 * ATT_EXP)) // 16) * 16
+    ffn_cap = -(-min(group, group * TOPK * 5 // (4 * owners)) // 16) * 16
     rows = owners * att_cap
     seq_len = owners * group
     piece = width // shares
     local = kv_weight.shape[0]
     head_width = kv_weight.shape[2]
 
+    def choice_places(places_here, routes):
+        names = jnp.arange(places_here.shape[0], dtype=jnp.int32)
+        picks = (routes[:, :, None] == names).astype(BF)
+        return jnp.einsum("mst,tjm->jtms", places_here, picks)
+
+    place_ffn = slot_places(ffn_routes[0], owners, ffn_cap)
+    pick_ffn = choice_places(place_ffn, ffn_routes[0])
+    ffn_gate = ffn_gates[0]
+    gate_slot = jnp.einsum("jtms,tj->ms", pick_ffn, ffn_gate, precision=lax.Precision.HIGHEST)
+    upstream = cotangent[0]
+    grad_rows = (dot("mst,td->msd", place_ffn, upstream) * gate_slot[:, :, None]).astype(BF)
+
     kv_parts = jnp.transpose(kv_weight.reshape(local, 2, columns, HD), (2, 0, 1, 3))
     kv_parts = jnp.repeat(kv_parts.reshape(columns, local, 2 * HD), 2, axis=0)
     gains = jnp.pad(jnp.stack([attn_gain, ffn_gain], 1), ((0, 0), (0, HD - 2)))
     gains = jnp.broadcast_to(gains[None], (owners, local, HD))
     first_pack = swap(jnp.concatenate([kv_parts, gains, query_weight], 2), "expert")
-    second_pack = swap(jnp.swapaxes(out_weight, 1, 2), "expert")
+    down_full = lax.all_gather(down_weight[0], "dp", axis=0, tiled=False)
+    marks = jnp.pad(att_routes[0].astype(BF), ((0, 0), (0, HD - TOPK)))
+    early = width * 5 // 8
+    token_pack = jnp.concatenate([tokens[0, :, early:], marks], 1)
+    early_tokens, first_pack = lax.optimization_barrier((tokens[0, :, :early], first_pack))
+    early_tokens = spread(early_tokens, "expert")
+    first_pack, down_full, early_tokens, token_pack, out_parts = lax.optimization_barrier(
+        (first_pack, down_full, early_tokens, token_pack, jnp.swapaxes(out_weight, 1, 2))
+    )
     first_full = lax.all_gather(first_pack.reshape(owners * local, -1), "dp", axis=0, tiled=True)
+    second_pack = swap(out_parts, "expert")
+    token_pack, second_pack, grad_rows = lax.optimization_barrier(
+        (token_pack, second_pack, grad_rows)
+    )
     out_full = lax.all_gather(second_pack.reshape(owners * local, -1), "dp", axis=0, tiled=True)
+    late_tokens = spread(token_pack, "expert")
+    late_tokens, grad_rows = lax.optimization_barrier((late_tokens, grad_rows))
+    expert_grad = swap(grad_rows, "expert").reshape(-1, width)
+    first_full, expert_grad = lax.optimization_barrier((first_full, expert_grad))
+    gate_up = jnp.concatenate([gate_weight[0], up_weight[0]], 1)
+    gate_up_full = lax.all_gather(gate_up, "dp", axis=0, tiled=True)
+    units = gate_weight.shape[2]
     key_value = first_full[:, : 2 * HD]
     gain_one = first_full[:, 2 * HD].astype(F32)
     gain_two = first_full[:, 2 * HD + 1].astype(F32)
     query_full = first_full[:, 3 * HD :]
-    gate_full = lax.all_gather(gate_weight[0], "dp", axis=0, tiled=True)
-    up_full = lax.all_gather(up_weight[0], "dp", axis=0, tiled=True)
-    down_full = lax.all_gather(down_weight[0], "dp", axis=0, tiled=False)
-
-    marks = jnp.pad(att_routes[0].astype(BF), ((0, 0), (0, HD - TOPK)))
-    gathered = spread(jnp.concatenate([tokens[0], marks], 1), "expert")
-    routes_all = gathered[:, :, width : width + TOPK].astype(jnp.int32)
-    inputs_all = gathered[:, :, :width].astype(F32)
+    gate_up = jnp.concatenate([gate_weight[0], up_weight[0]], 1)
+    out_full, gate_up = lax.optimization_barrier((out_full, gate_up))
+    gate_up_full = lax.all_gather(gate_up, "dp", axis=0, tiled=True)
+    units = gate_weight.shape[2]
+
+    routes_all = late_tokens[:, :, width - early : width - early + TOPK].astype(jnp.int32)
+    inputs_all = jnp.concatenate([early_tokens, late_tokens[:, :, : width - early]], 2).astype(F32)
     inv_all = lax.rsqrt(jnp.mean(inputs_all * inputs_all, -1, keepdims=True) + EPSILON)
     normed = (inputs_all * inv_all * gain_one).astype(BF)
     places = slot_places(routes_all, ATT_EXP, att_cap)
@@ -159,11 +563,6 @@
         parts = jnp.swapaxes(parts, 0, 1).reshape(owners * shares, -1, piece)
         return swap(parts, ("expert", "tensor"))
 
-    def choice_places(places_here, routes):
-        names = jnp.arange(places_here.shape[0], dtype=jnp.int32)
-        picks = (routes[:, :, None] == names).astype(BF)
-        return jnp.einsum("mst,tjm->jtms", places_here, picks)
-
     def from_slots(selection, parts):
         selection = jnp.broadcast_to(
             selection[..., None, :], selection.shape[:-1] + (shares, selection.shape[-1])
@@ -187,17 +586,10 @@
     inv_two = lax.rsqrt(jnp.mean(state * state, -1, keepdims=True) + EPSILON)
     normed_two = (state * inv_two * gain_two).astype(BF)
 
-    place_ffn = slot_places(ffn_routes[0], owners, ffn_cap)
-    pick_ffn = choice_places(place_ffn, ffn_routes[0])
-    ffn_gate = ffn_gates[0]
-    gate_slot = jnp.einsum("jtms,tj->ms", pick_ffn, ffn_gate, precision=lax.Precision.HIGHEST)
-    upstream = cotangent[0]
-    grad_rows = (dot("mst,td->msd", place_ffn, upstream) * gate_slot[:, :, None]).astype(BF)
-    expert_grad = swap(grad_rows, "expert").reshape(-1, width)
     send_rows = dot("mst,td->msd", place_ffn, normed_two).astype(BF)
     expert_in = swap(send_rows, "expert").reshape(-1, width)
-    gate_act = dot("cd,df->cf", expert_in, gate_full)
-    up_act = dot("cd,df->cf", expert_in, up_full)
+    both_act = dot("cd,df->cf", expert_in, gate_up_full)
+    gate_act, up_act = both_act[:, :units], both_act[:, units:]
     sigma = jax.nn.sigmoid(gate_act)
     hidden = (gate_act * sigma * up_act).astype(BF)
     expert_out = dot("cf,kfd->kcd", hidden, down_full)
@@ -210,83 +602,108 @@
     d_hidden = dot("ckd,kfd->cf", split_grad, down_full)
     d_gate = (d_hidden * up_act * sigma * (1.0 + gate_act * (1.0 - sigma))).astype(BF)
     d_up = (d_hidden * gate_act * sigma).astype(BF)
-    d_expert_in = dot("cf,df->cd", d_gate, gate_full) + dot("cf,df->cd", d_up, up_full)
-    d_expert_in = jnp.swapaxes(d_expert_in.reshape(-1, shares, piece), 0, 1)
-    d_norm_rows = to_blocks(d_expert_in)
-    d_normed_two = join(
-        from_slots(jnp.transpose(place_ffn, (2, 0, 1)), d_norm_rows).astype(BF)
-    ).astype(F32)
+    d_both = jnp.concatenate([d_gate, d_up], 1)
+    d_expert_in = dot("cf,df->cd", d_both, gate_up_full)
+    used = min(group, group * TOPK * 5 // (4 * owners))
+
+    def tight(array):
+        array = array.reshape((owners, ffn_cap) + array.shape[1:])[:, :used]
+        return array.reshape((-1,) + array.shape[2:])
+
+    hidden_all = lax.all_gather(tight(hidden), "dp", axis=0, tiled=True)
+    d_both_all = lax.all_gather(tight(d_both), "dp", axis=0, tiled=True)
+    slices = jnp.concatenate([expert_in.reshape(-1, dps, piece), expert_grad.reshape(-1, dps, piece)], 2)
+    slices = swap(jnp.swapaxes(tight(slices), 0, 1), "dp").reshape(-1, 2 * piece)
+    d_parts = jnp.transpose(d_expert_in.astype(BF).reshape(owners, ffn_cap, 2, 2, piece), (3, 2, 0, 1, 4))
 
     def scatter(grad):
         return lax.psum_scatter(grad.astype(BF), "dp", scatter_dimension=0, tiled=True)
 
-    down_grad = scatter(dot("cf,ckd->kfd", hidden, split_grad)).astype(F32)
-    gate_grad = scatter(dot("cd,cf->df", expert_in, d_gate)).astype(F32)[None]
-    up_grad = scatter(dot("cd,cf->df", expert_in, d_up)).astype(F32)[None]
-
-    upstream = upstream.astype(F32)
-    scaled_two = gain_two * d_normed_two
-    d_gain_two = jnp.sum(d_normed_two * state * inv_two, 0)
-    d_state = (
-        upstream
-        + inv_two * scaled_two
-        - state * inv_two**3 * jnp.mean(state * scaled_two, -1, keepdims=True)
-    )
-    d_branch = (att_gate.T[:, :, None] * d_state[None]).astype(BF)
-    branch_rows = dot("jtms,jtd->msd", pick_att, d_branch).astype(BF)
-    d_rows = swap(branch_rows, "expert").reshape(rows, width)
-    d_mixed = to_heads(dot("cd,dh->ch", d_rows, out_full))
-    out_grad = scatter(dot("cd,ch->dh", d_rows, mixed)).reshape(owners, local, head_width)
-    out_grad = jnp.swapaxes(swap(out_grad, "expert"), 1, 2).astype(F32)
-
-    scores = dot("qd,kd->qk", queries, keys) * scale
-    probs = jnp.where(visible, jnp.exp(scores - log_sum), 0.0)
-    d_probs = dot("qd,kd->qk", d_mixed, values)
-    delta = jnp.sum(probs * d_probs, -1, keepdims=True)
-    d_scores = (probs * (d_probs - delta)).astype(BF)
-    d_queries = dot("qk,kd->qd", d_scores, keys) * scale
-    d_keys = dot("qk,qd->kd", d_scores, queries) * scale
-    d_values = dot("qk,qd->kd", probs.astype(BF), d_mixed)
     cos_row, sin_row = rope_tables(row_pos)
-    d_query_rows = to_maps(rotate(d_queries, cos_row, -sin_row))
-    first = column_half == 0
-    pairs = [(i, i + 1 - 2 * (i % 2)) for i in range(owners)]
-    d_other = lax.ppermute(jnp.where(first, d_values, d_keys).astype(BF), "expert", pairs)
-    d_own = jnp.where(first, d_keys, d_values) + d_other.astype(F32)
-    d_own = jnp.where(first, rotate(d_own, cos_key, -sin_key), d_own).astype(BF)
-    own_weight = jnp.where(first, key_value[:, :HD], key_value[:, HD:])
-
-    d_query_tokens = dot(
-        "bst,bsh->bth", place_owned, d_query_rows.reshape(owners, att_cap, head_width)
-    )
-    d_proj = jnp.concatenate([d_query_tokens.astype(BF).reshape(seq_len, -1), d_own], 1)
-    weight_cat = jnp.concatenate([query_full, own_weight], 1).reshape(shares, piece, -1)
-    d_normed = dot("th,kdh->ktd", d_proj, weight_cat)
-    d_parts = to_blocks(d_normed)
-    d_normed_one = jnp.sum(d_parts.astype(F32), 0).astype(BF)
-    both = spread(jnp.concatenate([d_normed_one, output_part], 1), "tensor")
-    d_normed_one = jnp.swapaxes(both[:, :, :piece], 0, 1).reshape(group, width).astype(F32)
-    output = jnp.swapaxes(both[:, :, piece:], 0, 1).reshape(1, group, width)
-    scaled_one = gain_one * d_normed_one
+    slots = att_cap
+    d_state, d_gain_two, d_rows, d_proj = call_kernel(
+        middle_kernel,
+        1,
+        [
+            ((group, width), F32),
+            ((1, width), F32),
+            ((2, owners, slots, width // 2), BF),
+            ((seq_len, head_width + HD), BF),
+        ],
+        [
+            ((2, owners, ffn_cap, piece), BF),
+            ((2, owners, ffn_cap, piece), BF),
+            ((2, owners, ffn_cap, piece), BF),
+            ((shares, group, piece), BF),
+            ((owners, slots, width // 2), BF),
+            ((owners, columns * slots, HD), BF),
+            ((owners, columns * slots, HD), BF),
+            ((owners, columns * slots, HD), BF),
+            ((owners, columns * slots, HD), BF),
+            ((seq_len, HD), BF),
+            ((seq_len, HD), BF),
+            ((seq_len, HD), F32),
+            ((seq_len, HD), F32),
+        ],
+        [3, 3, 2 * owners, 2 * owners, shares, shares, owners, owners, owners, owners, owners, owners],
+        [
+            d_parts,
+            jnp.transpose(place_ffn, (2, 0, 1)).reshape(group, -1),
+            state,
+            inv_two,
+            upstream,
+            gain_two[None],
+            jnp.transpose(pick_att, (2, 3, 0, 1)).reshape(rows, -1),
+            att_gate.T[:, :, None],
+            out_full,
+            queries,
+            keys,
+            values,
+            log_sum,
+            row_pos[:, None],
+            row_seg[:, None],
+            key_pos[None],
+            key_seg[None],
+            jnp.concatenate([cos_row, cos_row], 1),
+            jnp.concatenate([sin_row, -sin_row], 1),
+            jnp.concatenate([cos_key, cos_key], 1),
+            jnp.concatenate([sin_key, -sin_key], 1),
+            jnp.swapaxes(place_owned, 1, 2),
+        ],
+    )
     inv_one = lax.rsqrt(jnp.mean(inputs * inputs, -1, keepdims=True) + EPSILON)
-    d_gain_one = jnp.sum(d_normed_one * inputs * inv_one, 0)
-    input_grad = (
-        d_state
-        + inv_one * scaled_one
-        - inputs * inv_one**3 * jnp.mean(inputs * scaled_one, -1, keepdims=True)
-    )[None]
-
+    output, input_grad, d_gain_one = call_kernel(
+        last_kernel,
+        2,
+        [((group, width), BF), ((group, width), F32), ((1, width), F32)],
+        [
+            ((2, owners, group, piece), BF),
+            ((2, owners, group, piece), BF),
+            ((2, owners, group, piece), BF),
+            ((2, owners, group, piece), BF),
+            ((shares, 2, group, piece), BF),
+        ],
+        [2, 2, 2 * owners, 2 * owners, shares, shares],
+        [d_proj, first_full, output_part, tokens[0], inv_one, gain_one[None], d_state],
+    )
+    out_grad = scatter(dot("kcd,ch->kdh", d_rows.reshape(2, rows, -1), mixed).reshape(width, -1))
+    out_grad = swap(out_grad.reshape(owners, local, head_width), "expert")
+    out_grad = jnp.swapaxes(out_grad, 1, 2).astype(F32)
+
+    down_grad = dot("cf,cd->fd", hidden_all, slices[:, piece:])[None]
+    gate_up_grad = dot("cd,cf->df", slices[:, :piece], d_both_all)
+    gate_grad, up_grad = gate_up_grad[None, :, :units], gate_up_grad[None, :, units:]
     map_grad = scatter(dot("td,th->dh", normed, d_proj)).reshape(owners, local, -1)
     map_grad = swap(map_grad, "expert").astype(F32)
     query_grad = map_grad[:, :, :head_width]
     kv_grad = jnp.transpose(
         map_grad[:, :, head_width:].reshape(columns, 2, local, HD), (2, 1, 0, 3)
     ).reshape(local, 2, head_width)
-    gain_grads = jnp.stack([d_gain_one, d_gain_two]).reshape(2, dps * owners, local)
+    gain_grads = jnp.stack([d_gain_one[0], d_gain_two[0]]).reshape(2, dps * owners, local)
     gain_grads = jnp.sum(swap(jnp.swapaxes(gain_grads, 0, 1), ("dp", "expert")), 0)
     return (
-        output,
-        input_grad,
+        output[None],
+        input_grad[None],
         kv_grad,
         query_grad,
         out_grad,

time: 699 us -> 647 us (0.926)
  Pallas kernels: 0 us -> 135 us
  waiting for transfers between devices: 280 us -> 192 us
  starting transfers between devices: 99.2 us -> 64.3 us
  matrix products: 119 us -> 84.7 us
  other arithmetic: 62.5 us -> 44.3 us
  local copies, waits for them, and re-layouts: 84 us -> 73.5 us
    pallas_call x0 -> x2, Pallas kernels: none -> 135 us  [call_kernel(): pl.pallas_call(kernel, out_shape=[jax.ShapeDtypeStruct(shape, dtype) for...]
    all_to_all x18 -> x13, waiting for transfers between devices: 223 us -> 135 us  [swap(): return lax.all_to_all(blocks, axes, split_axis=0, concat_axis=0, tiled=True)]
    dot_general x31 -> x19, matrix products: 111 us -> 77.4 us  [dot(): return jnp.einsum(spec, left, right, preferred_element_type=F32)]
    all_to_all x18 -> x13, starting transfers between devices: 97 us -> 64 us  [swap(): return lax.all_to_all(blocks, axes, split_axis=0, concat_axis=0, tiled=True)]
    all_gather x1, waiting for transfers between devices: 31 us -> 1.92 us  [per_device(): down_full = lax.all_gather(down_weight[0], 'dp', axis=0, tiled=False)]
    all_gather x2 -> x3, waiting for transfers between devices: 0.01 us -> 27.3 us  [the longest x1 27.3 us: per_device(): d_both_all = lax.all_gather(tight(d_both), 'dp', axis=0, tiled=True)]
    all_gather x1, waiting for transfers between devices: 0.02 us -> 26.4 us  [per_device(): lax.all_gather(second_pack.reshape(owners * local, -1), 'dp', axis=0, til...]
    reduce_scatter x5 -> x2, waiting for transfers between devices: 25 us -> 0.01 us  [scatter(): lax.psum_scatter(grad.astype(BF), 'dp', scatter_dimension=0, tiled=True)]
  transfers between devices with their start and end apart: 29 -> 21, of which waited for: 17 -> 13; matrix products, arithmetic and copies ran while one was open for 31% -> 23% of each run, Pallas kernels for 0% -> 10%
where the time goes in v2:
time: 647 us; the launch traced here: 638 us
  waiting for transfers between devices  192 us (30%)
  Pallas kernels  135 us (21%)
  matrix products  84.7 us (13%)
  local copies, waits for them, and re-layouts  73.5 us (11%)
  starting transfers between devices  64.3 us (10%)
  other arithmetic  44.3 us (7%)
  blocking collectives  28.3 us (4%)
  between operations  15.6 us (2%)
    pallas_call x2, Pallas kernels, call_kernel(): pl.pallas_call(kernel, out_shape=[jax.ShapeDtypeStruct(shape, dtype) for...  135 us
    all_to_all x13, waiting for transfers between devices, swap(): return lax.all_to_all(blocks, axes, split_axis=0, concat_axis=0, tiled=True)  135 us
    dot_general x19, matrix products, dot(): return jnp.einsum(spec, left, right, preferred_element_type=F32)  77.4 us
    all_to_all x13, starting transfers between devices, swap(): return lax.all_to_all(blocks, axes, split_axis=0, concat_axis=0, tiled=True)  64 us
    all_to_all x2, blocking collectives, swap(): return lax.all_to_all(blocks, axes, split_axis=0, concat_axis=0, tiled=True)  28.3 us
    all_gather x1, waiting for transfers between devices, per_device(): d_both_all = lax.all_gather(tight(d_both), 'dp', axis=0, tiled=True)  27.3 us
    all_gather x1, waiting for transfers between devices, per_device(): lax.all_gather(second_pack.reshape(owners * local, -1), 'dp', axis=0, til...  26.4 us
  transfers between devices with their start and end apart: 21, of which 13 were waited for; matrix products, arithmetic and copies ran while one was open for 23% of the time, Pallas kernels for 10%

profile of v2, /device:TPU:1, one launch (start us, length us, event | category | flops | bytes accessed | tf_op | source)
XLA Modules:
  0.0 638.1 jit_solution(3075170437830794174)
XLA Ops:
  10.1 6.2 all-to-all-start
  16.4 13.3 %all-to-all-done = bf16[8,64,896]{2,1,0:T(8,128)(2,1)S(1)} async-done(((bf16[8,64,896]{2,1,0:T(8,128)(2,1)}), bf16[8,64,896]{2,1,0:T(8,128)(2,1)S(1)}, u32[]{:S(2)}, u32[]{:S(2)}) %all-to-all-start) | async-done | bytes 917536 | tf_op jit(solution)/shard_map/all_to_all | solution.py:21
  35.7 36.6 %all-to-all-done.1 = bf16[8,128,1280]{2,1,0:T(8,128)(2,1)S(1)} async-done(((bf16[8,128,1280]{2,1,0:T(8,128)(2,1)}), bf16[8,128,1280]{2,1,0:T(8,128)(2,1)S(1)}, u32[]{:S(2)}, u32[]{:S(2)}) %all-to-all-start.1) | async-done | bytes 2621472 | tf_op jit(solution)/shard_map/all_to_all | solution.py:21
  74.3 5.0 all-to-all-start.2
  82.6 5.4 all-to-all-done.2
  93.2 26.4 %all-gather.11.cloned.1.call-done.out_full = bf16[2048,512]{1,0:T(8,128)(2,1)} async-done(((bf16[512,512]{1,0:T(8,128)(2,1)}), bf16[2048,512]{1,0:T(8,128)(2,1)}) %all-gather.11.cloned.1.call-update) | async-done | bytes 2097168 | tf_op jit(solution)/shard_map/all_gather | solution.py:496
  121.1 5.0 all-to-all-start.3
  127.0 25.8 %all-to-all-done.3 = bf16[8,128,896]{2,1,0:T(8,128)(2,1)S(1)} async-done(((bf16[8,128,896]{2,1,0:T(8,128)(2,1)}), bf16[8,128,896]{2,1,0:T(8,128)(2,1)S(1)}, u32[]{:S(2)}, u32[]{:S(2)}) %all-to-all-start.3) | async-done | bytes 1835040 | tf_op jit(solution)/shard_map/all_to_all | solution.py:21
  167.1 4.7 fusion.84
  171.8 6.6 %all-to-all-done.4 = bf16[8,48,2048]{2,1,0:T(8,128)(2,1)S(1)} async-done(((bf16[8,48,2048]{2,1,0:T(8,128)(2,1)}), bf16[8,48,2048]{2,1,0:T(8,128)(2,1)S(1)}, u32[]{:S(2)}, u32[]{:S(2)}) %all-to-all-start.4) | async-done | bytes 1572896 | tf_op jit(solution)/shard_map/all_to_all | solution.py:21
  187.8 5.6 fusion.21
  213.8 11.6 %all_to_all.75 = bf16[8,192,128]{2,1,0:T(8,128)(2,1)S(1)} all-to-all(bf16[8,192,128]{2,1,0:T(8,128)(2,1)S(1)} %bitcast.280), channel_id=1, replica_groups=mesh['dp'=4,'expert'=8,'tensor'=4] {'expert'}, dimensions={0} | all-to-all | bytes 786432 | tf_op jit(solution)/shard_map/all_to_all | solution.py:21
  229.9 8.9 %all-to-all-start.7 = ((bf16[32,48,512]{2,1,0:T(8,128)(2,1)}), bf16[32,48,512]{2,1,0:T(8,128)(2,1)S(1)}, u32[]{:S(2)}, u32[]{:S(2)}) async-start(bf16[32,48,512]{2,1,0:T(8,128)(2,1)} %bitcast.60), calls=%async_computation.7 | async-start | bytes 3145728 | tf_op jit(solution)/shard_map/all_to_all | solution.py:21
  241.8 19.2 %all-to-all-done.7 = bf16[32,48,512]{2,1,0:T(8,128)(2,1)S(1)} async-done(((bf16[32,48,512]{2,1,0:T(8,128)(2,1)}), bf16[32,48,512]{2,1,0:T(8,128)(2,1)S(1)}, u32[]{:S(2)}, u32[]{:S(2)}) %all-to-all-start.7) | async-done | bytes 1572896 | tf_op jit(solution)/shard_map/all_to_all | solution.py:21
  272.2 7.1 %all-to-all-done.8 = bf16[4,128,512]{2,1,0:T(8,128)(2,1)} async-done(((bf16[4,128,512]{2,1,0:T(8,128)(2,1)}), bf16[4,128,512]{2,1,0:T(8,128)(2,1)}, u32[]{:S(2)}, u32[]{:S(2)}) %all-to-all-start.8) | async-done | bytes 524320 | tf_op jit(solution)/shard_map/all_to_all | solution.py:21
  282.6 4.4 all-to-all-start.9
  298.1 9.5 %copy.112 = bf16[384,2048]{0,1:T(8,128)(2,1)} copy(bf16[384,2048]{1,0:T(8,128)(2,1)S(1)} %bitcast.234) | data formatting | bytes 3145728 | tf_op jit(solution)/shard_map/optimization_barrier | solution.py:500
  310.9 8.4 %fusion.89 = f32[384,2816]{1,0:T(8,128)S(1)} fusion(bf16[384,2048]{1,0:T(8,128)(2,1)} %bitcast.68, bf16[2048,2816]{1,0:T(8,128)(2,1)} %all-gather.13.cloned.1.call-done), kind=kOutput, calls=%fused_computation.168 | convolution fusion | flops 4429185024 | bytes 17432576 | tf_op jit(solution)/shard_map/cd,df->cf/dot_general | solution.py:17
  319.4 7.0 %multiply_convert_fusion.4 = (bf16[384,1408]{1,0:T(8,128)(2,1)S(1)}, bf16[384,1408]{1,0:T(8,128)(2,1)S(1)}, bf16[384,1408]{1,0:T(8,128)(2,1)}) fusion(f32[384,2816]{1,0:T(8,128)S(1)} %fusion.89, bf16[384,4,512]{0,2,1:T(8,128)(2,1)S(1)} %bitcast.255, bf16[4,1408,512]{2,1,0:T(8,128)(2,1)} %all-gather.7.cloned.1.call-done), kind=kOutput, calls=%fused_computation.35 | convolution fusion | flops 2223243264 | bytes 14909440 | tf_op jit(solution)/shard_map/ckd,kfd->cf/dot_general | solution.py:17
  327.7 12.9 %convolution_convert_fusion.2 = bf16[384,2048]{1,0:T(8,128)(2,1)} fusion(bf16[2048,2816]{1,0:T(8,128)(2,1)} %all-gather.13.cloned.1.call-done, bf16[384,1408]{1,0:T(8,128)(2,1)S(1)} %get-tuple-element.61, bf16[384,1408]{1,0:T(8,128)(2,1)S(1)} %get-tuple-element.60), kind=kOutput, calls=%fused_computation.27 | convolution fusion | flops 4434296832 | bytes 15269888 | tf_op jit(solution)/shard_map/cf,df->cd/dot_general | solution.py:17
  344.9 70.7 %shard_map.222 = (f32[128,2048]{1,0:T(8,128)}, f32[1,2048]{1,0:T(1,128)}, bf16[2,8,48,1024]{3,2,1,0:T(8,128)(2,1)}, bf16[1024,640]{1,0:T(8,128)(2,1)}) custom-call(bf16[2,2,8,48,512]{4,3,2,1,0:T(8,128)(2,1)} %bitcast.244, bf16[128,384]{1,0:T(8,128)(2,1)} %and_convert_fusion.sel_ffn, f32[128,2048]{1,0:T(8,128)} %copy-done.2, f32[128,1]{1,0:T(8,128)} %copy.131.inv_two, ...), custom_call_target="tpu_custom_call" | custom-call | tf_op jit(solution)/shard_map/pallas_call | solution.py:419
  422.5 7.3 %convolution_convert_fusion = bf16[2048,640]{1,0:T(8,128)(2,1)} fusion(bf16[1024,640]{1,0:T(8,128)(2,1)} %get-tuple-element.49.d_proj, bf16[1024,768]{1,0:T(8,128)(2,1)S(1)} %bitcast.241, bf16[1024,1280]{1,0:T(8,128)(2,1)} %bitcast.237, f32[2048]{0:T(1024)S(1)} %get-tuple-element.57, f32[1024]{0:T(1024)S(1)} %copy-done.48), kind=kOutput, calls=%fused_computation.18 | convolution fusion | flops 2700345344 | bytes 8138752 | tf_op jit(solution)/shard_map/td,th->dh/dot_general | solution.py:17
  435.4 5.3 convolution_convert_fusion.4
  442.0 6.6 %all-to-all-start.10 = ((bf16[32,48,512]{2,1,0:T(8,128)(2,1)}), bf16[32,48,512]{2,1,0:T(8,128)(2,1)S(1)}, u32[]{:S(2)}, u32[]{:S(2)}) async-start(bf16[32,48,512]{2,1,0:T(8,128)(2,1)} %bitcast.86), calls=%async_computation.10 | async-start | bytes 3145728 | tf_op jit(solution)/shard_map/all_to_all | solution.py:21
  459.8 10.9 %all-to-all-done.10 = bf16[32,48,512]{2,1,0:T(8,128)(2,1)S(1)} async-done(((bf16[32,48,512]{2,1,0:T(8,128)(2,1)}), bf16[32,48,512]{2,1,0:T(8,128)(2,1)S(1)}, u32[]{:S(2)}, u32[]{:S(2)}) %all-to-all-start.10) | async-done | bytes 1572896 | tf_op jit(solution)/shard_map/all_to_all | solution.py:21
  470.7 4.7 all-to-all-start.14
  480.8 64.8 %shard_map.223 = (bf16[128,2048]{1,0:T(8,128)(2,1)}, f32[128,2048]{1,0:T(8,128)}, f32[1,2048]{1,0:T(1,128)}) custom-call(bf16[1024,640]{1,0:T(8,128)(2,1)} %get-tuple-element.49.d_proj, bf16[2048,896]{1,0:T(8,128)(2,1)} %all-gather.9.cloned.1.call-done.weights, bf16[128,512]{1,0:T(8,128)(2,1)} %fusion.50.output_part, bf16[128,2048]{1,0:T(8,128)(2,1)} %bitcast.245, ...), custom_call_target="tpu_custom_call" | custom-call | tf_op jit(solution)/shard_map/pallas_call | solution.py:419
  546.6 16.7 %all_to_all.76 = f32[32,1,128]{2,1,0:T(1,128)S(1)} all-to-all(f32[32,1,128]{2,1,0:T(1,128)S(1)} %reshape.414), channel_id=1, replica_groups=mesh['dp'=4,'expert'=8,'tensor'=4] {'dp','expert'}, dimensions={0} | all-to-all | bytes 32768 | tf_op jit(solution)/shard_map/all_to_all | solution.py:21
  568.7 7.2 %all-to-all-done.12 = bf16[8,64,512]{2,1,0:T(8,128)(2,1)S(1)} async-done(((bf16[8,64,512]{2,1,0:T(8,128)(2,1)}), bf16[8,64,512]{2,1,0:T(8,128)(2,1)S(1)}, u32[]{:S(2)}, u32[]{:S(2)}) %all-to-all-start.12) | async-done | bytes 524320 | tf_op jit(solution)/shard_map/all_to_all | solution.py:21
  580.8 6.1 convolution_bitcast_fusion
  591.7 27.3 %all-gather.15.cloned.1.call-done = bf16[1280,2816]{1,0:T(8,128)(2,1)} async-done(((bf16[320,2816]{1,0:T(8,128)(2,1)}), bf16[1280,2816]{1,0:T(8,128)(2,1)}) %all-gather.15.cloned.1.call-update) | async-done | bytes 7208976 | tf_op jit(solution)/shard_map/all_gather | solution.py:614
  619.1 7.0 %fusion.18 = f32[512,2816]{1,0:T(8,128)S(1)} fusion(bf16[1280,2816]{1,0:T(8,128)(2,1)} %all-gather.15.cloned.1.call-done, bf16[1280,1024]{1,0:T(8,128)(2,1)} %bitcast.107), kind=kOutput, calls=%fused_computation.44 | convolution fusion | flops 3690987520 | bytes 14286848 | tf_op jit(solution)/shard_map/cd,cf->df/dot_general | solution.py:17
  (276 shorter events, 158.1 us)
Async XLA Ops:
  7.2 67.1 %all-gather.7.cloned.1.call-start = ((), (), s32[]{:S(2)}) async-start(), calls=%async_computation.17 | async-start | bytes 7208960 | tf_op jit(solution)/shard_map/all_gather | solution.py:482
  10.1 19.5 %all-to-all-start = ((bf16[8,64,896]{2,1,0:T(8,128)(2,1)}), bf16[8,64,896]{2,1,0:T(8,128)(2,1)S(1)}, u32[]{:S(2)}, u32[]{:S(2)}) async-start(bf16[8,64,896]{2,1,0:T(8,128)(2,1)} %pad_maximum_fusion.5), calls=%async_computation | async-start | bytes 1835008 | tf_op jit(solution)/shard_map/all_to_all | solution.py:21
  31.5 47.9 %copy-start.52 = (f32[1,128,2]{1,2,0:T(2,128)S(1)}, f32[1,128,2]{1,2,0:T(2,128)}, u32[]{:S(2)}) copy-start(f32[1,128,2]{1,2,0:T(2,128)} %param.21) | copy-start | bytes 3076
  31.5 40.9 %all-to-all-start.1 = ((bf16[8,128,1280]{2,1,0:T(8,128)(2,1)}), bf16[8,128,1280]{2,1,0:T(8,128)(2,1)S(1)}, u32[]{:S(2)}, u32[]{:S(2)}) async-start(bf16[8,128,1280]{2,1,0:T(8,128)(2,1)} %broadcast_in_dim.35), calls=%async_computation.1 | async-start | bytes 5242880 | tf_op jit(solution)/shard_map/all_to_all | solution.py:21
  35.4 54.1 %copy-start.36 = (pred[8,128]{1,0:T(8,128)(4,1)}, pred[8,128]{1,0:T(8,128)(4,1)S(1)}, u32[]{:S(2)}) copy-start(pred[8,128]{1,0:T(8,128)(4,1)S(1)} %fusion.71) | copy-start | bytes 3076
  35.6 57.5 %copy-start.38 = (bf16[128,8,2]{0,1,2:T(8,128)(2,1)}, bf16[128,8,2]{0,1,2:T(8,128)(2,1)S(1)}, u32[]{:S(2)}) copy-start(bf16[128,8,2]{0,1,2:T(8,128)(2,1)S(1)} %fusion.74) | copy-start | bytes 12292
  35.7 57.5 %copy-start.27 = (bf16[128,8,48]{0,2,1:T(8,128)(2,1)}, bf16[128,8,48]{0,2,1:T(8,128)(2,1)S(1)}, u32[]{:S(2)}) copy-start(bf16[128,8,48]{0,2,1:T(8,128)(2,1)S(1)} %fusion.60) | copy-start | bytes 294916
  74.3 13.7 %all-to-all-start.2 = ((bf16[8,64,512]{2,1,0:T(8,128)(2,1)}), bf16[8,64,512]{2,1,0:T(8,128)(2,1)S(1)}, u32[]{:S(2)}, u32[]{:S(2)}) async-start(bf16[8,64,512]{2,1,0:T(8,128)(2,1)} %bitcast.277), calls=%async_computation.2 | async-start | bytes 1048576 | tf_op jit(solution)/shard_map/all_to_all | solution.py:21
  79.3 40.3 %all-gather.11.cloned.1.call-start = ((), (), s32[]{:S(2)}) async-start(), calls=%async_computation.19 | async-start | bytes 2621440 | tf_op jit(solution)/shard_map/all_gather | solution.py:496
  88.8 89.6 %all-gather.9.cloned.1.call-start = ((), (), s32[]{:S(2)}) async-start(), calls=%async_computation.18 | async-start | bytes 4587520 | tf_op jit(solution)/shard_map/all_gather | solution.py:491
  89.5 221.4 %all-gather.13.cloned.1.call-start = ((), (), s32[]{:S(2)}) async-start(), calls=%async_computation.20 | async-start | bytes 14417920 | tf_op jit(solution)/shard_map/all_gather | solution.py:510
  121.1 31.6 %all-to-all-start.3 = ((bf16[8,128,896]{2,1,0:T(8,128)(2,1)}), bf16[8,128,896]{2,1,0:T(8,128)(2,1)S(1)}, u32[]{:S(2)}, u32[]{:S(2)}) async-start(bf16[8,128,896]{2,1,0:T(8,128)(2,1)} %broadcast_in_dim.36), calls=%async_computation.3 | async-start | bytes 3670016 | tf_op jit(solution)/shard_map/all_to_all | solution.py:21
  126.3 39.4 %copy-start.42 = (f32[64]{0:T(128)}, f32[64]{0:T(128)S(1)}, u32[]{:S(2)}) copy-start(f32[64]{0:T(128)S(1)} %negate_power_fusion) | copy-start | bytes 772
  152.7 25.7 %all-to-all-start.4 = ((bf16[8,48,2048]{2,1,0:T(8,128)(2,1)}), bf16[8,48,2048]{2,1,0:T(8,128)(2,1)S(1)}, u32[]{:S(2)}, u32[]{:S(2)}) async-start(bf16[8,48,2048]{2,1,0:T(8,128)(2,1)} %multiply_convert_fusion.1), calls=%async_computation.4 | async-start | bytes 3145728 | tf_op jit(solution)/shard_map/all_to_all | solution.py:21
  163.0 45.6 %copy-start.34 = (s32[1536]{0:T(1024)}, s32[1536]{0:T(1024)S(1)}, u32[]{:S(2)}) copy-start(s32[1536]{0:T(1024)S(1)} %convert_reduce_fusion.2) | copy-start | bytes 18436
  165.7 35.1 %copy-start.47 = (f32[1024]{0:T(1024)}, f32[1024]{0:T(1024)S(1)}, u32[]{:S(2)}) copy-start(f32[1024]{0:T(1024)S(1)} %get-tuple-element.85) | copy-start | bytes 12292
  187.8 93.0 %copy-start.29 = (f32[2048]{0:T(1024)}, f32[2048]{0:T(1024)S(1)}, u32[]{:S(2)}) copy-start(f32[2048]{0:T(1024)S(1)} %get-tuple-element.56) | copy-start | bytes 24580
  187.8 234.6 %copy-start.31 = (f32[2048]{0:T(1024)}, f32[2048]{0:T(1024)S(1)}, u32[]{:S(2)}) copy-start(f32[2048]{0:T(1024)S(1)} %get-tuple-element.57) | copy-start | bytes 24580
  196.4 12.2 %all-to-all-start.5 = ((bf16[8,192,128]{2,1,0:T(8,128)(2,1)}), bf16[8,192,128]{2,1,0:T(8,128)(2,1)}, u32[]{:S(2)}, u32[]{:S(2)}) async-start(bf16[8,192,128]{2,1,0:T(8,128)(2,1)} %bitcast.262), calls=%async_computation.5 | async-start | bytes 786432 | tf_op jit(solution)/shard_map/all_to_all | solution.py:21
  229.9 31.1 %all-to-all-start.7 = ((bf16[32,48,512]{2,1,0:T(8,128)(2,1)}), bf16[32,48,512]{2,1,0:T(8,128)(2,1)S(1)}, u32[]{:S(2)}, u32[]{:S(2)}) async-start(bf16[32,48,512]{2,1,0:T(8,128)(2,1)} %bitcast.60), calls=%async_computation.7 | async-start | bytes 3145728 | tf_op jit(solution)/shard_map/all_to_all | solution.py:21
  241.7 20.9 %copy-start.30 = (f32[128,2,1]{1,2,0:T(1,128)S(1)}, f32[128,2,1]{1,2,0:T(1,128)}, u32[]{:S(2)}) copy-start(f32[128,2,1]{1,2,0:T(1,128)} %copy.151) | copy-start | bytes 3076
  265.6 13.6 %all-to-all-start.8 = ((bf16[4,128,512]{2,1,0:T(8,128)(2,1)}), bf16[4,128,512]{2,1,0:T(8,128)(2,1)}, u32[]{:S(2)}, u32[]{:S(2)}) async-start(bf16[4,128,512]{2,1,0:T(8,128)(2,1)} %broadcast_in_dim.39), calls=%async_computation.8 | async-start | bytes 1048576 | tf_op jit(solution)/shard_map/all_to_all | solution.py:21
  282.6 28.3 %all-to-all-start.9 = ((bf16[8,48,2048]{2,1,0:T(8,128)(2,1)}), bf16[8,48,2048]{2,1,0:T(8,128)(2,1)}, u32[]{:S(2)}, u32[]{:S(2)}) async-start(bf16[8,48,2048]{2,1,0:T(8,128)(2,1)} %convolution_convert_fusion.3), calls=%async_computation.9 | async-start | bytes 3145728 | tf_op jit(solution)/shard_map/all_to_all | solution.py:21
  287.1 276.2 %reduce-scatter.5.cloned.1.call-start = ((), (), s32[]{:S(2)}) async-start(), calls=%async_computation.22 | async-start | bytes 2621440 | tf_op jit(solution)/shard_map/reduce_scatter | solution.py:620
  422.4 153.5 %reduce-scatter.3.cloned.1.call-start = ((), (), s32[]{:S(2)}) async-start(), calls=%async_computation.21 | async-start | bytes 3276800 | tf_op jit(solution)/shard_map/reduce_scatter | solution.py:620
  429.8 151.0 %all-gather.17.cloned.1.call-start = ((), (), s32[]{:S(2)}) async-start(), calls=%async_computation.24 | async-start | bytes 4505600 | tf_op jit(solution)/shard_map/all_gather | solution.py:613
  432.3 186.8 %all-gather.15.cloned.1.call-start = ((), (), s32[]{:S(2)}) async-start(), calls=%async_computation.23 | async-start | bytes 9011200 | tf_op jit(solution)/shard_map/all_gather | solution.py:614
  442.0 28.7 %all-to-all-start.10 = ((bf16[32,48,512]{2,1,0:T(8,128)(2,1)}), bf16[32,48,512]{2,1,0:T(8,128)(2,1)S(1)}, u32[]{:S(2)}, u32[]{:S(2)}) async-start(bf16[32,48,512]{2,1,0:T(8,128)(2,1)} %bitcast.86), calls=%async_computation.10 | async-start | bytes 3145728 | tf_op jit(solution)/shard_map/all_to_all | solution.py:21
  470.7 75.8 %all-to-all-start.14 = ((bf16[4,320,1024]{2,1,0:T(8,128)(2,1)}), bf16[4,320,1024]{2,1,0:T(8,128)(2,1)}, u32[]{:S(2)}, u32[]{:S(2)}) async-start(bf16[4,320,1024]{2,1,0:T(8,128)(2,1)} %bitcast.106), calls=%async_computation.16 | async-start | bytes 5242880 | tf_op jit(solution)/shard_map/all_to_all | solution.py:21
  480.8 64.8 %copy-start.41 = (f32[1,2048]{1,0:T(1,128)S(1)}, f32[1,2048]{1,0:T(1,128)}, u32[]{:S(2)}) copy-start(f32[1,2048]{1,0:T(1,128)} %get-tuple-element.55) | copy-start | bytes 24580
  563.3 12.6 %all-to-all-start.12 = ((bf16[8,64,512]{2,1,0:T(8,128)(2,1)}), bf16[8,64,512]{2,1,0:T(8,128)(2,1)S(1)}, u32[]{:S(2)}, u32[]{:S(2)}) async-start(bf16[8,64,512]{2,1,0:T(8,128)(2,1)} %bitcast.278), calls=%async_computation.14 | async-start | bytes 1048576 | tf_op jit(solution)/shard_map/all_to_all | solution.py:21
  575.9 13.6 %all-to-all-start.11 = ((bf16[8,64,640]{2,1,0:T(8,128)(2,1)}), bf16[8,64,640]{2,1,0:T(8,128)(2,1)S(1)}, u32[]{:S(2)}, u32[]{:S(2)}) async-start(bf16[8,64,640]{2,1,0:T(8,128)(2,1)} %bitcast.275), calls=%async_computation.12 | async-start | bytes 1310720 | tf_op jit(solution)/shard_map/all_to_all | solution.py:21
  (44 other events, 247.3 us)
Sparse Core Ops, SparseCore 0:
  9.7 64.5 all-gather.6
  88.9 30.6 all-gather.10
  121.8 43.9 all-gather.8
  167.9 109.9 all-gather.12
  422.5 28.5 reduce-scatter.4
  454.1 40.5 reduce-scatter.2
  497.1 47.4 all-gather.16
  546.3 72.6 all-gather.14

commit v3 on v2

v3 whole, which is shorter than its diff:
```python
import jax
import jax.numpy as jnp
import numpy as np
from jax import lax
from jax.experimental import pallas as pl
from jax.experimental.pallas import tpu as pltpu
from jax.sharding import PartitionSpec as P

HD = 128
ATT_EXP = 8
TOPK = 2
EPSILON = 1e-06
BF = jnp.bfloat16
F32 = jnp.float32


def dot(spec, left, right):
    return jnp.einsum(spec, left, right, preferred_element_type=F32)


def swap(blocks, axes):
    return lax.all_to_all(blocks, axes, split_axis=0, concat_axis=0, tiled=True)


def slot_places(routes, expert_count, capacity):
    length = routes.shape[-2]
    names = jnp.arange(expert_count, dtype=jnp.int32)[:, None]
    member = jnp.any(jnp.swapaxes(routes, -1, -2)[..., None, :] == names, -3)
    order = jnp.arange(length)
    before = (order[:, None] < order[None, :]).astype(BF)
    rank = dot("...et,tu->...eu", member.astype(BF), before)
    slots = jnp.arange(capacity, dtype=F32)[:, None]
    return (member[..., None, :] & (rank[..., None, :] == slots)).astype(BF)


def remote(src, dst, send, recv, device):
    return pltpu.make_async_remote_copy(
        src_ref=src,
        dst_ref=dst,
        send_sem=send,
        recv_sem=recv,
        device_id=device,
        device_id_type=pl.DeviceIdType.MESH,
    )


def each(count, body, start=1):
    def step(index, carry):
        body(index)
        return carry

    lax.fori_loop(start, count, step, 0)


def mm(left, right, left_dim=1, right_dim=0, precision=None):
    return lax.dot_general(
        left,
        right,
        (((left_dim,), (right_dim,)), ((), ())),
        precision=precision,
        preferred_element_type=F32,
    )


def enter(own, half, core, owners, around=()):
    semaphore = pltpu.get_barrier_semaphore()
    for index in around:
        pl.semaphore_signal(
            semaphore, inc=1, device_id={"dp": index}, device_id_type=pl.DeviceIdType.MESH
        )

    def hello(expert, tensor):
        pl.semaphore_signal(
            semaphore,
            inc=1,
            device_id={"expert": expert, "tensor": tensor},
            device_id_type=pl.DeviceIdType.MESH,
        )

    def column(step):
        hello(
            lax.rem(own + lax.div(step, 2), owners),
            2 * lax.rem(half + lax.rem(step, 2), 2) + core,
        )

    each(2 * owners, column)
    hello(own, 2 * half + 1 - core)
    hello(own, 2 * (1 - half) + 1 - core)
    pl.semaphore_wait(semaphore, 2 * owners + 1 + len(around))


def send_home(merged, landing, sends, recvs, own, half, core, owners):
    def outgoing(step):
        to, side = lax.rem(own + lax.div(step, 2), owners), lax.rem(half + lax.rem(step, 2), 2)
        return remote(
            merged.at[side, to],
            landing.at[half, own],
            sends.at[step],
            recvs.at[step],
            {"expert": to, "tensor": 2 * side + core},
        )

    each(2 * owners, lambda step: outgoing(step).start())
    landing[half, own] = merged[half, own]
    return outgoing


def wait_home(outgoing, owners):
    each(2 * owners, lambda step: outgoing(step).wait())


def share_slices(slices, sends, recvs, own, share, shares):
    def copy(step):
        return remote(
            slices.at[share],
            slices.at[share],
            sends.at[step],
            recvs.at[step],
            {"expert": own, "tensor": lax.rem(share + step, shares)},
        )

    each(shares, lambda step: copy(step).start())
    each(shares, lambda step: copy(step).wait())


class Ring:
    def __init__(self, buffer, sends, recvs, base, index, count):
        self.buffer, self.sends, self.recvs, self.base = buffer, sends, recvs, base
        self.index = index
        self.after, self.before = lax.rem(index + 1, count), lax.rem(index + count - 1, count)
        self.cut = buffer.shape[1] // 2

    def copy(self, kind, source=None):
        buffer, cut = self.buffer, self.cut
        if kind < 2:
            src = buffer.at[self.index] if source is None else source
            dst = buffer.at[self.index]
        elif kind == 2:
            src = dst = buffer.at[self.before, pl.ds(0, cut)]
        else:
            src = dst = buffer.at[self.after, pl.ds(cut, cut)]
        place = self.base + kind
        device = {"dp": self.after if kind % 2 == 0 else self.before}
        return remote(src, dst, self.sends.at[place], self.recvs.at[place], device)

    def start(self, source=None):
        self.copy(0, source).start()
        self.copy(1, source).start()

    def forward(self):
        self.copy(0).wait_recv()
        self.copy(2).start()
        self.copy(1).wait_recv()
        self.copy(3).start()

    def finish(self):
        self.copy(2).wait_recv()
        self.copy(3).wait_recv()

    def drain(self, source=None):
        self.copy(0, source).wait_send()
        self.copy(1, source).wait_send()
        self.copy(2).wait_send()
        self.copy(3).wait_send()


def first_kernel(
    tokens,
    marks,
    pack_one,
    pack_two,
    gate_weight,
    up_weight,
    down_weight,
    upstream,
    sel_ffn,
    gate_slot,
    pick_att,
    att_gate,
    pick_ffn,
    ffn_gate,
    ends,
    cos_key,
    sin_key,
    first_full,
    out_full,
    normed,
    gains,
    inv_one,
    queries,
    keys,
    values,
    row_info,
    cos_slot,
    sin_slot,
    place,
    mixed,
    state,
    inv_two,
    features_all,
    hidden,
    d_both,
    d_parts,
    output_part,
    features,
    expert_in,
    expert_grad,
    routes,
    slot_keys,
    inv_all,
    heads_out,
    mixed_out,
    mixed_in,
    far,
    near,
    sibling,
    landing,
    landing_two,
    slices,
    rows_out,
    grads_out,
    gate_up,
    down,
    act,
    ring_send,
    ring_recv,
    local,
    pack_send,
    pack_recv,
    token_send,
    token_recv,
    mark_send,
    mark_recv,
    one_send,
    one_recv,
    head_send,
    head_recv,
    back_send,
    back_recv,
    home_send,
    home_recv,
    home_two_send,
    home_two_recv,
    slice_send,
    slice_recv,
    row_send,
    row_recv,
    grad_send,
    grad_recv,
    feature_send,
    feature_recv,
):
    own, share, dp = lax.axis_index("expert"), lax.axis_index("tensor"), lax.axis_index("dp")
    owners, shares, dps = heads_out.shape[0], slices.shape[0], first_full.shape[0]
    half, core = lax.div(share, 2), lax.rem(share, 2)
    group, piece = slices.shape[1], slices.shape[2]
    width = shares * piece
    wide = width // 2
    slots = rows_out.shape[1]
    rows = owners * slots
    head_rows = heads_out.shape[1]
    columns = owners // 2
    part = lax.rem(own, 2)
    local_rows = pack_one.shape[1]
    units = gate_weight.shape[1]
    other = {"expert": own, "tensor": 2 * half + 1 - core}
    enter(own, half, core, owners, [lax.rem(dp + step, dps) for step in range(1, dps)])

    down_ring = Ring(down, ring_send, ring_recv, 0, dp, dps)
    one_ring = Ring(first_full, ring_send, ring_recv, 4, dp, dps)
    two_ring = Ring(out_full, ring_send, ring_recv, 8, dp, dps)
    gate_ring = Ring(gate_up.at[0], ring_send, ring_recv, 12, dp, dps)
    up_ring = Ring(gate_up.at[1], ring_send, ring_recv, 16, dp, dps)
    own_rows = pl.ds(pl.multiple_of(own * local_rows, local_rows), local_rows)

    def to_owner(src, dst, sends, recvs, step):
        to = lax.rem(own + step, owners)
        device = {"expert": to, "tensor": share}
        return remote(src(to), dst, sends.at[step], recvs.at[step], device)

    def pack_copy(step):
        return to_owner(pack_one.at.__getitem__, first_full.at[dp, own_rows], pack_send, pack_recv, step)

    def second_copy(step):
        to = lax.rem(own + step, owners)
        return remote(
            pack_two.at[to],
            out_full.at[dp, own_rows],
            pack_send.at[owners + step],
            pack_recv.at[owners + step],
            {"expert": to, "tensor": share},
        )

    def token_copy(step):
        start = pl.multiple_of(core * wide, wide)
        return to_owner(
            lambda to: tokens.at[:, pl.ds(start, wide)],
            normed.at[core, own],
            token_send,
            token_recv,
            step,
        )

    def mark_copy(step):
        return to_owner(lambda to: marks, routes.at[own], mark_send, mark_recv, step)

    down_ring.start(down_weight)
    each(owners, lambda step: pack_copy(step).start())
    each(owners, lambda step: mark_copy(step).start())
    each(owners, lambda step: token_copy(step).start())
    each(owners, lambda step: second_copy(step).start())
    own_copies = [
        pltpu.make_async_copy(pack_one.at[own], first_full.at[dp, own_rows], local.at[0]),
        pltpu.make_async_copy(pack_two.at[own], out_full.at[dp, own_rows], local.at[1]),
        pltpu.make_async_copy(gate_weight, gate_up.at[0, dp], local.at[2]),
        pltpu.make_async_copy(up_weight, gate_up.at[1, dp], local.at[3]),
        pltpu.make_async_copy(down_weight, down.at[dp], local.at[4]),
    ]
    for copy in own_copies:
        copy.start()
    routes[own] = marks[...]
    normed[core, own] = tokens[:, pl.ds(pl.multiple_of(core * wide, wide), wide)]

    own_copies[0].wait()
    each(owners, lambda step: pack_copy(step).wait())
    one_ring.start()
    each(owners, lambda step: mark_copy(step).wait())

    def picked_rows(source, out, scale):
        for index in range(2):
            cut = pl.ds(pl.multiple_of(core * wide + index * piece, piece), piece)
            taken = mm(sel_ffn[...], source[:, cut], 0, 0)
            if scale is not None:
                taken = taken * scale
            taken = taken.astype(BF).reshape(owners, slots, piece)
            out[:, :, index * piece : (index + 1) * piece] = taken

    picked_rows(upstream, grads_out, gate_slot[...])

    def grad_copy(step):
        return to_owner(grads_out.at.__getitem__, expert_grad.at[core, own], grad_send, grad_recv, step)

    token_rows = lax.broadcasted_iota(jnp.int32, (group, group), 0)
    token_columns = lax.broadcasted_iota(jnp.int32, (group, group), 1)
    before = (token_rows < token_columns).astype(F32).astype(BF)
    token_names = token_rows.astype(F32).astype(BF)
    slot_names = lax.broadcasted_iota(jnp.int32, (slots, group), 0).astype(F32)
    first_routes = jnp.concatenate([routes[index, 0:1, :] for index in range(owners)], 0)
    second_routes = jnp.concatenate([routes[index, 1:2, :] for index in range(owners)], 0)

    def map_keys(name):
        member = (first_routes == name) | (second_routes == name)
        rank = mm(jnp.where(member, 1.0, 0.0).astype(BF), before)
        return jnp.where(member, rank, -1.0)

    for name in range(owners):
        slot_keys[name] = map_keys(float(name))

    def one_hot(name, block):
        key = slot_keys[name, pl.ds(block, 1), :]
        return jnp.where(key == slot_names, 1.0, 0.0)

    def table(hot, array, block):
        span = pl.ds(pl.multiple_of(block * group, group), group)
        return mm(hot, array[span, :], precision=lax.Precision.HIGHEST)

    def row_block(index, carry):
        name, block = lax.div(index, columns), part * columns + lax.rem(index, columns)
        hot = one_hot(name, block)
        pos = mm(hot.astype(BF), token_names) + (block * group).astype(F32)
        start = jnp.zeros_like(pos)
        for end in range(ends.shape[0]):
            bound = ends[end : end + 1, :]
            start = jnp.maximum(start, jnp.where(bound <= pos, bound, 0.0))
        span = pl.ds(pl.multiple_of(index * slots, slots), slots)
        row_info[span, 0:1] = pos[:, 0:1]
        row_info[span, 1:2] = start[:, 0:1]
        return carry

    lax.fori_loop(0, owners * columns, row_block, 0)

    each(owners, lambda step: token_copy(step).wait())
    across = remote(normed.at[core], normed.at[core], one_send.at[0], one_recv.at[0], other)
    across.start()
    each(owners, lambda step: grad_copy(step).start())
    expert_grad[core, own] = grads_out[own]
    own_copies[1].wait()
    each(owners, lambda step: second_copy(step).wait())
    two_ring.start()
    gate_ring.start(gate_weight)
    up_ring.start(up_weight)
    across.wait()

    def squares(index, carry):
        low, high = normed[0, index].astype(F32), normed[1, index].astype(F32)
        total = jnp.sum(low * low, 1, keepdims=True) + jnp.sum(high * high, 1, keepdims=True)
        inv_all[index] = lax.rsqrt(total / width + EPSILON)
        return carry

    lax.fori_loop(0, owners, squares, 0)
    inv_one[...] = inv_all[own]
    one_ring.forward()
    down_ring.forward()
    one_ring.finish()

    for index in range(dps):
        turned = jnp.transpose(first_full[index, :, 2 * HD : 3 * HD].astype(F32))
        gains[:, index * piece : (index + 1) * piece] = turned[0:2, :]

    chosen = expert_in
    def norm_block(index, carry):
        hot = one_hot(own, index)
        place[index] = hot.astype(BF)
        span = pl.ds(pl.multiple_of(index * slots, slots), slots)
        cos_slot[span, :] = table(hot, cos_key, index)
        sin_slot[span, :] = table(hot, sin_key, index)
        for side in range(2):
            cut = slice(side * wide, (side + 1) * wide)
            rounded = normed[side, index].astype(F32) * inv_all[index] * gains[0:1, cut]
            rounded = rounded.astype(BF)
            normed[side, index] = rounded
            chosen[side, index] = mm(hot.astype(BF), rounded).astype(BF)
        return carry

    lax.fori_loop(0, owners, norm_block, 0)
    query = jnp.zeros((rows, columns * HD), F32)
    for index in range(dps):
        cut = slice((index % 2) * piece, (index % 2 + 1) * piece)
        taken = chosen[index // 2, :, :, cut].reshape(rows, piece)
        query = query + mm(taken, first_full[index, :, 3 * HD :])
    for column in range(columns):
        head = query[:, column * HD : (column + 1) * HD]
        head = (head * cos_slot[...] + pltpu.roll(head, HD // 2, 1) * sin_slot[...]).astype(BF)
        for side in range(2):
            heads_out[2 * column + side] = head[side * head_rows : (side + 1) * head_rows]

    def head_copy(step):
        return to_owner(heads_out.at.__getitem__, queries.at[own], head_send, head_recv, step)

    each(owners, lambda step: head_copy(step).start())
    queries[own] = heads_out[own]

    def key_block(index, carry):
        both = jnp.zeros((group, 2 * HD), F32)
        for step in range(dps):
            cut = slice((step % 2) * piece, (step % 2 + 1) * piece)
            both = both + mm(normed[step // 2, index, :, cut], first_full[step, :, : 2 * HD])
        span = pl.ds(pl.multiple_of(index * group, group), group)
        key = both[:, :HD]
        key = key * cos_key[span, :] + pltpu.roll(key, HD // 2, 1) * sin_key[span, :]
        keys[span, :] = key.astype(BF)
        values[span, :] = both[:, HD:].astype(BF)
        return carry

    lax.fori_loop(0, owners, key_block, 0)
    two_ring.forward()

    scale = HD ** (-0.5)
    key_pos = lax.broadcasted_iota(jnp.int32, (1, owners * group), 1).astype(F32)

    def attend(index):
        span = pl.ds(pl.multiple_of(index * head_rows, head_rows), head_rows)
        scores = mm(queries[index], keys[...], 1, 1) * scale
        visible = (key_pos <= row_info[span, 0:1]) & (key_pos >= row_info[span, 1:2])
        scores = jnp.where(visible, scores, -1e30)
        top = jnp.max(scores, 1, keepdims=True)
        shifted = jnp.exp(scores - top)
        total = jnp.sum(shifted, 1, keepdims=True)
        row_info[span, 2:3] = top + jnp.log(total)
        probs = (shifted / total).astype(BF)
        mixed_out[index] = mm(probs, values[...]).astype(BF)

    def back_copy(step):
        to = lax.rem(own + owners - step, owners)
        return remote(
            mixed_out.at[to],
            mixed_in.at[own],
            back_send.at[step],
            back_recv.at[step],
            {"expert": to, "tensor": share},
        )

    def attend_other(step):
        head_copy(step).wait()
        attend(lax.rem(own + owners - step, owners))
        back_copy(step).start()

    attend(own)
    mixed_in[own] = mixed_out[own]
    each(owners, attend_other)
    gate_ring.forward()
    two_ring.finish()
    each(owners, lambda step: back_copy(step).wait())
    for column in range(columns):
        for side in range(2):
            mixed[
                side * head_rows : (side + 1) * head_rows, column * HD : (column + 1) * HD
            ] = mixed_in[2 * column + side]

    def chip_sum(product, far, near, sibling, base):
        def across(side):
            place = base + side
            return remote(far.at[side], sibling.at[side], one_send.at[place], one_recv.at[place], other)

        for side in range(2):
            far[side] = product(2 * side + 1 - core)
            across(side).start()
        for side in range(2):
            near[side] = product(2 * side + core)
        for side in range(2):
            across(side).wait()
            near[side] = (near[side].astype(F32) + sibling[side].astype(F32)).astype(BF)

    def at_tokens(pick, gate, landing):
        total = jnp.zeros((group, piece), F32)
        for choice in range(TOPK):
            taken = mm(pick[choice], landing[0].reshape(rows, piece))
            taken = taken + mm(pick[choice], landing[1].reshape(rows, piece))
            total = total + gate[choice] * taken
        return total

    def map_product(index):
        return mm(mixed[...], out_full[index], 1, 1).astype(BF).reshape(owners, slots, piece)

    chip_sum(map_product, far, near, sibling, 1)
    outgoing = send_home(near, landing, home_send, home_recv, own, half, core, owners)
    up_ring.forward()
    wait_home(outgoing, owners)
    slices[share] = at_tokens(pick_att, att_gate, landing).astype(BF)
    share_slices(slices, slice_send, slice_recv, own, share, shares)

    total = jnp.zeros((group, 1), F32)
    for index in range(shares):
        cut = slice(index * piece, (index + 1) * piece)
        value = tokens[:, cut].astype(F32) + slices[index].astype(F32)
        state[:, cut] = value
        total = total + jnp.sum(value * value, 1, keepdims=True)
    inv = lax.rsqrt(total / width + EPSILON)
    inv_two[...] = inv
    for index in range(2):
        cut = pl.ds(pl.multiple_of(core * wide + index * piece, piece), piece)
        rounded = (state[:, cut] * inv * gains[1:2, cut]).astype(BF)
        taken = mm(sel_ffn[...], rounded, 0, 0).astype(BF).reshape(owners, slots, piece)
        rows_out[:, :, index * piece : (index + 1) * piece] = taken

    def row_copy(step):
        return to_owner(rows_out.at.__getitem__, expert_in.at[core, own], row_send, row_recv, step)

    each(owners, lambda step: row_copy(step).start())
    expert_in[core, own] = rows_out[own]
    each(owners, lambda step: grad_copy(step).wait())
    across = remote(expert_grad.at[core], expert_grad.at[core], one_send.at[5], one_recv.at[5], other)
    across.start()
    each(owners, lambda step: row_copy(step).wait())
    across_rows = remote(expert_in.at[core], expert_in.at[core], one_send.at[6], one_recv.at[6], other)
    across_rows.start()
    across.wait()
    across_rows.wait()

    used = hidden.shape[0] // owners

    def tight(array):
        pieces = [array[index * slots : index * slots + used] for index in range(owners)]
        return jnp.concatenate(pieces, 0)

    def loose(array):
        blank = jnp.zeros((slots - used, array.shape[1]), F32)
        pieces = []
        for index in range(owners):
            pieces += [array[index * used : (index + 1) * used], blank]
        return jnp.concatenate(pieces, 0).astype(BF).reshape(owners, slots, piece)

    for index in range(dps):
        cut = slice((index % 2) * piece, (index % 2 + 1) * piece)
        for side, source in enumerate((expert_in, expert_grad)):
            taken = source[index // 2, :, :, cut].reshape(rows, piece).astype(F32)
            features[index, :, side * piece : (side + 1) * piece] = tight(taken).astype(BF)
    def feature_copy(step):
        to = lax.rem(dp + step, dps)
        return remote(
            features.at[to],
            features_all.at[dp],
            feature_send.at[step],
            feature_recv.at[step],
            {"dp": to},
        )

    each(dps, lambda step: feature_copy(step).start())
    keep = pltpu.make_async_copy(features.at[dp], features_all.at[dp], feature_send.at[0])
    keep.start()
    for copy in own_copies[2:]:
        copy.wait()
    tile = 2 * HD

    def unit_tiles(body):
        def step(index, carry):
            body(pl.ds(pl.multiple_of(index * tile, tile), tile))
            return carry

        lax.fori_loop(0, units // tile, step, 0)
        if units % tile:
            body(pl.ds(units - units % tile, units % tile))

    gate_ring.finish()

    def gate_tile(cut):
        total = mm(features[0, :, :piece], gate_up[0, 0, :, cut])
        for index in range(1, dps):
            total = total + mm(features[index, :, :piece], gate_up[0, index, :, cut])
        act[0, :, cut] = total

    unit_tiles(gate_tile)
    up_ring.finish()

    def up_tile(cut):
        up = mm(features[0, :, :piece], gate_up[1, 0, :, cut])
        for index in range(1, dps):
            up = up + mm(features[index, :, :piece], gate_up[1, index, :, cut])
        act[1, :, cut] = up
        gate = act[0, :, cut]
        hidden[:, cut] = (gate / (1.0 + jnp.exp(-gate)) * up).astype(BF)

    unit_tiles(up_tile)
    down_ring.finish()
    chip_sum(lambda index: loose(mm(hidden[...], down[index])), far, near, sibling, 7)
    outgoing_two = send_home(
        near, landing_two, home_two_send, home_two_recv, own, half, core, owners
    )

    def grad_tile(cut):
        grad = mm(features[0, :, piece:], down[0, cut, :], 1, 1)
        for index in range(1, dps):
            grad = grad + mm(features[index, :, piece:], down[index, cut, :], 1, 1)
        gate, up = act[0, :, cut], act[1, :, cut]
        sigma = 1.0 / (1.0 + jnp.exp(-gate))
        d_both[0, :, cut] = (grad * up * sigma * (1.0 + gate * (1.0 - sigma))).astype(BF)
        d_both[1, :, cut] = (grad * gate * sigma).astype(BF)

    unit_tiles(grad_tile)
    for index in range(dps):
        total = mm(d_both[0], gate_up[0, index], 1, 1) + mm(d_both[1], gate_up[1, index], 1, 1)
        d_parts[index % 2, index // 2] = loose(total)
    wait_home(outgoing_two, owners)
    rest = at_tokens(pick_ffn, ffn_gate, landing_two)
    span = pl.ds(pl.multiple_of(share * piece, piece), piece)
    output_part[...] = (state[:, span] + rest).astype(BF)
    keep.wait()
    each(dps, lambda step: feature_copy(step).wait())
    one_ring.drain()
    two_ring.drain()
    gate_ring.drain(gate_weight)
    up_ring.drain(up_weight)
    down_ring.drain(down_weight)


def middle_kernel(
    parts,
    sel_ffn,
    state,
    inv_two,
    upstream,
    gains,
    sel_att,
    att_gate,
    out_full,
    queries,
    keys,
    values,
    row_info,
    cos_slot,
    sin_slot,
    cos_key,
    sin_key,
    place,
    hidden,
    d_both,
    d_state,
    gain_grad,
    d_rows,
    d_proj,
    hidden_all,
    d_both_all,
    sibling,
    merged,
    landing,
    slices,
    rows_out,
    heads_out,
    heads_in,
    queries_out,
    queries_in,
    pair_out,
    pair_in,
    d_keys,
    d_values,
    one_send,
    one_recv,
    home_send,
    home_recv,
    slice_send,
    slice_recv,
    row_send,
    row_recv,
    head_send,
    head_recv,
    back_send,
    back_recv,
    ring_send,
    ring_recv,
):
    own, share = lax.axis_index("expert"), lax.axis_index("tensor")
    owners, shares = heads_out.shape[0], slices.shape[0]
    half, core = lax.div(share, 2), lax.rem(share, 2)
    piece, width = slices.shape[2], state.shape[1]
    slots = merged.shape[2]
    rows = owners * slots
    wide = width // 2
    head_rows = heads_out.shape[1]
    columns = owners // 2
    other = {"expert": own, "tensor": 2 * half + 1 - core}
    dp, dps = lax.axis_index("dp"), hidden_all.shape[0]
    enter(own, half, core, owners, (lax.rem(dp + 1, dps), lax.rem(dp + dps - 1, dps)))

    both_ring = Ring(d_both_all, ring_send, ring_recv, 0, dp, dps)
    hidden_ring = Ring(hidden_all, ring_send, ring_recv, 4, dp, dps)
    both_ring.start(d_both)
    hidden_ring.start(hidden)
    keeps = [
        pltpu.make_async_copy(d_both, d_both_all.at[dp], ring_send.at[8]),
        pltpu.make_async_copy(hidden, hidden_all.at[dp], ring_send.at[9]),
    ]
    for keep in keeps:
        keep.start()

    across = remote(parts.at[1 - core], sibling, one_send.at[0], one_recv.at[0], other)
    across.start()
    across.wait()
    for side in range(2):
        merged[side] = (parts[core, side].astype(F32) + sibling[side].astype(F32)).astype(BF)
    outgoing = send_home(merged, landing, home_send, home_recv, own, half, core, owners)
    wait_home(outgoing, owners)
    total = mm(sel_ffn[...], landing[0].reshape(rows, piece))
    total = total + mm(sel_ffn[...], landing[1].reshape(rows, piece))
    slices[share] = total.astype(BF)
    share_slices(slices, slice_send, slice_recv, own, share, shares)

    inv = inv_two[...]
    mean = jnp.zeros_like(inv)
    for index in range(shares):
        cut = slice(index * piece, (index + 1) * piece)
        grad, value = slices[index].astype(F32), state[:, cut]
        mean = mean + jnp.sum(value * gains[1:2, cut] * grad, 1, keepdims=True)
        gain_grad[:, cut] = jnp.sum(grad * value * inv, 0, keepdims=True)
    mean = mean * (inv * inv * inv / width)
    for index in range(shares):
        cut = slice(index * piece, (index + 1) * piece)
        grad = gains[1:2, cut] * slices[index].astype(F32)
        d_state[:, cut] = upstream[:, cut].astype(F32) + inv * grad - state[:, cut] * mean

    for index in range(2):
        start = pl.multiple_of(core * wide + index * piece, piece)
        grad = d_state[:, pl.ds(start, piece)]
        both = jnp.concatenate(
            [(att_gate[0] * grad).astype(BF), (att_gate[1] * grad).astype(BF)], 0
        )
        picked = mm(sel_att[...], both).astype(BF).reshape(owners, slots, piece)
        rows_out[:, :, index * piece : (index + 1) * piece] = picked

    def row_copy(step):
        to = lax.rem(own + step, owners)
        return remote(
            rows_out.at[to],
            d_rows.at[core, own],
            row_send.at[step],
            row_recv.at[step],
            {"expert": to, "tensor": share},
        )

    each(owners, lambda step: row_copy(step).start())
    d_rows[core, own] = rows_out[own]
    each(owners, lambda step: row_copy(step).wait())
    across = remote(d_rows.at[core], d_rows.at[core], one_send.at[1], one_recv.at[1], other)
    across.start()

    def half_product(side):
        taken = d_rows[side].reshape(rows, wide)
        return mm(taken[:, :piece], out_full[2 * side]) + mm(taken[:, piece:], out_full[2 * side + 1])

    d_mixed = half_product(core)
    across.wait()
    d_mixed = (d_mixed + half_product(1 - core)).astype(BF)
    for column in range(columns):
        for part in range(2):
            heads_out[2 * column + part] = d_mixed[
                part * head_rows : (part + 1) * head_rows, column * HD : (column + 1) * HD
            ]

    def head_copy(step):
        to = lax.rem(own + step, owners)
        return remote(
            heads_out.at[to],
            heads_in.at[own],
            head_send.at[step],
            head_recv.at[step],
            {"expert": to, "tensor": share},
        )

    each(owners, lambda step: head_copy(step).start())
    heads_in[own] = heads_out[own]

    scale = HD ** (-0.5)
    key_pos = lax.broadcasted_iota(jnp.int32, (1, keys.shape[0]), 1).astype(F32)
    d_keys[...] = jnp.zeros_like(d_keys)
    d_values[...] = jnp.zeros_like(d_values)

    def attend(index):
        span = pl.ds(pl.multiple_of(index * head_rows, head_rows), head_rows)
        query, key, value, grad = queries[index], keys[...], values[...], heads_in[index]
        scores = mm(query, key, 1, 1) * scale
        visible = (key_pos <= row_info[span, 0:1]) & (key_pos >= row_info[span, 1:2])
        probs = jnp.where(visible, jnp.exp(scores - row_info[span, 2:3]), 0.0)
        d_probs = mm(grad, value, 1, 1)
        delta = jnp.sum(probs * d_probs, 1, keepdims=True)
        d_scores = (probs * (d_probs - delta)).astype(BF)
        queries_out[index] = (mm(d_scores, key) * scale).astype(BF)
        d_keys[...] += mm(d_scores, query, 0, 0)
        d_values[...] += mm(probs.astype(BF), grad, 0, 0)

    def query_copy(step):
        to = lax.rem(own + owners - step, owners)
        return remote(
            queries_out.at[to],
            queries_in.at[own],
            back_send.at[step],
            back_recv.at[step],
            {"expert": to, "tensor": share},
        )

    def attend_other(step):
        head_copy(step).wait()
        attend(lax.rem(own + owners - step, owners))
        query_copy(step).start()

    both_ring.forward()
    attend(own)
    queries_in[own] = queries_out[own]
    each(owners, attend_other)

    first = lax.rem(own, 2) == 0
    pair_out[...] = jnp.where(first, d_values[...], d_keys[...] * scale).astype(BF)
    pair = {"expert": own + 1 - 2 * lax.rem(own, 2), "tensor": share}
    across = remote(pair_out, pair_in, one_send.at[2], one_recv.at[2], pair)
    across.start()
    each(owners, lambda step: query_copy(step).wait())
    group = place.shape[2]
    for part in range(2):
        for index in range(columns):
            block = part * columns + index
            cut = slice(index * slots, (index + 1) * slots)
            span = slice(block * slots, (block + 1) * slots)
            turned = []
            for column in range(columns):
                grad = queries_in[2 * column + part, cut, :].astype(F32)
                back = pltpu.roll(grad, HD // 2, 1) * sin_slot[span, :]
                turned.append((grad * cos_slot[span, :] - back).astype(BF))
            picked = jnp.concatenate(turned, 1)
            d_proj[block * group : (block + 1) * group, : columns * HD] = mm(
                place[block], picked, 0, 0
            ).astype(BF)
    hidden_ring.forward()
    across.wait()
    mine = jnp.where(first, d_keys[...] * scale, d_values[...]) + pair_in[...].astype(F32)
    turned = mine * cos_key[...] + pltpu.roll(mine, HD // 2, 1) * sin_key[...]
    d_proj[:, columns * HD :] = jnp.where(first, turned, mine).astype(BF)
    both_ring.finish()
    hidden_ring.finish()
    both_ring.drain(d_both)
    hidden_ring.drain(hidden)
    for keep in keeps:
        keep.wait()


def last_kernel(
    d_proj,
    weights,
    output_part,
    tokens,
    inv_one,
    gains,
    d_state,
    output,
    input_grad,
    gain_grad,
    far,
    near,
    sibling,
    landing,
    slices,
    one_send,
    one_recv,
    home_send,
    home_recv,
    slice_send,
    slice_recv,
):
    own, share = lax.axis_index("expert"), lax.axis_index("tensor")
    owners, shares = near.shape[1], slices.shape[0]
    half, core = lax.div(share, 2), lax.rem(share, 2)
    group, piece = near.shape[2], near.shape[3]
    width = shares * piece
    head_width = d_proj.shape[1] - HD
    other = {"expert": own, "tensor": 2 * half + 1 - core}
    enter(own, half, core, owners)
    part = lax.rem(own, 2)

    def product(index):
        queries = mm(d_proj[:, :head_width], weights[index, :, 3 * HD :], 1, 1)
        side = weights[index, :, pl.ds(pl.multiple_of(part * HD, HD), HD)]
        return (queries + mm(d_proj[:, head_width:], side, 1, 1)).reshape(owners, group, piece)

    def across(side):
        return remote(far.at[side], sibling.at[side], one_send.at[side], one_recv.at[side], other)

    for side in range(2):
        far[side] = product(2 * side + 1 - core).astype(BF)
        across(side).start()
    for side in range(2):
        near[side] = product(2 * side + core).astype(BF)
    for side in range(2):
        across(side).wait()
        near[side] = (near[side].astype(F32) + sibling[side].astype(F32)).astype(BF)
    outgoing = send_home(near, landing, home_send, home_recv, own, half, core, owners)
    wait_home(outgoing, owners)
    total = jnp.zeros((group, piece), F32)
    for side in range(2):
        for index in range(owners):
            total = total + landing[side, index].astype(F32)
    slices[share, 0] = total.astype(BF)
    slices[share, 1] = output_part[...]
    share_slices(slices, slice_send, slice_recv, own, share, shares)
    inv = inv_one[...]
    mean = jnp.zeros_like(inv)
    for index in range(shares):
        cut = slice(index * piece, (index + 1) * piece)
        grad, value = slices[index, 0].astype(F32), tokens[:, cut].astype(F32)
        output[:, cut] = slices[index, 1]
        mean = mean + jnp.sum(value * gains[0:1, cut] * grad, 1, keepdims=True)
        gain_grad[:, cut] = jnp.sum(grad * value * inv, 0, keepdims=True)
    mean = mean * (inv * inv * inv / width)
    for index in range(shares):
        cut = slice(index * piece, (index + 1) * piece)
        grad = gains[0:1, cut] * slices[index, 0].astype(F32)
        value = tokens[:, cut].astype(F32)
        input_grad[:, cut] = d_state[:, cut] + inv * grad - value * mean


def call_kernel(kernel, collective_id, outs, scratch, semaphores, args, far_args=(), far_outs=()):
    def specs(count, far):
        spaces = [pl.ANY if index in far else pltpu.VMEM for index in range(count)]
        return [pl.BlockSpec(memory_space=space) for space in spaces]

    return pl.pallas_call(
        kernel,
        out_shape=[jax.ShapeDtypeStruct(shape, dtype) for shape, dtype in outs],
        in_specs=specs(len(args), far_args),
        out_specs=specs(len(outs), far_outs),
        scratch_shapes=[pltpu.VMEM(shape, dtype) for shape, dtype in scratch]
        + [pltpu.SemaphoreType.DMA((count,)) for count in semaphores],
        compiler_params=pltpu.CompilerParams(
            collective_id=collective_id, has_side_effects=True, vmem_limit_bytes=60 * 2**20
        ),
    )(*args)


def per_device(
    tokens,
    cotangent,
    doc_lengths,
    att_routes,
    att_gates,
    ffn_routes,
    ffn_gates,
    kv_weight,
    query_weight,
    out_weight,
    attn_gain,
    ffn_gain,
    gate_weight,
    up_weight,
    down_weight,
):
    _, group, width = tokens.shape
    owners = lax.axis_size("expert")
    shares = lax.axis_size("tensor")
    dps = lax.axis_size("dp")
    own = lax.axis_index("expert")
    share = lax.axis_index("tensor")
    columns = owners // 2
    column_half = own % 2
    att_cap = -(-min(group, group * TOPK * 5 // (4 * ATT_EXP)) // 16) * 16
    ffn_cap = -(-min(group, group * TOPK * 5 // (4 * owners)) // 16) * 16
    rows = owners * att_cap
    seq_len = owners * group
    piece = width // shares
    local = kv_weight.shape[0]
    head_width = kv_weight.shape[2]

    def choice_places(places_here, routes):
        names = jnp.arange(places_here.shape[0], dtype=jnp.int32)
        picks = (routes[:, :, None] == names).astype(BF)
        return jnp.einsum("mst,tjm->jtms", places_here, picks)

    place_ffn = slot_places(ffn_routes[0], owners, ffn_cap)
    pick_ffn = choice_places(place_ffn, ffn_routes[0])
    ffn_gate = ffn_gates[0]
    gate_slot = jnp.einsum("jtms,tj->ms", pick_ffn, ffn_gate, precision=lax.Precision.HIGHEST)

    kv_parts = jnp.transpose(kv_weight.reshape(local, 2, columns, HD), (2, 0, 1, 3))
    kv_parts = jnp.repeat(kv_parts.reshape(columns, local, 2 * HD), 2, axis=0)
    both_gains = jnp.pad(jnp.stack([attn_gain, ffn_gain], 1), ((0, 0), (0, HD - 2)))
    both_gains = jnp.broadcast_to(both_gains[None], (owners, local, HD))
    pack_one = jnp.concatenate([kv_parts, both_gains, query_weight], 2)
    pack_two = jnp.swapaxes(out_weight, 1, 2)
    marks = jnp.pad(att_routes[0].T.astype(F32), ((0, 8 - TOPK), (0, 0)), constant_values=-1.0)
    place_att = slot_places(att_routes[0], ATT_EXP, att_cap)
    pick_att = choice_places(place_att, att_routes[0])
    att_gate = att_gates[0]
    ends = jnp.cumsum(doc_lengths[0], dtype=jnp.int32).astype(F32)
    ends = jnp.broadcast_to(ends[:, None], (ends.shape[0], HD))
    angles = np.arange(seq_len)[:, None] * 10000.0 ** (-np.arange(HD // 2) * 2.0 / HD)
    cos_key = jnp.asarray(np.concatenate([np.cos(angles)] * 2, 1), F32)
    sin_key = jnp.asarray(np.concatenate([-np.sin(angles), np.sin(angles)], 1), F32)
    used = min(group, group * TOPK * 5 // (4 * owners))
    units = gate_weight.shape[2]
    slots = att_cap
    head_rows = columns * slots
    block = (2, owners, slots, piece)
    (
        first_full,
        out_full,
        normed,
        gains,
        inv_one,
        queries,
        keys,
        values,
        row_info,
        cos_slot,
        sin_slot,
        place,
        mixed,
        state,
        inv_two,
        features_all,
        hidden,
        d_both,
        d_parts,
        output_part,
    ) = call_kernel(
        first_kernel,
        3,
        [
            ((dps, owners * local, 3 * HD + head_width), BF),
            ((dps, owners * local, head_width), BF),
            ((2, owners, group, width // 2), BF),
            ((2, width), F32),
            ((group, 1), F32),
            ((owners, head_rows, HD), BF),
            ((seq_len, HD), BF),
            ((seq_len, HD), BF),
            ((owners * head_rows, HD), F32),
            ((rows, HD), F32),
            ((rows, HD), F32),
            ((owners, slots, group), BF),
            ((rows, head_width), BF),
            ((group, width), F32),
            ((group, 1), F32),
            ((dps, owners * used, 2 * piece), BF),
            ((owners * used, units), BF),
            ((2, owners * used, units), BF),
            ((2,) + block, BF),
            ((group, piece), BF),
        ],
        [
            ((dps, owners * used, 2 * piece), BF),
            ((2, owners, slots, width // 2), BF),
            ((2, owners, slots, width // 2), BF),
            ((owners, 8, group), F32),
            ((owners, owners, group), F32),
            ((owners, group, 1), F32),
            ((owners, head_rows, HD), BF),
            ((owners, head_rows, HD), BF),
            ((owners, head_rows, HD), BF),
        ]
        + [(block, BF)] * 5
        + [
            ((shares, group, piece), BF),
            ((owners, slots, width // 2), BF),
            ((owners, slots, width // 2), BF),
            ((2, dps, width // dps, units), BF),
            ((dps, units, piece), BF),
            ((2, owners * used, units), F32),
        ],
        [20, 20, 5, 2 * owners, 2 * owners]
        + [owners] * 4
        + [9, 9]
        + [owners] * 4
        + [2 * owners] * 4
        + [shares, shares]
        + [owners] * 4
        + [dps, dps],
        [
            tokens[0],
            marks,
            pack_one,
            pack_two,
            gate_weight[0],
            up_weight[0],
            down_weight[0],
            cotangent[0],
            jnp.transpose(place_ffn, (2, 0, 1)).reshape(group, -1),
            gate_slot.reshape(-1, 1),
            pick_att.reshape(TOPK, group, rows),
            att_gate.T[:, :, None],
            pick_ffn.reshape(TOPK, group, rows),
            ffn_gate.T[:, :, None],
            ends,
            cos_key,
            sin_key,
        ],
        far_args=(2, 3, 4, 5, 6),
        far_outs=(15,),
    )

    def scatter(grad):
        return lax.psum_scatter(grad.astype(BF), "dp", scatter_dimension=0, tiled=True)

    d_state, d_gain_two, d_rows, d_proj, hidden_all, d_both_all = call_kernel(
        middle_kernel,
        1,
        [
            ((group, width), F32),
            ((1, width), F32),
            ((2, owners, slots, width // 2), BF),
            ((seq_len, head_width + HD), BF),
            ((dps, owners * used, units), BF),
            ((dps, 2 * owners * used, units), BF),
        ],
        [
            (block, BF),
            (block, BF),
            (block, BF),
            ((shares, group, piece), BF),
            ((owners, slots, width // 2), BF),
            ((owners, columns * slots, HD), BF),
            ((owners, columns * slots, HD), BF),
            ((owners, columns * slots, HD), BF),
            ((owners, columns * slots, HD), BF),
            ((seq_len, HD), BF),
            ((seq_len, HD), BF),
            ((seq_len, HD), F32),
            ((seq_len, HD), F32),
        ],
        [3, 3, 2 * owners, 2 * owners, shares, shares] + [owners] * 6 + [10, 8],
        [
            d_parts,
            jnp.transpose(place_ffn, (2, 0, 1)).reshape(group, -1),
            state,
            inv_two,
            cotangent[0],
            gains,
            jnp.transpose(pick_att, (2, 3, 0, 1)).reshape(rows, -1),
            att_gate.T[:, :, None],
            out_full,
            queries,
            keys,
            values,
            row_info,
            cos_slot,
            sin_slot,
            cos_key,
            -sin_key,
            place,
            hidden,
            d_both.reshape(2 * owners * used, units),
        ],
        far_args=(18, 19),
        far_outs=(4, 5),
    )
    output, input_grad, d_gain_one = call_kernel(
        last_kernel,
        2,
        [((group, width), BF), ((group, width), F32), ((1, width), F32)],
        [((2, owners, group, piece), BF)] * 4 + [((shares, 2, group, piece), BF)],
        [2, 2, 2 * owners, 2 * owners, shares, shares],
        [d_proj, first_full, output_part, tokens[0], inv_one, gains, d_state],
    )
    normed = normed.reshape(2, seq_len, width // 2)
    out_grad = scatter(dot("kcd,ch->kdh", d_rows.reshape(2, rows, -1), mixed).reshape(width, -1))
    out_grad = swap(out_grad.reshape(owners, local, head_width), "expert")
    out_grad = jnp.swapaxes(out_grad, 1, 2).astype(F32)

    slices = features_all.reshape(-1, 2 * piece)
    d_both_all = d_both_all.reshape(dps, 2, -1, units)
    down_grad = dot("cf,cd->fd", hidden_all.reshape(-1, units), slices[:, piece:])[None]
    inputs_all = features_all[:, :, :piece]
    gate_grad = dot("scd,scf->df", inputs_all, d_both_all[:, 0])[None]
    up_grad = dot("scd,scf->df", inputs_all, d_both_all[:, 1])[None]
    map_grad = scatter(dot("std,th->sdh", normed, d_proj).reshape(width, -1))
    map_grad = map_grad.reshape(owners, local, -1)
    map_grad = swap(map_grad, "expert").astype(F32)
    query_grad = map_grad[:, :, :head_width]
    kv_grad = jnp.transpose(
        map_grad[:, :, head_width:].reshape(columns, 2, local, HD), (2, 1, 0, 3)
    ).reshape(local, 2, head_width)
    gain_grads = jnp.stack([d_gain_one[0], d_gain_two[0]]).reshape(2, dps * owners, local)
    gain_grads = jnp.sum(swap(jnp.swapaxes(gain_grads, 0, 1), ("dp", "expert")), 0)
    return (
        output[None],
        input_grad[None],
        kv_grad,
        query_grad,
        out_grad,
        gain_grads[0],
        gain_grads[1],
        gate_grad,
        up_grad,
        down_grad,
    )


def solution(mesh):
    in_specs = (
        P("dp", "expert", None),
        P("dp", "expert", None),
        P("dp", None),
        P("dp", "expert", None),
        P("dp", "expert", None),
        P("dp", "expert", None),
        P("dp", "expert", None),
        P(("dp", "expert"), None, "tensor"),
        P(None, ("dp", "expert"), "tensor"),
        P(None, "tensor", ("dp", "expert")),
        P(("dp", "expert")),
        P(("dp", "expert")),
        P("expert", "dp", "tensor"),
        P("expert", "dp", "tensor"),
        P("expert", "tensor", "dp"),
    )
    out_specs = (
        P("dp", "expert", None),
        P("dp", "expert", None),
        P(("dp", "expert"), None, "tensor"),
        P(None, ("dp", "expert"), "tensor"),
        P(None, "tensor", ("dp", "expert")),
        P(("dp", "expert")),
        P(("dp", "expert")),
        P("expert", "dp", "tensor"),
        P("expert", "dp", "tensor"),
        P("expert", "tensor", "dp"),
    )
    return jax.shard_map(
        per_device, mesh=mesh, in_specs=in_specs, out_specs=out_specs, check_vma=False
    )
```

time: 647 us -> 516 us (0.80)
  Pallas kernels: 135 us -> 412 us
  waiting for transfers between devices: 192 us -> 6.04 us
  matrix products: 84.7 us -> 28.3 us
  local copies, waits for them, and re-layouts: 73.5 us -> 22.2 us
  starting transfers between devices: 64.3 us -> 14.8 us
  other arithmetic: 44.3 us -> 9.18 us
  blocking collectives: 28.3 us -> 0 us
    pallas_call x2 -> x3, Pallas kernels: 135 us -> 412 us  [call_kernel(): pl.pallas_call(kernel, out_shape=[jax.ShapeDtypeStruct(shape, dtype) for...]
    all_to_all x13 -> x3, waiting for transfers between devices: 135 us -> 6 us  [swap(): return lax.all_to_all(blocks, axes, split_axis=0, concat_axis=0, tiled=True)]
    all_gather x6 -> x0, waiting for transfers between devices: 55.7 us -> none  [the longest x1 27.3 us: per_device(): d_both_all = lax.all_gather(tight(d_both), 'dp', axis=0, tiled=True)]
    dot_general x19 -> x7, matrix products: 77.4 us -> 27.3 us  [dot(): return jnp.einsum(spec, left, right, preferred_element_type=F32)]
    all_to_all x13 -> x3, starting transfers between devices: 64 us -> 14.7 us  [swap(): return lax.all_to_all(blocks, axes, split_axis=0, concat_axis=0, tiled=True)]
    all_to_all x2 -> x0, blocking collectives: 28.3 us -> none  [swap(): return lax.all_to_all(blocks, axes, split_axis=0, concat_axis=0, tiled=True)]
    concatenate x8 -> x1, other arithmetic: 11.6 us -> 1.05 us  [per_device(): pack_one = jnp.concatenate([kv_parts, both_gains, query_weight], 2)]
    optimization_barrier x1 -> x0, local copies, waits for them, and re-layouts: 9.53 us -> none  [per_device(): lax.optimization_barrier((first_full, expert_grad))]
  transfers between devices with their start and end apart: 21 -> 5, of which waited for: 13 -> 3; matrix products, arithmetic and copies ran while one was open for 23% -> 7% of each run, Pallas kernels for 10% -> 13%
where the time goes in v3:
time: 516 us; the launch traced here: 508 us
  Pallas kernels  412 us (80%)
  matrix products  28.3 us (5%)
  local copies, waits for them, and re-layouts  22.2 us (4%)
  starting transfers between devices  14.8 us (3%)
  between operations  14.8 us (3%)
  other arithmetic  9.18 us (2%)
  waiting for transfers between devices  6.04 us (1%)
    pallas_call x3, Pallas kernels, call_kernel(): pl.pallas_call(kernel, out_shape=[jax.ShapeDtypeStruct(shape, dtype) for...  412 us
    dot_general x7, matrix products, dot(): return jnp.einsum(spec, left, right, preferred_element_type=F32)  27.3 us
    all_to_all x3, starting transfers between devices, swap(): return lax.all_to_all(blocks, axes, split_axis=0, concat_axis=0, tiled=True)  14.7 us
  transfers between devices with their start and end apart: 5, of which 3 were waited for; matrix products, arithmetic and copies ran while one was open for 7% of the time, Pallas kernels for 13%

profile of v3, /device:TPU:1, one launch (start us, length us, event | category | flops | bytes accessed | tf_op | source)
XLA Modules:
  0.0 507.6 jit_solution(13482495796499989385)
XLA Ops:
  7.3 0.7 fusion.15
  9.3 1.0 convolution_reduce_fusion
  10.3 0.8 dot_general.76.gate_slot
  11.1 0.8 copy.74.pick_ffn
  14.2 0.8 copy.72.pick_att
  15.0 0.8 copy.73.att_gate
  16.2 0.8 copy.75.ffn_gate
  17.4 0.7 copy.93
  19.4 1.0 pad_maximum_fusion.pack_one
  21.1 245.5 %shard_map.240 = (bf16[4,512,896]{2,1,0:T(8,128)(2,1)}, bf16[4,512,512]{2,1,0:T(8,128)(2,1)}, bf16[2,8,128,1024]{3,2,1,0:T(8,128)(2,1)}, f32[2,2048]{1,0:T(2,128...) custom-call(bf16[128,2048]{1,0:T(8,128)(2,1)} %bitcast.132, ...), custom_call_target="tpu_custom_call" | custom-call | tf_op jit(solution)/shard_map/pallas_call | solution.py:962
  266.6 99.7 %shard_map.241 = (f32[128,2048]{1,0:T(8,128)}, f32[1,2048]{1,0:T(1,128)}, bf16[2,8,48,1024]{3,2,1,0:T(8,128)(2,1)}, bf16[1024,640]{1,0:T(8,128)(2,1)}, bf16[4,32...) custom-call(bf16[2,2,8,48,512]{4,3,2,1,0:T(8,128)(2,1)} %get-tuple-element.39.parts, ...), custom_call_target="tpu_custom_call" | custom-call | tf_op jit(solution)/shard_map/pallas_call | solution.py:962
  366.3 1.9 copy.80
  368.2 2.6 convolution_convert_fusion.1
  370.9 6.6 %copy.78 = bf16[2,1024,1024]{1,2,0:T(8,128)(2,1)} copy(bf16[2,1024,1024]{2,1,0:T(8,128)(2,1)} %bitcast.127) | data formatting | bytes 8388608 | tf_op jit(solution)/shard_map/reshape | solution.py:1198
  377.5 7.2 %convolution_convert_fusion = bf16[2048,640]{1,0:T(8,128)(2,1)} fusion(bf16[2048,1024]{1,0:T(8,128)(2,1)} %bitcast.128, bf16[1024,640]{1,0:T(8,128)(2,1)S(1)} %copy-done.4), kind=kOutput, calls=%fused_computation.7 | convolution fusion | flops 2685665280 | bytes 8126464 | tf_op jit(solution)/shard_map/std,th->sdh/dot_general | solution.py:18
  384.7 67.2 %shard_map.242 = (bf16[128,2048]{1,0:T(8,128)(2,1)}, f32[128,2048]{1,0:T(8,128)}, f32[1,2048]{1,0:T(1,128)}) custom-call(bf16[1024,640]{1,0:T(8,128)(2,1)} %get-tuple-element.53.d_proj, bf16[4,512,896]{2,1,0:T(8,128)(2,1)} %get-tuple-element.54.weights, bf16[128,512]{1,0:T(8,128)(2,1)} %get-tuple-element.55.output_part, bf16[128,2048]{1,0:T(8,128)(2,1)} %bitcast.133, ...), custom_call_target="tpu_custom_call" | custom-call | tf_op jit(solution)/shard_map/pallas_call | solution.py:962
  451.9 0.7 pad_maximum_fusion.1
  453.4 7.2 %all-to-all-start.2 = ((f32[32,1,128]{2,1,0:T(1,128)}), f32[32,1,128]{2,1,0:T(1,128)S(1)}, u32[]{:S(2)}, u32[]{:S(2)}) async-start(f32[32,1,128]{2,1,0:T(1,128)} %reshape.142), calls=%async_computation.4 | async-start | bytes 32768 | tf_op jit(solution)/shard_map/all_to_all | solution.py:22
  460.6 5.8 %fusion.3 = f32[1,512,1408]{2,1,0:T(8,128)} fusion(bf16[4,2,320,1408]{3,2,1,0:T(8,128)(2,1)} %bitcast.125, bf16[4,320,1024]{2,1,0:T(8,128)(2,1)S(1)} %copy-done.2), kind=kOutput, calls=%fused_computation.5 | convolution fusion | flops 1845493760 | bytes 7798784 | tf_op jit(solution)/shard_map/scd,scf->df/dot_general | solution.py:18
  466.4 1.2 all-to-all-done.2
  467.6 4.0 all-to-all-start.1
  471.6 5.8 %fusion.2 = f32[1,512,1408]{2,1,0:T(8,128)} fusion(bf16[4,2,320,1408]{3,2,1,0:T(8,128)(2,1)} %bitcast.126, bf16[4,320,1024]{2,1,0:T(8,128)(2,1)S(1)} %copy-done.2), kind=kOutput, calls=%fused_computation.4 | convolution fusion | flops 1845493760 | bytes 7798784 | tf_op jit(solution)/shard_map/scd,scf->df/dot_general | solution.py:18
  477.5 3.0 all-to-all-done.1
  480.5 0.8 copy-done.3
  481.3 3.5 all-to-all-start
  484.8 5.7 %convolution_bitcast_fusion = f32[1,1408,512]{2,1,0:T(8,128)} fusion(bf16[1280,1408]{1,0:T(8,128)(2,1)} %bitcast.164, bf16[1280,1024]{1,0:T(8,128)(2,1)S(1)} %bitcast.129), kind=kOutput, calls=%fused_computation.6 | convolution fusion | flops 1845493760 | bytes 7798784 | tf_op jit(solution)/shard_map/cf,cd->fd/dot_general | solution.py:18
  492.4 2.2 convert_bitcast_fusion
  494.6 1.8 all-to-all-done
  496.6 0.9 reshape.130
  497.5 1.1 slice.33
  498.6 0.8 copy.97
  499.4 1.0 copy.98
  (74 shorter events, 9.3 us)
Async XLA Ops:
  7.2 8.7 %copy-start = (bf16[64,2,512]{2,1,0:T(2,128)(2,1)S(1)}, bf16[64,2,512]{2,1,0:T(2,128)(2,1)}, u32[]{:S(2)}) copy-start(bf16[64,2,512]{2,1,0:T(2,128)(2,1)} %param.24) | copy-start | bytes 393220
  7.2 9.0 %copy-start.9 = (f32[1,128,2]{1,2,0:T(2,128)S(1)}, f32[1,128,2]{1,2,0:T(2,128)}, u32[]{:S(2)}) copy-start(f32[1,128,2]{1,2,0:T(2,128)} %param.23) | copy-start | bytes 3076
  7.2 7.8 %copy-start.10 = (f32[1,128,2]{1,2,0:T(2,128)S(1)}, f32[1,128,2]{1,2,0:T(2,128)}, u32[]{:S(2)}) copy-start(f32[1,128,2]{1,2,0:T(2,128)} %param.21) | copy-start | bytes 3076
  7.2 8.8 %copy-start.13 = (bf16[64]{0:T(256)(128)(2,1)S(1)}, bf16[64]{0:T(256)(128)(2,1)}, u32[]{:S(2)}) copy-start(bf16[64]{0:T(256)(128)(2,1)} %param.27) | copy-start | bytes 388
  7.2 8.8 %copy-start.12 = (bf16[64]{0:T(256)(128)(2,1)S(1)}, bf16[64]{0:T(256)(128)(2,1)}, u32[]{:S(2)}) copy-start(bf16[64]{0:T(256)(128)(2,1)} %param.28) | copy-start | bytes 388
  7.2 9.8 %copy-start.14 = (s32[1,8]{1,0:T(1,128)S(1)}, s32[1,8]{1,0:T(1,128)}, u32[]{:S(2)}) copy-start(s32[1,8]{1,0:T(1,128)} %param.19) | copy-start | bytes 100
  7.2 460.3 %reduce-scatter.5.cloned.1.call-start = ((), (), s32[]{:S(2)}) async-start(), calls=%async_computation.6 | async-start | bytes 2621440 | tf_op jit(solution)/shard_map/reduce_scatter | solution.py:1136
  8.2 11.2 %copy-start.6 = (bf16[8,64,512]{2,1,0:T(8,128)(2,1)S(1)}, bf16[8,64,512]{2,1,0:T(8,128)(2,1)}, u32[]{:S(2)}) copy-start(bf16[8,64,512]{2,1,0:T(8,128)(2,1)} %param.25) | copy-start | bytes 1572868
  366.3 1.9 copy-start.11
  370.8 109.7 %reduce-scatter.3.cloned.1.call-start = ((), (), s32[]{:S(2)}) async-start(), calls=%async_computation.5 | async-start | bytes 3276800 | tf_op jit(solution)/shard_map/reduce_scatter | solution.py:1136
  370.9 6.6 %copy-start.4 = (bf16[1024,640]{1,0:T(8,128)(2,1)S(1)}, bf16[1024,640]{1,0:T(8,128)(2,1)}, u32[]{:S(2)}) copy-start(bf16[1024,640]{1,0:T(8,128)(2,1)} %get-tuple-element.53.d_proj) | copy-start | bytes 3932164
  384.7 67.2 %copy-start.8 = (f32[1,2048]{1,0:T(1,128)S(1)}, f32[1,2048]{1,0:T(1,128)}, u32[]{:S(2)}) copy-start(f32[1,2048]{1,0:T(1,128)} %get-tuple-element.64) | copy-start | bytes 24580
  384.7 75.9 %copy-start.2 = (bf16[4,320,1024]{2,1,0:T(8,128)(2,1)S(1)}, bf16[4,320,1024]{2,1,0:T(8,128)(2,1)}, u32[]{:S(2)}) copy-start(bf16[4,320,1024]{2,1,0:T(8,128)(2,1)} %get-tuple-element.65) | copy-start | bytes 7864324
  453.4 14.2 %all-to-all-start.2 = ((f32[32,1,128]{2,1,0:T(1,128)}), f32[32,1,128]{2,1,0:T(1,128)S(1)}, u32[]{:S(2)}, u32[]{:S(2)}) async-start(f32[32,1,128]{2,1,0:T(1,128)} %reshape.142), calls=%async_computation.4 | async-start | bytes 32768 | tf_op jit(solution)/shard_map/all_to_all | solution.py:22
  467.6 12.9 %all-to-all-start.1 = ((bf16[8,64,512]{2,1,0:T(8,128)(2,1)}), bf16[8,64,512]{2,1,0:T(8,128)(2,1)S(1)}, u32[]{:S(2)}, u32[]{:S(2)}) async-start(bf16[8,64,512]{2,1,0:T(8,128)(2,1)} %bitcast.152), calls=%async_computation.3 | async-start | bytes 1048576 | tf_op jit(solution)/shard_map/all_to_all | solution.py:22
  480.5 0.8 copy-start.3
  481.3 15.1 %all-to-all-start = ((bf16[8,64,640]{2,1,0:T(8,128)(2,1)}), bf16[8,64,640]{2,1,0:T(8,128)(2,1)S(1)}, u32[]{:S(2)}, u32[]{:S(2)}) async-start(bf16[8,64,640]{2,1,0:T(8,128)(2,1)} %bitcast.149), calls=%async_computation.1 | async-start | bytes 1310720 | tf_op jit(solution)/shard_map/all_to_all | solution.py:22
  492.4 6.2 %copy-start.7 = (bf16[128,2048]{1,0:T(8,128)(2,1)S(1)}, bf16[128,2048]{1,0:T(8,128)(2,1)}, u32[]{:S(2)}) copy-start(bf16[128,2048]{1,0:T(8,128)(2,1)} %get-tuple-element.58) | copy-start | bytes 1572868
  494.6 4.8 copy-start.5
  496.6 3.8 copy-start.1
Sparse Core Ops, SparseCore 0:
  370.9 27.3 reduce-scatter.4
  401.4 33.6 reduce-scatter.2

commit v4 on v3

--- a/solution.py
+++ b/solution.py
@@ -62,7 +62,7 @@
     )
 
 
-def enter(own, half, core, owners, around=()):
+def enter(own, half, core, owners, around=(), greeted=0):
     semaphore = pltpu.get_barrier_semaphore()
     for index in around:
         pl.semaphore_signal(
@@ -86,7 +86,7 @@
     each(2 * owners, column)
     hello(own, 2 * half + 1 - core)
     hello(own, 2 * (1 - half) + 1 - core)
-    pl.semaphore_wait(semaphore, 2 * owners + 1 + len(around))
+    pl.semaphore_wait(semaphore, 2 * owners + 1 + len(around) + greeted)
 
 
 def send_home(merged, landing, sends, recvs, own, half, core, owners):
@@ -167,6 +167,7 @@
 def first_kernel(
     tokens,
     marks,
+    own_gains,
     pack_one,
     pack_two,
     gate_weight,
@@ -188,8 +189,7 @@
     gains,
     inv_one,
     queries,
-    keys,
-    values,
+    pairs,
     row_info,
     cos_slot,
     sin_slot,
@@ -206,6 +206,7 @@
     expert_in,
     expert_grad,
     routes,
+    gain_parts,
     slot_keys,
     inv_all,
     heads_out,
@@ -249,6 +250,8 @@
     grad_recv,
     feature_send,
     feature_recv,
+    gain_send,
+    gain_recv,
 ):
     own, share, dp = lax.axis_index("expert"), lax.axis_index("tensor"), lax.axis_index("dp")
     owners, shares, dps = heads_out.shape[0], slices.shape[0], first_full.shape[0]
@@ -269,8 +272,10 @@
     down_ring = Ring(down, ring_send, ring_recv, 0, dp, dps)
     one_ring = Ring(first_full, ring_send, ring_recv, 4, dp, dps)
     two_ring = Ring(out_full, ring_send, ring_recv, 8, dp, dps)
-    gate_ring = Ring(gate_up.at[0], ring_send, ring_recv, 12, dp, dps)
-    up_ring = Ring(gate_up.at[1], ring_send, ring_recv, 16, dp, dps)
+    up_ring = Ring(gate_up.at[1], ring_send, ring_recv, 12, dp, dps)
+    low, high = pl.ds(0, piece // 2), pl.ds(piece // 2, piece // 2)
+    low_ring = Ring(gate_up.at[0, :, low], ring_send, ring_recv, 16, dp, dps)
+    high_ring = Ring(gate_up.at[0, :, high], ring_send, ring_recv, 20, dp, dps)
     own_rows = pl.ds(pl.multiple_of(own * local_rows, local_rows), local_rows)
 
     def to_owner(src, dst, sends, recvs, step):
@@ -304,11 +309,26 @@
     def mark_copy(step):
         return to_owner(lambda to: marks, routes.at[own], mark_send, mark_recv, step)
 
-    down_ring.start(down_weight)
     each(owners, lambda step: pack_copy(step).start())
     each(owners, lambda step: mark_copy(step).start())
-    each(owners, lambda step: token_copy(step).start())
-    each(owners, lambda step: second_copy(step).start())
+
+    def gain_copy(step):
+        return to_owner(lambda to: own_gains, gain_parts.at[dp, own], gain_send, gain_recv, step)
+
+    def far_gain_copy(step):
+        to = lax.rem(dp + step, dps)
+        place = owners + step
+        return remote(
+            gain_parts.at[dp],
+            gain_parts.at[dp],
+            gain_send.at[place],
+            gain_recv.at[place],
+            {"dp": to},
+        )
+
+    gain_parts[dp, own] = own_gains[...]
+    each(owners, lambda step: gain_copy(step).start())
+    low_ring.start(gate_weight.at[low])
     own_copies = [
         pltpu.make_async_copy(pack_one.at[own], first_full.at[dp, own_rows], local.at[0]),
         pltpu.make_async_copy(pack_two.at[own], out_full.at[dp, own_rows], local.at[1]),
@@ -324,7 +344,12 @@
     own_copies[0].wait()
     each(owners, lambda step: pack_copy(step).wait())
     one_ring.start()
+    high_ring.start(gate_weight.at[high])
+    each(owners, lambda step: token_copy(step).start())
+    each(owners, lambda step: second_copy(step).start())
     each(owners, lambda step: mark_copy(step).wait())
+    each(owners, lambda step: gain_copy(step).wait())
+    each(dps, lambda step: far_gain_copy(step).start())
 
     def picked_rows(source, out, scale):
         for index in range(2):
@@ -386,8 +411,9 @@
     expert_grad[core, own] = grads_out[own]
     own_copies[1].wait()
     each(owners, lambda step: second_copy(step).wait())
+    one_ring.forward()
     two_ring.start()
-    gate_ring.start(gate_weight)
+    low_ring.forward()
     up_ring.start(up_weight)
     across.wait()
 
@@ -399,13 +425,15 @@
 
     lax.fori_loop(0, owners, squares, 0)
     inv_one[...] = inv_all[own]
-    one_ring.forward()
-    down_ring.forward()
     one_ring.finish()
 
-    for index in range(dps):
-        turned = jnp.transpose(first_full[index, :, 2 * HD : 3 * HD].astype(F32))
-        gains[:, index * piece : (index + 1) * piece] = turned[0:2, :]
+    each(dps, lambda step: far_gain_copy(step).wait())
+    left = lax.broadcasted_iota(jnp.int32, (8, HD), 1) < HD // 2
+    for index in range(dps * owners // 2):
+        name, side = index // columns, 2 * (index % columns)
+        turned = pltpu.roll(gain_parts[name, side + 1], HD // 2, 1)
+        joined = jnp.where(left, gain_parts[name, side], turned)
+        gains[:, index * HD : (index + 1) * HD] = joined[0:2, :]
 
     chosen = expert_in
     def norm_block(index, carry):
@@ -427,7 +455,7 @@
     for index in range(dps):
         cut = slice((index % 2) * piece, (index % 2 + 1) * piece)
         taken = chosen[index // 2, :, :, cut].reshape(rows, piece)
-        query = query + mm(taken, first_full[index, :, 3 * HD :])
+        query = query + mm(taken, first_full[index, :, HD:])
     for column in range(columns):
         head = query[:, column * HD : (column + 1) * HD]
         head = (head * cos_slot[...] + pltpu.roll(head, HD // 2, 1) * sin_slot[...]).astype(BF)
@@ -440,27 +468,29 @@
     each(owners, lambda step: head_copy(step).start())
     queries[own] = heads_out[own]
 
+    first = part == 0
+
     def key_block(index, carry):
-        both = jnp.zeros((group, 2 * HD), F32)
+        taken = jnp.zeros((group, HD), F32)
         for step in range(dps):
             cut = slice((step % 2) * piece, (step % 2 + 1) * piece)
-            both = both + mm(normed[step // 2, index, :, cut], first_full[step, :, : 2 * HD])
+            taken = taken + mm(normed[step // 2, index, :, cut], first_full[step, :, :HD])
         span = pl.ds(pl.multiple_of(index * group, group), group)
-        key = both[:, :HD]
-        key = key * cos_key[span, :] + pltpu.roll(key, HD // 2, 1) * sin_key[span, :]
-        keys[span, :] = key.astype(BF)
-        values[span, :] = both[:, HD:].astype(BF)
+        turned = taken * cos_key[span, :] + pltpu.roll(taken, HD // 2, 1) * sin_key[span, :]
+        pairs[part, span, :] = jnp.where(first, turned, taken).astype(BF)
         return carry
 
     lax.fori_loop(0, owners, key_block, 0)
-    two_ring.forward()
+    pair = {"expert": own + 1 - 2 * part, "tensor": share}
+    swapped = remote(pairs.at[part], pairs.at[part], one_send.at[10], one_recv.at[10], pair)
+    swapped.start()
 
     scale = HD ** (-0.5)
     key_pos = lax.broadcasted_iota(jnp.int32, (1, owners * group), 1).astype(F32)
 
     def attend(index):
         span = pl.ds(pl.multiple_of(index * head_rows, head_rows), head_rows)
-        scores = mm(queries[index], keys[...], 1, 1) * scale
+        scores = mm(queries[index], pairs[0], 1, 1) * scale
         visible = (key_pos <= row_info[span, 0:1]) & (key_pos >= row_info[span, 1:2])
         scores = jnp.where(visible, scores, -1e30)
         top = jnp.max(scores, 1, keepdims=True)
@@ -468,7 +498,7 @@
         total = jnp.sum(shifted, 1, keepdims=True)
         row_info[span, 2:3] = top + jnp.log(total)
         probs = (shifted / total).astype(BF)
-        mixed_out[index] = mm(probs, values[...]).astype(BF)
+        mixed_out[index] = mm(probs, pairs[1]).astype(BF)
 
     def back_copy(step):
         to = lax.rem(own + owners - step, owners)
@@ -485,10 +515,13 @@
         attend(lax.rem(own + owners - step, owners))
         back_copy(step).start()
 
+    swapped.wait()
     attend(own)
     mixed_in[own] = mixed_out[own]
     each(owners, attend_other)
-    gate_ring.forward()
+    two_ring.forward()
+    high_ring.forward()
+    down_ring.start(down_weight)
     two_ring.finish()
     each(owners, lambda step: back_copy(step).wait())
     for column in range(columns):
@@ -574,19 +607,18 @@
         cut = slice((index % 2) * piece, (index % 2 + 1) * piece)
         for side, source in enumerate((expert_in, expert_grad)):
             taken = source[index // 2, :, :, cut].reshape(rows, piece).astype(F32)
-            features[index, :, side * piece : (side + 1) * piece] = tight(taken).astype(BF)
+            features[side, index] = tight(taken).astype(BF)
     def feature_copy(step):
         to = lax.rem(dp + step, dps)
         return remote(
-            features.at[to],
-            features_all.at[dp],
+            features.at[core, to],
+            features_all.at[core, dp],
             feature_send.at[step],
             feature_recv.at[step],
             {"dp": to},
         )
 
-    each(dps, lambda step: feature_copy(step).start())
-    keep = pltpu.make_async_copy(features.at[dp], features_all.at[dp], feature_send.at[0])
+    keep = pltpu.make_async_copy(features.at[core, dp], features_all.at[core, dp], feature_send.at[0])
     keep.start()
     for copy in own_copies[2:]:
         copy.wait()
@@ -601,36 +633,39 @@
         if units % tile:
             body(pl.ds(units - units % tile, units % tile))
 
-    gate_ring.finish()
+    low_ring.finish()
+    high_ring.finish()
 
     def gate_tile(cut):
-        total = mm(features[0, :, :piece], gate_up[0, 0, :, cut])
+        total = mm(features[0, 0], gate_up[0, 0, :, cut])
         for index in range(1, dps):
-            total = total + mm(features[index, :, :piece], gate_up[0, index, :, cut])
+            total = total + mm(features[0, index], gate_up[0, index, :, cut])
         act[0, :, cut] = total
 
     unit_tiles(gate_tile)
+    down_ring.forward()
     up_ring.finish()
 
     def up_tile(cut):
-        up = mm(features[0, :, :piece], gate_up[1, 0, :, cut])
+        up = mm(features[0, 0], gate_up[1, 0, :, cut])
         for index in range(1, dps):
-            up = up + mm(features[index, :, :piece], gate_up[1, index, :, cut])
+            up = up + mm(features[0, index], gate_up[1, index, :, cut])
         act[1, :, cut] = up
         gate = act[0, :, cut]
         hidden[:, cut] = (gate / (1.0 + jnp.exp(-gate)) * up).astype(BF)
 
     unit_tiles(up_tile)
     down_ring.finish()
+    each(dps, lambda step: feature_copy(step).start())
     chip_sum(lambda index: loose(mm(hidden[...], down[index])), far, near, sibling, 7)
     outgoing_two = send_home(
         near, landing_two, home_two_send, home_two_recv, own, half, core, owners
     )
 
     def grad_tile(cut):
-        grad = mm(features[0, :, piece:], down[0, cut, :], 1, 1)
+        grad = mm(features[1, 0], down[0, cut, :], 1, 1)
         for index in range(1, dps):
-            grad = grad + mm(features[index, :, piece:], down[index, cut, :], 1, 1)
+            grad = grad + mm(features[1, index], down[index, cut, :], 1, 1)
         gate, up = act[0, :, cut], act[1, :, cut]
         sigma = 1.0 / (1.0 + jnp.exp(-gate))
         d_both[0, :, cut] = (grad * up * sigma * (1.0 + gate * (1.0 - sigma))).astype(BF)
@@ -640,20 +675,26 @@
     for index in range(dps):
         total = mm(d_both[0], gate_up[0, index], 1, 1) + mm(d_both[1], gate_up[1, index], 1, 1)
         d_parts[index % 2, index // 2] = loose(total)
+    keep.wait()
+    each(dps, lambda step: feature_copy(step).wait())
+    across = remote(
+        features_all.at[core], features_all.at[core], one_send.at[9], one_recv.at[9], other
+    )
+    across.start()
     wait_home(outgoing_two, owners)
     rest = at_tokens(pick_ffn, ffn_gate, landing_two)
     span = pl.ds(pl.multiple_of(share * piece, piece), piece)
     output_part[...] = (state[:, span] + rest).astype(BF)
-    keep.wait()
-    each(dps, lambda step: feature_copy(step).wait())
+    across.wait()
     one_ring.drain()
     two_ring.drain()
-    gate_ring.drain(gate_weight)
+    low_ring.drain(gate_weight.at[low])
+    high_ring.drain(gate_weight.at[high])
     up_ring.drain(up_weight)
     down_ring.drain(down_weight)
 
 
-def middle_kernel(
+def back_kernel(
     parts,
     sel_ffn,
     state,
@@ -664,26 +705,38 @@
     att_gate,
     out_full,
     queries,
-    keys,
-    values,
+    pairs,
     row_info,
     cos_slot,
     sin_slot,
     cos_key,
     sin_key,
     place,
+    d_both,
     hidden,
-    d_both,
-    d_state,
-    gain_grad,
+    output_part,
+    tokens,
+    inv_one,
+    mixed,
+    far_weights,
+    far_normed,
+    far_features,
+    output,
+    input_grad,
+    gain_grads,
+    query_grad,
+    out_grad,
+    kv_grad,
+    gate_grad,
+    up_grad,
+    down_grad,
+    d_both_all,
+    hidden_all,
+    d_gain_two,
     d_rows,
     d_proj,
-    hidden_all,
-    d_both_all,
-    sibling,
-    merged,
-    landing,
-    slices,
+    return_in,
+    parts_joined,
     rows_out,
     heads_out,
     heads_in,
@@ -693,12 +746,30 @@
     pair_in,
     d_keys,
     d_values,
-    one_send,
-    one_recv,
-    home_send,
-    home_recv,
-    slice_send,
-    slice_recv,
+    far,
+    near,
+    sibling,
+    landing,
+    slices,
+    map_grads,
+    early,
+    late,
+    maps_in,
+    gain_out,
+    gain_in,
+    weights,
+    normed,
+    features,
+    acts,
+    features_turned,
+    wide_tiles,
+    tall_tiles,
+    first_send,
+    first_recv,
+    return_send,
+    return_recv,
+    join_send,
+    join_recv,
     row_send,
     row_recv,
     head_send,
@@ -707,59 +778,97 @@
     back_recv,
     ring_send,
     ring_recv,
+    local,
+    one_send,
+    one_recv,
+    home_send,
+    home_recv,
+    slice_send,
+    slice_recv,
+    step_send,
+    step_recv,
+    map_send,
+    map_recv,
+    gain_send,
+    gain_recv,
+    tile_sem,
 ):
     own, share = lax.axis_index("expert"), lax.axis_index("tensor")
-    owners, shares = heads_out.shape[0], slices.shape[0]
+    owners, shares = heads_out.shape[0], parts_joined.shape[0]
     half, core = lax.div(share, 2), lax.rem(share, 2)
-    piece, width = slices.shape[2], state.shape[1]
-    slots = merged.shape[2]
+    piece, width = parts_joined.shape[2], state.shape[1]
+    slots = rows_out.shape[1]
     rows = owners * slots
     wide = width // 2
     head_rows = heads_out.shape[1]
     columns = owners // 2
     other = {"expert": own, "tensor": 2 * half + 1 - core}
-    dp, dps = lax.axis_index("dp"), hidden_all.shape[0]
-    enter(own, half, core, owners, (lax.rem(dp + 1, dps), lax.rem(dp + dps - 1, dps)))
+    dp, dps = lax.axis_index("dp"), d_both_all.shape[0]
+
+    def owner_at(step):
+        return lax.rem(dp + lax.div(step, owners), dps), lax.rem(own + lax.rem(step, owners), owners)
+
+    def hello(step):
+        to_dp, to = owner_at(step)
+        pl.semaphore_signal(
+            pltpu.get_barrier_semaphore(),
+            inc=1,
+            device_id={"dp": to_dp, "expert": to},
+            device_id_type=pl.DeviceIdType.MESH,
+        )
+
+    each(dps * owners, hello)
+    enter(own, half, core, owners, greeted=dps * owners - 1)
+    loads = [
+        pltpu.make_async_copy(far_weights, weights, local.at[4]),
+        pltpu.make_async_copy(far_normed, normed, local.at[5]),
+        pltpu.make_async_copy(far_features.at[1], features, local.at[6]),
+        pltpu.make_async_copy(far_features.at[0], acts.at[:, :, pl.ds(0, width // shares)], local.at[2]),
+    ]
+    for copy in loads:
+        copy.start()
 
     both_ring = Ring(d_both_all, ring_send, ring_recv, 0, dp, dps)
+    both_ring.start(d_both)
     hidden_ring = Ring(hidden_all, ring_send, ring_recv, 4, dp, dps)
-    both_ring.start(d_both)
     hidden_ring.start(hidden)
     keeps = [
-        pltpu.make_async_copy(d_both, d_both_all.at[dp], ring_send.at[8]),
-        pltpu.make_async_copy(hidden, hidden_all.at[dp], ring_send.at[9]),
+        pltpu.make_async_copy(d_both, d_both_all.at[dp], local.at[0]),
+        pltpu.make_async_copy(hidden, hidden_all.at[dp], local.at[7]),
     ]
-    for keep in keeps:
-        keep.start()
-
-    across = remote(parts.at[1 - core], sibling, one_send.at[0], one_recv.at[0], other)
+    for copy in keeps:
+        copy.start()
+
+    used_slots = pl.ds(0, slots)
+    return_near, return_out = sibling.at[:, :, used_slots], near.at[:, :, used_slots]
+    across = remote(parts.at[1 - core], return_near, first_send.at[0], first_recv.at[0], other)
     across.start()
     across.wait()
     for side in range(2):
-        merged[side] = (parts[core, side].astype(F32) + sibling[side].astype(F32)).astype(BF)
-    outgoing = send_home(merged, landing, home_send, home_recv, own, half, core, owners)
+        return_out[side] = (parts[core, side].astype(F32) + return_near[side].astype(F32)).astype(BF)
+    outgoing = send_home(return_out, return_in, return_send, return_recv, own, half, core, owners)
     wait_home(outgoing, owners)
-    total = mm(sel_ffn[...], landing[0].reshape(rows, piece))
-    total = total + mm(sel_ffn[...], landing[1].reshape(rows, piece))
-    slices[share] = total.astype(BF)
-    share_slices(slices, slice_send, slice_recv, own, share, shares)
+    total = mm(sel_ffn[...], return_in[0].reshape(rows, piece))
+    total = total + mm(sel_ffn[...], return_in[1].reshape(rows, piece))
+    parts_joined[share] = total.astype(BF)
+    share_slices(parts_joined, join_send, join_recv, own, share, shares)
 
     inv = inv_two[...]
     mean = jnp.zeros_like(inv)
     for index in range(shares):
         cut = slice(index * piece, (index + 1) * piece)
-        grad, value = slices[index].astype(F32), state[:, cut]
+        grad, value = parts_joined[index].astype(F32), state[:, cut]
         mean = mean + jnp.sum(value * gains[1:2, cut] * grad, 1, keepdims=True)
-        gain_grad[:, cut] = jnp.sum(grad * value * inv, 0, keepdims=True)
+        d_gain_two[:, cut] = jnp.sum(grad * value * inv, 0, keepdims=True)
     mean = mean * (inv * inv * inv / width)
     for index in range(shares):
         cut = slice(index * piece, (index + 1) * piece)
-        grad = gains[1:2, cut] * slices[index].astype(F32)
-        d_state[:, cut] = upstream[:, cut].astype(F32) + inv * grad - state[:, cut] * mean
+        grad = gains[1:2, cut] * parts_joined[index].astype(F32)
+        input_grad[:, cut] = upstream[:, cut].astype(F32) + inv * grad - state[:, cut] * mean
 
     for index in range(2):
         start = pl.multiple_of(core * wide + index * piece, piece)
-        grad = d_state[:, pl.ds(start, piece)]
+        grad = input_grad[:, pl.ds(start, piece)]
         both = jnp.concatenate(
             [(att_gate[0] * grad).astype(BF), (att_gate[1] * grad).astype(BF)], 0
         )
@@ -779,7 +888,7 @@
     each(owners, lambda step: row_copy(step).start())
     d_rows[core, own] = rows_out[own]
     each(owners, lambda step: row_copy(step).wait())
-    across = remote(d_rows.at[core], d_rows.at[core], one_send.at[1], one_recv.at[1], other)
+    across = remote(d_rows.at[core], d_rows.at[core], first_send.at[1], first_recv.at[1], other)
     across.start()
 
     def half_product(side):
@@ -809,13 +918,13 @@
     heads_in[own] = heads_out[own]
 
     scale = HD ** (-0.5)
-    key_pos = lax.broadcasted_iota(jnp.int32, (1, keys.shape[0]), 1).astype(F32)
+    key_pos = lax.broadcasted_iota(jnp.int32, (1, pairs.shape[1]), 1).astype(F32)
     d_keys[...] = jnp.zeros_like(d_keys)
     d_values[...] = jnp.zeros_like(d_values)
 
     def attend(index):
         span = pl.ds(pl.multiple_of(index * head_rows, head_rows), head_rows)
-        query, key, value, grad = queries[index], keys[...], values[...], heads_in[index]
+        query, key, value, grad = queries[index], pairs[0], pairs[1], heads_in[index]
         scores = mm(query, key, 1, 1) * scale
         visible = (key_pos <= row_info[span, 0:1]) & (key_pos >= row_info[span, 1:2])
         probs = jnp.where(visible, jnp.exp(scores - row_info[span, 2:3]), 0.0)
@@ -841,15 +950,15 @@
         attend(lax.rem(own + owners - step, owners))
         query_copy(step).start()
 
-    both_ring.forward()
     attend(own)
     queries_in[own] = queries_out[own]
     each(owners, attend_other)
+    both_ring.forward()
 
     first = lax.rem(own, 2) == 0
     pair_out[...] = jnp.where(first, d_values[...], d_keys[...] * scale).astype(BF)
     pair = {"expert": own + 1 - 2 * lax.rem(own, 2), "tensor": share}
-    across = remote(pair_out, pair_in, one_send.at[2], one_recv.at[2], pair)
+    across = remote(pair_out, pair_in, first_send.at[2], first_recv.at[2], pair)
     across.start()
     each(owners, lambda step: query_copy(step).wait())
     group = place.shape[2]
@@ -867,56 +976,57 @@
             d_proj[block * group : (block + 1) * group, : columns * HD] = mm(
                 place[block], picked, 0, 0
             ).astype(BF)
-    hidden_ring.forward()
     across.wait()
     mine = jnp.where(first, d_keys[...] * scale, d_values[...]) + pair_in[...].astype(F32)
     turned = mine * cos_key[...] + pltpu.roll(mine, HD // 2, 1) * sin_key[...]
     d_proj[:, columns * HD :] = jnp.where(first, turned, mine).astype(BF)
-    both_ring.finish()
-    hidden_ring.finish()
-    both_ring.drain(d_both)
-    hidden_ring.drain(hidden)
-    for keep in keeps:
-        keep.wait()
-
-
-def last_kernel(
-    d_proj,
-    weights,
-    output_part,
-    tokens,
-    inv_one,
-    gains,
-    d_state,
-    output,
-    input_grad,
-    gain_grad,
-    far,
-    near,
-    sibling,
-    landing,
-    slices,
-    one_send,
-    one_recv,
-    home_send,
-    home_recv,
-    slice_send,
-    slice_recv,
-):
-    own, share = lax.axis_index("expert"), lax.axis_index("tensor")
-    owners, shares = near.shape[1], slices.shape[0]
-    half, core = lax.div(share, 2), lax.rem(share, 2)
+
     group, piece = near.shape[2], near.shape[3]
-    width = shares * piece
     head_width = d_proj.shape[1] - HD
-    other = {"expert": own, "tensor": 2 * half + 1 - core}
-    enter(own, half, core, owners)
-    part = lax.rem(own, 2)
+    local_rows = maps_in.shape[1]
+    used, units = acts.shape[1], acts.shape[2]
+    after, before = lax.rem(dp + 1, dps), lax.rem(dp + dps - 1, dps)
+    facing = lax.rem(dp + 2, dps)
+    for copy in loads:
+        copy.wait()
+    for index in range(dps):
+        features_turned[index] = jnp.transpose(acts[index, :, :piece].astype(F32)).astype(BF)
+
+    def load(side):
+        source = hidden_all if side == 2 else d_both_all.at[:, pl.ds(side * used, used)]
+        return pltpu.make_async_copy(source, acts, local.at[1])
+
+    def map_grad(index):
+        cut = pl.ds(pl.multiple_of(lax.rem(index, 2) * piece, piece), piece)
+        inputs = normed[lax.div(index, 2), :, :, cut].reshape(owners * group, piece)
+        outs = d_rows[lax.div(index, 2), :, :, cut].reshape(-1, piece)
+        return mm(inputs, d_proj[...], 0, 0), mm(outs, mixed[...], 0, 0)
+
+    middle = head_width + HD
+
+    def keep_grad(index):
+        ins, outs = map_grad(index)
+        map_grads[index, :, :middle] = ins.astype(BF)
+        map_grads[index, :, middle:] = outs.astype(BF)
+
+    cut = piece // 2
+
+    def step_copy(kind):
+        to = {"dp": after if kind % 2 == 0 else before}
+        sems = (step_send.at[kind], step_recv.at[kind])
+        if kind < 2:
+            span = pl.ds(kind * cut, cut)
+            return remote(map_grads.at[facing, span], early.at[kind], *sems, to)
+        return remote(map_grads.at[after if kind == 2 else before], late.at[kind - 2], *sems, to)
+
+    keep_grad(facing)
+    step_copy(0).start()
+    step_copy(1).start()
 
     def product(index):
-        queries = mm(d_proj[:, :head_width], weights[index, :, 3 * HD :], 1, 1)
-        side = weights[index, :, pl.ds(pl.multiple_of(part * HD, HD), HD)]
-        return (queries + mm(d_proj[:, head_width:], side, 1, 1)).reshape(owners, group, piece)
+        queries = mm(d_proj[:, :head_width], weights[index, :, HD:], 1, 1)
+        side = mm(d_proj[:, head_width:], weights[index, :, :HD], 1, 1)
+        return (queries + side).reshape(owners, group, piece)
 
     def across(side):
         return remote(far.at[side], sibling.at[side], one_send.at[side], one_recv.at[side], other)
@@ -930,6 +1040,107 @@
         across(side).wait()
         near[side] = (near[side].astype(F32) + sibling[side].astype(F32)).astype(BF)
     outgoing = send_home(near, landing, home_send, home_recv, own, half, core, owners)
+
+    keep_grad(after)
+    keep_grad(before)
+    step_copy(0).wait()
+    step_copy(1).wait()
+    top, bottom = slice(0, cut), slice(cut, 2 * cut)
+    map_grads[after, top] = (map_grads[after, top].astype(F32) + early[0].astype(F32)).astype(BF)
+    map_grads[before, bottom] = (
+        map_grads[before, bottom].astype(F32) + early[1].astype(F32)
+    ).astype(BF)
+    step_copy(2).start()
+    step_copy(3).start()
+    both_ring.finish()
+    keeps[0].wait()
+    load(0).start()
+    hidden_ring.forward()
+
+    tile = 2 * HD
+    whole, rest = units // tile, units % tile
+    def unit_tiles(product, out, rows_first):
+        def store(slot, span, size):
+            if rows_first:
+                return pltpu.make_async_copy(
+                    tall_tiles.at[slot, pl.ds(0, size)], out.at[span], tile_sem.at[slot]
+                )
+            return pltpu.make_async_copy(
+                wide_tiles.at[slot, :, pl.ds(0, size)], out.at[:, span], tile_sem.at[slot]
+            )
+
+        def put(slot, value, size):
+            if rows_first:
+                tall_tiles[slot, :size] = value
+            else:
+                wide_tiles[slot, :, :size] = value
+
+        def pair(index, carry):
+            for slot in range(2):
+                span = pl.ds(pl.multiple_of((2 * index + slot) * tile, tile), tile)
+
+                @pl.when(index > 0)
+                def _(slot=slot, span=span):
+                    store(slot, span, tile).wait()
+
+                put(slot, product(span), tile)
+                store(slot, span, tile).start()
+            return carry
+
+        lax.fori_loop(0, whole // 2, pair, 0)
+        spans = [(0, pl.ds((whole - 2) * tile, tile), tile), (1, pl.ds((whole - 1) * tile, tile), tile)]
+        for slot, span, size in spans:
+            store(slot, span, size).wait()
+        if whole % 2:
+            span = pl.ds((whole - 1) * tile, tile)
+            put(0, product(span), tile)
+            store(0, span, tile).start()
+        if rest:
+            tail = pl.ds(whole * tile, rest)
+            put(1, product(tail), rest)
+            store(1, tail, rest).start()
+            store(1, tail, rest).wait()
+        if whole % 2:
+            store(0, span, tile).wait()
+
+    def wide_product(span):
+        total = mm(features_turned[0], acts[0, :, span])
+        for index in range(1, dps):
+            total = total + mm(features_turned[index], acts[index, :, span])
+        return total
+
+    def tall_product(span):
+        total = mm(acts[0, :, span], features[0], 0, 0)
+        for index in range(1, dps):
+            total = total + mm(acts[index, :, span], features[index], 0, 0)
+        return total
+
+    load(0).wait()
+    unit_tiles(wide_product, gate_grad, False)
+    load(1).start()
+    keep_grad(dp)
+
+    step_copy(2).wait()
+    step_copy(3).wait()
+    map_grads[dp] = (
+        map_grads[dp].astype(F32) + late[0].astype(F32) + late[1].astype(F32)
+    ).astype(BF)
+
+    def home_rows(index):
+        return pl.ds(pl.multiple_of(index * local_rows, local_rows), local_rows)
+
+    def map_copy(step):
+        to = lax.rem(own + step, owners)
+        return remote(
+            map_grads.at[dp, home_rows(to)],
+            maps_in.at[own],
+            map_send.at[step],
+            map_recv.at[step],
+            {"expert": to, "tensor": share},
+        )
+
+    each(owners, lambda step: map_copy(step).start())
+    maps_in[own] = map_grads[dp, home_rows(own), :]
     wait_home(outgoing, owners)
     total = jnp.zeros((group, piece), F32)
     for side in range(2):
@@ -941,17 +1152,58 @@
     inv = inv_one[...]
     mean = jnp.zeros_like(inv)
     for index in range(shares):
-        cut = slice(index * piece, (index + 1) * piece)
-        grad, value = slices[index, 0].astype(F32), tokens[:, cut].astype(F32)
-        output[:, cut] = slices[index, 1]
-        mean = mean + jnp.sum(value * gains[0:1, cut] * grad, 1, keepdims=True)
-        gain_grad[:, cut] = jnp.sum(grad * value * inv, 0, keepdims=True)
+        span = slice(index * piece, (index + 1) * piece)
+        grad, value = slices[index, 0].astype(F32), tokens[:, span].astype(F32)
+        output[:, span] = slices[index, 1]
+        mean = mean + jnp.sum(value * gains[0:1, span] * grad, 1, keepdims=True)
+        gain_one = jnp.sum(grad * value * inv, 0, keepdims=True)
+        for chunk in range(piece // HD):
+            lanes = slice(chunk * HD, (chunk + 1) * HD)
+            place = index * (piece // HD) + chunk
+            gain_out[place, 0:1] = gain_one[:, lanes]
+            gain_out[place, 1:2] = d_gain_two[:, place * HD : (place + 1) * HD]
+
+    def gain_copy(step):
+        to_dp, to = owner_at(step)
+        return remote(
+            gain_out.at[lax.div(to_dp * owners + to, HD // local_rows)],
+            gain_in.at[dp * owners + own],
+            gain_send.at[step],
+            gain_recv.at[step],
+            {"dp": to_dp, "expert": to},
+        )
+
+    each(dps * owners, lambda step: gain_copy(step).start())
+    gain_in[dp * owners + own] = gain_out[lax.div(dp * owners + own, HD // local_rows)]
     mean = mean * (inv * inv * inv / width)
     for index in range(shares):
-        cut = slice(index * piece, (index + 1) * piece)
-        grad = gains[0:1, cut] * slices[index, 0].astype(F32)
-        value = tokens[:, cut].astype(F32)
-        input_grad[:, cut] = d_state[:, cut] + inv * grad - value * mean
+        span = slice(index * piece, (index + 1) * piece)
+        grad = gains[0:1, span] * slices[index, 0].astype(F32)
+        value = tokens[:, span].astype(F32)
+        input_grad[:, span] = input_grad[:, span] + inv * grad - value * mean
+
+    load(1).wait()
+    unit_tiles(wide_product, up_grad, False)
+    hidden_ring.finish()
+    keeps[1].wait()
+    load(2).start()
+    each(owners, lambda step: map_copy(step).wait())
+    for index in range(owners):
+        query_grad[index] = maps_in[index, :, :head_width].astype(F32)
+        out_grad[index] = maps_in[index, :, middle:].astype(F32)
+        column = index // 2
+        kv_grad[index % 2, :, column * HD : (column + 1) * HD] = maps_in[
+            index, :, head_width:middle
+        ].astype(F32)
+    load(2).wait()
+    unit_tiles(tall_product, down_grad, True)
+    each(dps * owners, lambda step: gain_copy(step).wait())
+    total = gain_in[0, 0:2]
+    for index in range(1, dps * owners):
+        total = total + gain_in[index, 0:2]
+    gain_grads[...] = total
+    both_ring.drain(d_both)
+    hidden_ring.drain(hidden)
 
 
 def call_kernel(kernel, collective_id, outs, scratch, semaphores, args, far_args=(), far_outs=()):
@@ -1015,11 +1267,10 @@
     ffn_gate = ffn_gates[0]
     gate_slot = jnp.einsum("jtms,tj->ms", pick_ffn, ffn_gate, precision=lax.Precision.HIGHEST)
 
-    kv_parts = jnp.transpose(kv_weight.reshape(local, 2, columns, HD), (2, 0, 1, 3))
-    kv_parts = jnp.repeat(kv_parts.reshape(columns, local, 2 * HD), 2, axis=0)
-    both_gains = jnp.pad(jnp.stack([attn_gain, ffn_gain], 1), ((0, 0), (0, HD - 2)))
-    both_gains = jnp.broadcast_to(both_gains[None], (owners, local, HD))
-    pack_one = jnp.concatenate([kv_parts, both_gains, query_weight], 2)
+    kv_parts = jnp.transpose(kv_weight.reshape(local, 2, columns, HD), (2, 1, 0, 3))
+    pack_one = jnp.concatenate([kv_parts.reshape(owners, local, HD), query_weight], 2)
+    own_gains = jnp.stack([attn_gain, ffn_gain]).astype(F32)
+    own_gains = jnp.pad(own_gains, ((0, 8 - 2), (0, HD - local)))
     pack_two = jnp.swapaxes(out_weight, 1, 2)
     marks = jnp.pad(att_routes[0].T.astype(F32), ((0, 8 - TOPK), (0, 0)), constant_values=-1.0)
     place_att = slot_places(att_routes[0], ATT_EXP, att_cap)
@@ -1031,6 +1282,7 @@
     cos_key = jnp.asarray(np.concatenate([np.cos(angles)] * 2, 1), F32)
     sin_key = jnp.asarray(np.concatenate([-np.sin(angles), np.sin(angles)], 1), F32)
     used = min(group, group * TOPK * 5 // (4 * owners))
+    sel_ffn = jnp.transpose(place_ffn, (2, 0, 1)).reshape(group, -1)
     units = gate_weight.shape[2]
     slots = att_cap
     head_rows = columns * slots
@@ -1042,8 +1294,7 @@
         gains,
         inv_one,
         queries,
-        keys,
-        values,
+        pairs,
         row_info,
         cos_slot,
         sin_slot,
@@ -1060,14 +1311,13 @@
         first_kernel,
         3,
         [
-            ((dps, owners * local, 3 * HD + head_width), BF),
+            ((dps, owners * local, HD + head_width), BF),
             ((dps, owners * local, head_width), BF),
             ((2, owners, group, width // 2), BF),
             ((2, width), F32),
             ((group, 1), F32),
             ((owners, head_rows, HD), BF),
-            ((seq_len, HD), BF),
-            ((seq_len, HD), BF),
+            ((2, seq_len, HD), BF),
             ((owners * head_rows, HD), F32),
             ((rows, HD), F32),
             ((rows, HD), F32),
@@ -1075,17 +1325,18 @@
             ((rows, head_width), BF),
             ((group, width), F32),
             ((group, 1), F32),
-            ((dps, owners * used, 2 * piece), BF),
+            ((2, dps, owners * used, piece), BF),
             ((owners * used, units), BF),
             ((2, owners * used, units), BF),
             ((2,) + block, BF),
             ((group, piece), BF),
         ],
         [
-            ((dps, owners * used, 2 * piece), BF),
+            ((2, dps, owners * used, piece), BF),
             ((2, owners, slots, width // 2), BF),
             ((2, owners, slots, width // 2), BF),
             ((owners, 8, group), F32),
+            ((dps, owners, 8, HD), F32),
             ((owners, owners, group), F32),
             ((owners, group, 1), F32),
             ((owners, head_rows, HD), BF),
@@ -1101,24 +1352,26 @@
             ((dps, units, piece), BF),
             ((2, owners * used, units), F32),
         ],
-        [20, 20, 5, 2 * owners, 2 * owners]
+        [24, 24, 5, 2 * owners, 2 * owners]
         + [owners] * 4
-        + [9, 9]
+        + [11, 11]
         + [owners] * 4
         + [2 * owners] * 4
         + [shares, shares]
         + [owners] * 4
-        + [dps, dps],
+        + [dps, dps]
+        + [owners + dps] * 2,
         [
             tokens[0],
             marks,
+            own_gains,
             pack_one,
             pack_two,
             gate_weight[0],
             up_weight[0],
             down_weight[0],
             cotangent[0],
-            jnp.transpose(place_ffn, (2, 0, 1)).reshape(group, -1),
+            sel_ffn,
             gate_slot.reshape(-1, 1),
             pick_att.reshape(TOPK, group, rows),
             att_gate.T[:, :, None],
@@ -1128,43 +1381,105 @@
             cos_key,
             sin_key,
         ],
-        far_args=(2, 3, 4, 5, 6),
-        far_outs=(15,),
+        far_args=(3, 4, 5, 6, 7),
+        far_outs=(14,),
     )
 
-    def scatter(grad):
-        return lax.psum_scatter(grad.astype(BF), "dp", scatter_dimension=0, tiled=True)
-
-    d_state, d_gain_two, d_rows, d_proj, hidden_all, d_both_all = call_kernel(
-        middle_kernel,
+    grad_width = head_width + HD + head_width
+    (
+        output,
+        input_grad,
+        gain_grads,
+        query_grad,
+        out_grad,
+        kv_grad,
+        gate_grad,
+        up_grad,
+        down_grad,
+        *_,
+    ) = call_kernel(
+        back_kernel,
         1,
         [
+            ((group, width), BF),
             ((group, width), F32),
+            ((2, HD), F32),
+            ((owners, local, head_width), F32),
+            ((owners, local, head_width), F32),
+            ((2, local, head_width), F32),
+            ((piece, units), F32),
+            ((piece, units), F32),
+            ((units, piece), F32),
+            ((dps, 2 * owners * used, units), BF),
+            ((dps, owners * used, units), BF),
+        ],
+        [
             ((1, width), F32),
             ((2, owners, slots, width // 2), BF),
             ((seq_len, head_width + HD), BF),
-            ((dps, owners * used, units), BF),
-            ((dps, 2 * owners * used, units), BF),
-        ],
-        [
-            (block, BF),
-            (block, BF),
             (block, BF),
             ((shares, group, piece), BF),
             ((owners, slots, width // 2), BF),
-            ((owners, columns * slots, HD), BF),
-            ((owners, columns * slots, HD), BF),
-            ((owners, columns * slots, HD), BF),
-            ((owners, columns * slots, HD), BF),
+            ((owners, head_rows, HD), BF),
+            ((owners, head_rows, HD), BF),
+            ((owners, head_rows, HD), BF),
+            ((owners, head_rows, HD), BF),
             ((seq_len, HD), BF),
             ((seq_len, HD), BF),
             ((seq_len, HD), F32),
             ((seq_len, HD), F32),
+            ((2, owners, group, piece), BF),
+            ((2, owners, group, piece), BF),
+            ((2, owners, group, piece), BF),
+            ((2, owners, group, piece), BF),
+            ((shares, 2, group, piece), BF),
+            ((dps, piece, grad_width), BF),
+            ((2, piece // 2, grad_width), BF),
+            ((2, piece, grad_width), BF),
+            ((owners, local, grad_width), BF),
+            ((width // HD, 8, HD), F32),
+            ((dps * owners, 8, HD), F32),
+            ((dps, owners * local, HD + head_width), BF),
+            ((2, owners, group, width // 2), BF),
+            ((dps, owners * used, piece), BF),
+            ((dps, owners * used, units), BF),
+            ((dps, piece, owners * used), BF),
+            ((2, piece, 2 * HD), F32),
+            ((2, 2 * HD, piece), F32),
         ],
-        [3, 3, 2 * owners, 2 * owners, shares, shares] + [owners] * 6 + [10, 8],
+        [
+            3,
+            3,
+            2 * owners,
+            2 * owners,
+            shares,
+            shares,
+            owners,
+            owners,
+            owners,
+            owners,
+            owners,
+            owners,
+            8,
+            8,
+            8,
+            2,
+            2,
+            2 * owners,
+            2 * owners,
+            shares,
+            shares,
+            4,
+            4,
+            owners,
+            owners,
+            dps * owners,
+            dps * owners,
+            2,
+        ],
         [
             d_parts,
-            jnp.transpose(place_ffn, (2, 0, 1)).reshape(group, -1),
+            sel_ffn,
             state,
             inv_two,
             cotangent[0],
@@ -1173,48 +1488,31 @@
             att_gate.T[:, :, None],
             out_full,
             queries,
-            keys,
-            values,
+            pairs,
             row_info,
             cos_slot,
             sin_slot,
             cos_key,
             -sin_key,
             place,
+            d_both.reshape(2 * owners * used, units),
             hidden,
-            d_both.reshape(2 * owners * used, units),
+            output_part,
+            tokens[0],
+            inv_one,
+            mixed,
+            first_full,
+            normed,
+            features_all,
         ],
-        far_args=(18, 19),
-        far_outs=(4, 5),
+        far_args=(17, 18, 23, 24, 25),
+        far_outs=(6, 7, 8, 9, 10),
     )
-    output, input_grad, d_gain_one = call_kernel(
-        last_kernel,
-        2,
-        [((group, width), BF), ((group, width), F32), ((1, width), F32)],
-        [((2, owners, group, piece), BF)] * 4 + [((shares, 2, group, piece), BF)],
-        [2, 2, 2 * owners, 2 * owners, shares, shares],
-        [d_proj, first_full, output_part, tokens[0], inv_one, gains, d_state],
-    )
-    normed = normed.reshape(2, seq_len, width // 2)
-    out_grad = scatter(dot("kcd,ch->kdh", d_rows.reshape(2, rows, -1), mixed).reshape(width, -1))
-    out_grad = swap(out_grad.reshape(owners, local, head_width), "expert")
-    out_grad = jnp.swapaxes(out_grad, 1, 2).astype(F32)
-
-    slices = features_all.reshape(-1, 2 * piece)
-    d_both_all = d_both_all.reshape(dps, 2, -1, units)
-    down_grad = dot("cf,cd->fd", hidden_all.reshape(-1, units), slices[:, piece:])[None]
-    inputs_all = features_all[:, :, :piece]
-    gate_grad = dot("scd,scf->df", inputs_all, d_both_all[:, 0])[None]
-    up_grad = dot("scd,scf->df", inputs_all, d_both_all[:, 1])[None]
-    map_grad = scatter(dot("std,th->sdh", normed, d_proj).reshape(width, -1))
-    map_grad = map_grad.reshape(owners, local, -1)
-    map_grad = swap(map_grad, "expert").astype(F32)
-    query_grad = map_grad[:, :, :head_width]
-    kv_grad = jnp.transpose(
-        map_grad[:, :, head_width:].reshape(columns, 2, local, HD), (2, 1, 0, 3)
-    ).reshape(local, 2, head_width)
-    gain_grads = jnp.stack([d_gain_one[0], d_gain_two[0]]).reshape(2, dps * owners, local)
-    gain_grads = jnp.sum(swap(jnp.swapaxes(gain_grads, 0, 1), ("dp", "expert")), 0)
+    chunk = HD // local
+    place = lax.rem(own, chunk) * local
+    gain_grads = lax.dynamic_slice_in_dim(gain_grads, place, local, 1)
+    kv_grad = jnp.swapaxes(kv_grad, 0, 1)
+    out_grad = jnp.swapaxes(out_grad, 1, 2)
     return (
         output[None],
         input_grad[None],
@@ -1223,9 +1521,9 @@
         out_grad,
         gain_grads[0],
         gain_grads[1],
-        gate_grad,
-        up_grad,
-        down_grad,
+        gate_grad[None],
+        up_grad[None],
+        down_grad[None],
     )
 
 

time: 516 us -> 428 us (0.83); the launches traced: 508 us -> 427 us
  matrix products: 28.3 us -> 1.24 us
  Pallas kernels: 412 us -> 396 us
  starting transfers between devices: 14.8 us -> 0 us
  between operations: 14.8 us -> 0.81 us
  waiting for transfers between devices: 6.04 us -> 0 us
    dot_general x7 -> x2, matrix products: 27.3 us -> 0.26 us  [dot(): return jnp.einsum(spec, left, right, preferred_element_type=F32)]
    pallas_call x3 -> x2, Pallas kernels: 412 us -> 396 us  [call_kernel(): pl.pallas_call(kernel, out_shape=[jax.ShapeDtypeStruct(shape, dtype) for...]
    all_to_all x3 -> x0, starting transfers between devices: 14.7 us -> none  [swap(): return lax.all_to_all(blocks, axes, split_axis=0, concat_axis=0, tiled=True)]
    unnamed x36 -> x35, local copies, waits for them, and re-layouts: 4.23 us -> 16.8 us
    reshape x6 -> x2, local copies, waits for them, and re-layouts: 9.63 us -> 0.11 us  [per_device(): kv_weight.reshape(local, 2, columns, HD)]
    all_to_all x3 -> x0, waiting for transfers between devices: 6 us -> none  [swap(): return lax.all_to_all(blocks, axes, split_axis=0, concat_axis=0, tiled=True)]
  transfers between devices with their start and end apart: 5 -> 0, of which waited for: 3 -> 0; matrix products, arithmetic and copies ran while one was open for 7% -> 0% of each run, Pallas kernels for 13% -> 0%
where the time goes in v4:
time: 428 us; the launch traced here: 427 us
  Pallas kernels  396 us (93%)
  local copies, waits for them, and re-layouts  24.1 us (6%)
  other arithmetic  5.35 us (1%)
    pallas_call x2, Pallas kernels, call_kernel(): pl.pallas_call(kernel, out_shape=[jax.ShapeDtypeStruct(shape, dtype) for...  396 us
    unnamed x35, local copies, waits for them, and re-layouts  16.8 us

profile of v4, /device:TPU:1, one launch (start us, length us, event | category | flops | bytes accessed | tf_op | source)
XLA Modules:
  0.0 427.5 jit_solution(709805907710613564)
XLA Ops:
  0.7 0.8 fusion.8
  2.0 0.7 and_convert_fusion.sel_ffn
  2.8 0.7 fusion.13
  3.5 1.0 convolution_reduce_fusion
  4.5 0.8 dot_general.44.gate_slot
  5.3 0.8 copy.49.pick_ffn
  6.1 0.7 fusion.11
  7.0 0.7 fusion.12
  7.7 0.8 copy.47.pick_att
  8.5 0.8 copy.48.att_gate
  9.4 0.9 pad_maximum_fusion.pack_one
  10.4 0.8 copy.50.ffn_gate
  11.4 0.7 broadcast_in_dim.18.ends
  12.0 0.6 pad.10.marks
  12.6 0.6 fusion.20.own_gains
  13.2 218.9 %shard_map.240 = (bf16[4,512,640]{2,1,0:T(8,128)(2,1)}, bf16[4,512,512]{2,1,0:T(8,128)(2,1)}, bf16[2,8,128,1024]{3,2,1,0:T(8,128)(2,1)}, f32[2,2048]{1,0:T(2,128...) custom-call(bf16[128,2048]{1,0:T(8,128)(2,1)} %bitcast.80, ...), custom_call_target="tpu_custom_call" | custom-call | tf_op jit(solution)/shard_map/pallas_call | solution.py:1214
  232.2 0.2 copy.51
  232.4 0.7 copy.57
  233.1 177.1 %shard_map.241 = (bf16[128,2048]{1,0:T(8,128)(2,1)}, f32[128,2048]{1,0:T(8,128)}, f32[2,128]{1,0:T(2,128)}, f32[8,64,512]{2,1,0:T(8,128)}, f32[8,64,512]{2,1,0:T...) custom-call(bf16[2,2,8,48,512]{4,3,2,1,0:T(8,128)(2,1)} %get-tuple-e, ...), custom_call_target="tpu_custom_call" | custom-call | tf_op jit(solution)/shard_map/pallas_call | solution.py:1214
  410.2 1.9 copy.53
  412.1 0.7 constant_dynamic-slice_fusion
  412.8 0.5 slice_bitcast_fusion
  413.4 2.0 copy.65
  415.3 2.3 copy.66
  417.6 1.0 copy.67
  418.6 1.0 copy.68
  419.6 0.6 copy-done.2
  420.2 1.6 copy.69
  421.8 1.3 copy-done.1
  423.1 1.6 copy.70
  424.6 1.3 copy-done
  425.9 1.6 copy.71
  (40 shorter events, 1.2 us)
Async XLA Ops:
  0.6 7.9 %copy-start.9 = (f32[1,128,2]{1,2,0:T(2,128)S(1)}, f32[1,128,2]{1,2,0:T(2,128)}, u32[]{:S(2)}) copy-start(f32[1,128,2]{1,2,0:T(2,128)} %param.21) | copy-start | bytes 3076
  0.7 8.7 %copy-start.6 = (bf16[64,2,512]{2,1,0:T(2,128)(2,1)S(1)}, bf16[64,2,512]{2,1,0:T(2,128)(2,1)}, u32[]{:S(2)}) copy-start(bf16[64,2,512]{2,1,0:T(2,128)(2,1)} %param.24) | copy-start | bytes 393220
  0.7 8.8 %copy-start.5 = (bf16[8,64,512]{2,1,0:T(8,128)(2,1)S(1)}, bf16[8,64,512]{2,1,0:T(8,128)(2,1)}, u32[]{:S(2)}) copy-start(bf16[8,64,512]{2,1,0:T(8,128)(2,1)} %param.25) | copy-start | bytes 1572868
  1.6 8.8 %copy-start.8 = (f32[1,128,2]{1,2,0:T(2,128)S(1)}, f32[1,128,2]{1,2,0:T(2,128)}, u32[]{:S(2)}) copy-start(f32[1,128,2]{1,2,0:T(2,128)} %param.23) | copy-start | bytes 3076
  1.6 9.6 %copy-start.12 = (s32[1,8]{1,0:T(1,128)S(1)}, s32[1,8]{1,0:T(1,128)}, u32[]{:S(2)}) copy-start(s32[1,8]{1,0:T(1,128)} %param.19) | copy-start | bytes 100
  1.6 10.4 %copy-start.7 = (s32[1,128,2]{1,2,0:T(2,128)S(1)}, s32[1,128,2]{1,2,0:T(2,128)}, u32[]{:S(2)}) copy-start(s32[1,128,2]{1,2,0:T(2,128)} %param.20) | copy-start | bytes 3076
  1.6 11.0 %copy-start.10 = (bf16[64]{0:T(256)(128)(2,1)S(1)}, bf16[64]{0:T(256)(128)(2,1)}, u32[]{:S(2)}) copy-start(bf16[64]{0:T(256)(128)(2,1)} %param.28) | copy-start | bytes 388
  1.6 11.0 %copy-start.11 = (bf16[64]{0:T(256)(128)(2,1)S(1)}, bf16[64]{0:T(256)(128)(2,1)}, u32[]{:S(2)}) copy-start(bf16[64]{0:T(256)(128)(2,1)} %param.27) | copy-start | bytes 388
  410.2 7.4 %copy-start.4 = (f32[8,64,512]{2,1,0:T(8,128)S(1)}, f32[8,64,512]{2,1,0:T(8,128)}, u32[]{:S(2)}) copy-start(f32[8,64,512]{2,1,0:T(8,128)} %get-tuple-element.113) | copy-start | bytes 3145732
  413.4 5.2 %copy-start.3 = (f32[8,64,512]{2,1,0:T(8,128)S(1)}, f32[8,64,512]{2,1,0:T(8,128)}, u32[]{:S(2)}) copy-start(f32[8,64,512]{2,1,0:T(8,128)} %get-tuple-element.61) | copy-start | bytes 3145732
  417.6 2.6 copy-start.2
  420.2 2.9 copy-start.1
  423.0 2.9 copy-start

commit v5 on v4

--- a/solution.py
+++ b/solution.py
@@ -12,25 +12,6 @@
 EPSILON = 1e-06
 BF = jnp.bfloat16
 F32 = jnp.float32
-
-
-def dot(spec, left, right):
-    return jnp.einsum(spec, left, right, preferred_element_type=F32)
-
-
-def swap(blocks, axes):
-    return lax.all_to_all(blocks, axes, split_axis=0, concat_axis=0, tiled=True)
-
-
-def slot_places(routes, expert_count, capacity):
-    length = routes.shape[-2]
-    names = jnp.arange(expert_count, dtype=jnp.int32)[:, None]
-    member = jnp.any(jnp.swapaxes(routes, -1, -2)[..., None, :] == names, -3)
-    order = jnp.arange(length)
-    before = (order[:, None] < order[None, :]).astype(BF)
-    rank = dot("...et,tu->...eu", member.astype(BF), before)
-    slots = jnp.arange(capacity, dtype=F32)[:, None]
-    return (member[..., None, :] & (rank[..., None, :] == slots)).astype(BF)
 
 
 def remote(src, dst, send, recv, device):
@@ -109,7 +90,7 @@
     each(2 * owners, lambda step: outgoing(step).wait())
 
 
-def share_slices(slices, sends, recvs, own, share, shares):
+def share_start(slices, sends, recvs, own, share, shares):
     def copy(step):
         return remote(
             slices.at[share],
@@ -120,6 +101,11 @@
         )
 
     each(shares, lambda step: copy(step).start())
+    return copy
+
+
+def share_slices(slices, sends, recvs, own, share, shares):
+    copy = share_start(slices, sends, recvs, own, share, shares)
     each(shares, lambda step: copy(step).wait())
 
 
@@ -174,13 +160,7 @@
     up_weight,
     down_weight,
     upstream,
-    sel_ffn,
-    gate_slot,
-    pick_att,
-    att_gate,
-    pick_ffn,
-    ffn_gate,
-    ends,
+    lengths,
     cos_key,
     sin_key,
     first_full,
@@ -202,6 +182,10 @@
     d_both,
     d_parts,
     output_part,
+    sel_ffn,
+    sel_att,
+    gate_columns,
+    pick_ffn,
     features,
     expert_in,
     expert_grad,
@@ -354,13 +338,12 @@
     def picked_rows(source, out, scale):
         for index in range(2):
             cut = pl.ds(pl.multiple_of(core * wide + index * piece, piece), piece)
-            taken = mm(sel_ffn[...], source[:, cut], 0, 0)
+            taken = mm(sel_ffn[...], source[:, cut])
             if scale is not None:
                 taken = taken * scale
             taken = taken.astype(BF).reshape(owners, slots, piece)
             out[:, :, index * piece : (index + 1) * piece] = taken
 
-    picked_rows(upstream, grads_out, gate_slot[...])
 
     def grad_copy(step):
         return to_owner(grads_out.at.__getitem__, expert_grad.at[core, own], grad_send, grad_recv, step)
@@ -381,6 +364,30 @@
     for name in range(owners):
         slot_keys[name] = map_keys(float(name))
 
+    gate_columns[...] = jnp.transpose(marks[...])
+    names = lax.broadcasted_iota(jnp.int32, (owners, group), 0).astype(F32)
+    member = (marks[2:3, :] == names) | (marks[3:4, :] == names)
+    rank = mm(jnp.where(member, 1.0, 0.0).astype(BF), before)
+    ffn_keys = jnp.where(member, rank, -1.0)
+    gate_slots = []
+    for name in range(owners):
+        cut = slice(name * slots, (name + 1) * slots)
+        key = slot_keys[name, pl.ds(own, 1), :]
+        hot = jnp.where(key == slot_names, 1.0, 0.0)
+        for choice in range(TOPK):
+            chosen_here = jnp.where(marks[choice : choice + 1, :] == float(name), hot, 0.0)
+            sel_att[cut, choice * group : (choice + 1) * group] = chosen_here.astype(BF)
+        hot = jnp.where(ffn_keys[name : name + 1, :] == slot_names, 1.0, 0.0)
+        sel_ffn[cut, :] = hot.astype(BF)
+        gate = jnp.zeros((slots, 1), F32)
+        for choice in range(TOPK):
+            chosen_here = jnp.where(marks[2 + choice : 3 + choice, :] == float(name), hot, 0.0)
+            pick_ffn[cut, choice * group : (choice + 1) * group] = chosen_here.astype(BF)
+            weighed = chosen_here * marks[6 + choice : 7 + choice, :]
+            gate = gate + jnp.sum(weighed, 1, keepdims=True)
+        gate_slots.append(gate)
+    picked_rows(upstream, grads_out, jnp.concatenate(gate_slots, 0))
+
     def one_hot(name, block):
         key = slot_keys[name, pl.ds(block, 1), :]
         return jnp.where(key == slot_names, 1.0, 0.0)
@@ -393,9 +400,9 @@
         name, block = lax.div(index, columns), part * columns + lax.rem(index, columns)
         hot = one_hot(name, block)
         pos = mm(hot.astype(BF), token_names) + (block * group).astype(F32)
-        start = jnp.zeros_like(pos)
-        for end in range(ends.shape[0]):
-            bound = ends[end : end + 1, :]
+        start, bound = jnp.zeros_like(pos), jnp.zeros((1, group), F32)
+        for document in range(lengths.shape[0]):
+            bound = bound + lengths[document : document + 1, :]
             start = jnp.maximum(start, jnp.where(bound <= pos, bound, 0.0))
         span = pl.ds(pl.multiple_of(index * slots, slots), slots)
         row_info[span, 0:1] = pos[:, 0:1]
@@ -547,9 +554,10 @@
     def at_tokens(pick, gate, landing):
         total = jnp.zeros((group, piece), F32)
         for choice in range(TOPK):
-            taken = mm(pick[choice], landing[0].reshape(rows, piece))
-            taken = taken + mm(pick[choice], landing[1].reshape(rows, piece))
-            total = total + gate[choice] * taken
+            span = slice(choice * group, (choice + 1) * group)
+            taken = mm(pick[:, span], landing[0].reshape(rows, piece), 0, 0)
+            taken = taken + mm(pick[:, span], landing[1].reshape(rows, piece), 0, 0)
+            total = total + gate_columns[:, gate + choice : gate + choice + 1] * taken
         return total
 
     def map_product(index):
@@ -559,7 +567,7 @@
     outgoing = send_home(near, landing, home_send, home_recv, own, half, core, owners)
     up_ring.forward()
     wait_home(outgoing, owners)
-    slices[share] = at_tokens(pick_att, att_gate, landing).astype(BF)
+    slices[share] = at_tokens(sel_att, 4, landing).astype(BF)
     share_slices(slices, slice_send, slice_recv, own, share, shares)
 
     total = jnp.zeros((group, 1), F32)
@@ -573,7 +581,7 @@
     for index in range(2):
         cut = pl.ds(pl.multiple_of(core * wide + index * piece, piece), piece)
         rounded = (state[:, cut] * inv * gains[1:2, cut]).astype(BF)
-        taken = mm(sel_ffn[...], rounded, 0, 0).astype(BF).reshape(owners, slots, piece)
+        taken = mm(sel_ffn[...], rounded).astype(BF).reshape(owners, slots, piece)
         rows_out[:, :, index * piece : (index + 1) * piece] = taken
 
     def row_copy(step):
@@ -682,7 +690,7 @@
     )
     across.start()
     wait_home(outgoing_two, owners)
-    rest = at_tokens(pick_ffn, ffn_gate, landing_two)
+    rest = at_tokens(pick_ffn, 6, landing_two)
     span = pl.ds(pl.multiple_of(share * piece, piece), piece)
     output_part[...] = (state[:, span] + rest).astype(BF)
     across.wait()
@@ -702,7 +710,7 @@
     upstream,
     gains,
     sel_att,
-    att_gate,
+    gate_columns,
     out_full,
     queries,
     pairs,
@@ -724,9 +732,7 @@
     output,
     input_grad,
     gain_grads,
-    query_grad,
-    out_grad,
-    kv_grad,
+    maps_in,
     gate_grad,
     up_grad,
     down_grad,
@@ -754,9 +760,10 @@
     map_grads,
     early,
     late,
-    maps_in,
     gain_out,
     gain_in,
+    gain_mid,
+    gain_last,
     weights,
     normed,
     features,
@@ -805,20 +812,7 @@
     other = {"expert": own, "tensor": 2 * half + 1 - core}
     dp, dps = lax.axis_index("dp"), d_both_all.shape[0]
 
-    def owner_at(step):
-        return lax.rem(dp + lax.div(step, owners), dps), lax.rem(own + lax.rem(step, owners), owners)
-
-    def hello(step):
-        to_dp, to = owner_at(step)
-        pl.semaphore_signal(
-            pltpu.get_barrier_semaphore(),
-            inc=1,
-            device_id={"dp": to_dp, "expert": to},
-            device_id_type=pl.DeviceIdType.MESH,
-        )
-
-    each(dps * owners, hello)
-    enter(own, half, core, owners, greeted=dps * owners - 1)
+    enter(own, half, core, owners, [lax.rem(dp + step, dps) for step in range(1, dps)])
     loads = [
         pltpu.make_async_copy(far_weights, weights, local.at[4]),
         pltpu.make_async_copy(far_normed, normed, local.at[5]),
@@ -832,12 +826,6 @@
     both_ring.start(d_both)
     hidden_ring = Ring(hidden_all, ring_send, ring_recv, 4, dp, dps)
     hidden_ring.start(hidden)
-    keeps = [
-        pltpu.make_async_copy(d_both, d_both_all.at[dp], local.at[0]),
-        pltpu.make_async_copy(hidden, hidden_all.at[dp], local.at[7]),
-    ]
-    for copy in keeps:
-        copy.start()
 
     used_slots = pl.ds(0, slots)
     return_near, return_out = sibling.at[:, :, used_slots], near.at[:, :, used_slots]
@@ -848,8 +836,8 @@
         return_out[side] = (parts[core, side].astype(F32) + return_near[side].astype(F32)).astype(BF)
     outgoing = send_home(return_out, return_in, return_send, return_recv, own, half, core, owners)
     wait_home(outgoing, owners)
-    total = mm(sel_ffn[...], return_in[0].reshape(rows, piece))
-    total = total + mm(sel_ffn[...], return_in[1].reshape(rows, piece))
+    total = mm(sel_ffn[...], return_in[0].reshape(rows, piece), 0, 0)
+    total = total + mm(sel_ffn[...], return_in[1].reshape(rows, piece), 0, 0)
     parts_joined[share] = total.astype(BF)
     share_slices(parts_joined, join_send, join_recv, own, share, shares)
 
@@ -870,7 +858,7 @@
         start = pl.multiple_of(core * wide + index * piece, piece)
         grad = input_grad[:, pl.ds(start, piece)]
         both = jnp.concatenate(
-            [(att_gate[0] * grad).astype(BF), (att_gate[1] * grad).astype(BF)], 0
+            [(gate_columns[:, 4:5] * grad).astype(BF), (gate_columns[:, 5:6] * grad).astype(BF)], 0
         )
         picked = mm(sel_att[...], both).astype(BF).reshape(owners, slots, piece)
         rows_out[:, :, index * piece : (index + 1) * piece] = picked
@@ -992,9 +980,26 @@
     for index in range(dps):
         features_turned[index] = jnp.transpose(acts[index, :, :piece].astype(F32)).astype(BF)
 
-    def load(side):
-        source = hidden_all if side == 2 else d_both_all.at[:, pl.ds(side * used, used)]
-        return pltpu.make_async_copy(source, acts, local.at[1])
+    class load:
+        def __init__(self, side):
+            rows_here = pl.ds(0 if side == 2 else side * used, used)
+            mine, others = (hidden, hidden_all) if side == 2 else (d_both, d_both_all)
+            self.copies = [pltpu.make_async_copy(mine.at[rows_here], acts.at[dp], local.at[0])]
+            for step in range(1, dps):
+                index = lax.rem(dp + step, dps)
+                self.copies.append(
+                    pltpu.make_async_copy(
+                        others.at[index, rows_here], acts.at[index], local.at[8 + step]
+                    )
+                )
+
+        def start(self):
+            for copy in self.copies:
+                copy.start()
+
+        def wait(self):
+            for copy in self.copies:
+                copy.wait()
 
     def map_grad(index):
         cut = pl.ds(pl.multiple_of(lax.rem(index, 2) * piece, piece), piece)
@@ -1052,10 +1057,10 @@
     ).astype(BF)
     step_copy(2).start()
     step_copy(3).start()
+    hidden_ring.forward()
+    keep_grad(dp)
     both_ring.finish()
-    keeps[0].wait()
     load(0).start()
-    hidden_ring.forward()
 
     tile = 2 * HD
     whole, rest = units // tile, units % tile
@@ -1115,10 +1120,17 @@
             total = total + mm(acts[index, :, span], features[index], 0, 0)
         return total
 
+    wait_home(outgoing, owners)
+    total = jnp.zeros((group, piece), F32)
+    for side in range(2):
+        for index in range(owners):
+            total = total + landing[side, index].astype(F32)
+    slices[share, 0] = total.astype(BF)
+    slices[share, 1] = output_part[...]
+    joining = share_start(slices, slice_send, slice_recv, own, share, shares)
     load(0).wait()
     unit_tiles(wide_product, gate_grad, False)
     load(1).start()
-    keep_grad(dp)
 
     step_copy(2).wait()
     step_copy(3).wait()
@@ -1141,14 +1153,8 @@
 
     each(owners, lambda step: map_copy(step).start())
     maps_in[own] = map_grads[dp, home_rows(own), :]
-    wait_home(outgoing, owners)
-    total = jnp.zeros((group, piece), F32)
-    for side in range(2):
-        for index in range(owners):
-            total = total + landing[side, index].astype(F32)
-    slices[share, 0] = total.astype(BF)
-    slices[share, 1] = output_part[...]
-    share_slices(slices, slice_send, slice_recv, own, share, shares)
+
+    each(shares, lambda step: joining(step).wait())
     inv = inv_one[...]
     mean = jnp.zeros_like(inv)
     for index in range(shares):
@@ -1160,48 +1166,56 @@
         for chunk in range(piece // HD):
             lanes = slice(chunk * HD, (chunk + 1) * HD)
             place = index * (piece // HD) + chunk
-            gain_out[place, 0:1] = gain_one[:, lanes]
-            gain_out[place, 1:2] = d_gain_two[:, place * HD : (place + 1) * HD]
+            gain_out[index, chunk, 0:1] = gain_one[:, lanes]
+            gain_out[index, chunk, 1:2] = d_gain_two[:, place * HD : (place + 1) * HD]
 
     def gain_copy(step):
-        to_dp, to = owner_at(step)
+        to = lax.rem(own + step, owners)
         return remote(
-            gain_out.at[lax.div(to_dp * owners + to, HD // local_rows)],
-            gain_in.at[dp * owners + own],
+            gain_out.at[:, lax.div(to, 2)],
+            gain_in.at[own],
             gain_send.at[step],
             gain_recv.at[step],
-            {"dp": to_dp, "expert": to},
-        )
-
-    each(dps * owners, lambda step: gain_copy(step).start())
-    gain_in[dp * owners + own] = gain_out[lax.div(dp * owners + own, HD // local_rows)]
+            {"expert": to, "tensor": share},
+        )
+
+    def far_gain_copy(step):
+        to = lax.rem(dp + step, dps)
+        return remote(
+            gain_mid.at[to],
+            gain_last.at[dp],
+            gain_send.at[owners + step],
+            gain_recv.at[owners + step],
+            {"dp": to},
+        )
+
+    each(owners, lambda step: gain_copy(step).start())
+    gain_in[own] = gain_out[:, lax.div(own, 2)]
     mean = mean * (inv * inv * inv / width)
     for index in range(shares):
         span = slice(index * piece, (index + 1) * piece)
         grad = gains[0:1, span] * slices[index, 0].astype(F32)
         value = tokens[:, span].astype(F32)
         input_grad[:, span] = input_grad[:, span] + inv * grad - value * mean
-
     load(1).wait()
     unit_tiles(wide_product, up_grad, False)
+    each(owners, lambda step: gain_copy(step).wait())
+    total = gain_in[0]
+    for index in range(1, owners):
+        total = total + gain_in[index]
+    gain_mid[...] = total
+    each(dps, lambda step: far_gain_copy(step).start())
+    gain_last[dp] = gain_mid[dp]
     hidden_ring.finish()
-    keeps[1].wait()
     load(2).start()
-    each(owners, lambda step: map_copy(step).wait())
-    for index in range(owners):
-        query_grad[index] = maps_in[index, :, :head_width].astype(F32)
-        out_grad[index] = maps_in[index, :, middle:].astype(F32)
-        column = index // 2
-        kv_grad[index % 2, :, column * HD : (column + 1) * HD] = maps_in[
-            index, :, head_width:middle
-        ].astype(F32)
     load(2).wait()
     unit_tiles(tall_product, down_grad, True)
-    each(dps * owners, lambda step: gain_copy(step).wait())
-    total = gain_in[0, 0:2]
-    for index in range(1, dps * owners):
-        total = total + gain_in[index, 0:2]
+    each(dps, lambda step: far_gain_copy(step).wait())
+    total = gain_last[0, 0:2]
+    for index in range(1, dps):
+        total = total + gain_last[index, 0:2]
     gain_grads[...] = total
+    each(owners, lambda step: map_copy(step).wait())
     both_ring.drain(d_both)
     hidden_ring.drain(hidden)
 
@@ -1257,32 +1271,25 @@
     local = kv_weight.shape[0]
     head_width = kv_weight.shape[2]
 
-    def choice_places(places_here, routes):
-        names = jnp.arange(places_here.shape[0], dtype=jnp.int32)
-        picks = (routes[:, :, None] == names).astype(BF)
-        return jnp.einsum("mst,tjm->jtms", places_here, picks)
-
-    place_ffn = slot_places(ffn_routes[0], owners, ffn_cap)
-    pick_ffn = choice_places(place_ffn, ffn_routes[0])
-    ffn_gate = ffn_gates[0]
-    gate_slot = jnp.einsum("jtms,tj->ms", pick_ffn, ffn_gate, precision=lax.Precision.HIGHEST)
-
     kv_parts = jnp.transpose(kv_weight.reshape(local, 2, columns, HD), (2, 1, 0, 3))
     pack_one = jnp.concatenate([kv_parts.reshape(owners, local, HD), query_weight], 2)
     own_gains = jnp.stack([attn_gain, ffn_gain]).astype(F32)
     own_gains = jnp.pad(own_gains, ((0, 8 - 2), (0, HD - local)))
     pack_two = jnp.swapaxes(out_weight, 1, 2)
-    marks = jnp.pad(att_routes[0].T.astype(F32), ((0, 8 - TOPK), (0, 0)), constant_values=-1.0)
-    place_att = slot_places(att_routes[0], ATT_EXP, att_cap)
-    pick_att = choice_places(place_att, att_routes[0])
-    att_gate = att_gates[0]
-    ends = jnp.cumsum(doc_lengths[0], dtype=jnp.int32).astype(F32)
-    ends = jnp.broadcast_to(ends[:, None], (ends.shape[0], HD))
+    marks = jnp.concatenate(
+        [
+            att_routes[0].T.astype(F32),
+            ffn_routes[0].T.astype(F32),
+            att_gates[0].T,
+            ffn_gates[0].T,
+        ],
+        0,
+    )
+    lengths = jnp.broadcast_to(doc_lengths[0].astype(F32)[:, None], (doc_lengths.shape[1], HD))
     angles = np.arange(seq_len)[:, None] * 10000.0 ** (-np.arange(HD // 2) * 2.0 / HD)
     cos_key = jnp.asarray(np.concatenate([np.cos(angles)] * 2, 1), F32)
     sin_key = jnp.asarray(np.concatenate([-np.sin(angles), np.sin(angles)], 1), F32)
     used = min(group, group * TOPK * 5 // (4 * owners))
-    sel_ffn = jnp.transpose(place_ffn, (2, 0, 1)).reshape(group, -1)
     units = gate_weight.shape[2]
     slots = att_cap
     head_rows = columns * slots
@@ -1307,6 +1314,9 @@
         d_both,
         d_parts,
         output_part,
+        sel_ffn,
+        sel_att,
+        gate_columns,
     ) = call_kernel(
         first_kernel,
         3,
@@ -1330,8 +1340,12 @@
             ((2, owners * used, units), BF),
             ((2,) + block, BF),
             ((group, piece), BF),
+            ((rows, group), BF),
+            ((rows, TOPK * group), BF),
+            ((group, 8), F32),
         ],
         [
+            ((rows, TOPK * group), BF),
             ((2, dps, owners * used, piece), BF),
             ((2, owners, slots, width // 2), BF),
             ((2, owners, slots, width // 2), BF),
@@ -1371,13 +1385,7 @@
             up_weight[0],
             down_weight[0],
             cotangent[0],
-            sel_ffn,
-            gate_slot.reshape(-1, 1),
-            pick_att.reshape(TOPK, group, rows),
-            att_gate.T[:, :, None],
-            pick_ffn.reshape(TOPK, group, rows),
-            ffn_gate.T[:, :, None],
-            ends,
+            lengths,
             cos_key,
             sin_key,
         ],
@@ -1390,9 +1398,7 @@
         output,
         input_grad,
         gain_grads,
-        query_grad,
-        out_grad,
-        kv_grad,
+        map_grads,
         gate_grad,
         up_grad,
         down_grad,
@@ -1404,9 +1410,7 @@
             ((group, width), BF),
             ((group, width), F32),
             ((2, HD), F32),
-            ((owners, local, head_width), F32),
-            ((owners, local, head_width), F32),
-            ((2, local, head_width), F32),
+            ((owners, local, grad_width), BF),
             ((piece, units), F32),
             ((piece, units), F32),
             ((units, piece), F32),
@@ -1436,9 +1440,10 @@
             ((dps, piece, grad_width), BF),
             ((2, piece // 2, grad_width), BF),
             ((2, piece, grad_width), BF),
-            ((owners, local, grad_width), BF),
-            ((width // HD, 8, HD), F32),
-            ((dps * owners, 8, HD), F32),
+            ((dps, owners // 2, 8, HD), F32),
+            ((owners, dps, 8, HD), F32),
+            ((dps, 8, HD), F32),
+            ((dps, 8, HD), F32),
             ((dps, owners * local, HD + head_width), BF),
             ((2, owners, group, width // 2), BF),
             ((dps, owners * used, piece), BF),
@@ -1462,7 +1467,7 @@
             owners,
             8,
             8,
-            8,
+            12,
             2,
             2,
             2 * owners,
@@ -1473,8 +1478,8 @@
             4,
             owners,
             owners,
-            dps * owners,
-            dps * owners,
+            owners + dps,
+            owners + dps,
             2,
         ],
         [
@@ -1484,8 +1489,8 @@
             inv_two,
             cotangent[0],
             gains,
-            jnp.transpose(pick_att, (2, 3, 0, 1)).reshape(rows, -1),
-            att_gate.T[:, :, None],
+            sel_att,
+            gate_columns,
             out_full,
             queries,
             pairs,
@@ -1506,13 +1511,15 @@
             features_all,
         ],
         far_args=(17, 18, 23, 24, 25),
-        far_outs=(6, 7, 8, 9, 10),
+        far_outs=(4, 5, 6, 7, 8),
     )
     chunk = HD // local
     place = lax.rem(own, chunk) * local
     gain_grads = lax.dynamic_slice_in_dim(gain_grads, place, local, 1)
-    kv_grad = jnp.swapaxes(kv_grad, 0, 1)
-    out_grad = jnp.swapaxes(out_grad, 1, 2)
+    query_grad = map_grads[:, :, :head_width].astype(F32)
+    out_grad = jnp.swapaxes(map_grads[:, :, head_width + HD :].astype(F32), 1, 2)
+    kv_grad = map_grads[:, :, head_width : head_width + HD].reshape(columns, 2, local, HD)
+    kv_grad = jnp.transpose(kv_grad, (2, 1, 0, 3)).reshape(local, 2, head_width).astype(F32)
     return (
         output[None],
         input_grad[None],

time: 428 us -> 401 us (0.937)
  Pallas kernels: 396 us -> 373 us
  local copies, waits for them, and re-layouts: 24.1 us -> 15.9 us
    pallas_call x2, Pallas kernels: 396 us -> 373 us  [call_kernel(): pl.pallas_call(kernel, out_shape=[jax.ShapeDtypeStruct(shape, dtype) for...]
    unnamed x35 -> x13, local copies, waits for them, and re-layouts: 16.8 us -> 11.5 us
where the time goes in v5:
time: 401 us; the launch traced here: 398 us
  Pallas kernels  373 us (93%)
  local copies, waits for them, and re-layouts  15.9 us (4%)
  other arithmetic  8.7 us (2%)
    pallas_call x2, Pallas kernels, call_kernel(): pl.pallas_call(kernel, out_shape=[jax.ShapeDtypeStruct(shape, dtype) for...  373 us
    unnamed x13, local copies, waits for them, and re-layouts  11.5 us

profile of v5, /device:TPU:1, one launch (start us, length us, event | category | flops | bytes accessed | tf_op | source)
XLA Modules:
  0.0 398.1 jit_solution(15202218652161091086)
XLA Ops:
  0.6 0.7 convert_bitcast_fusion.2
  1.3 1.3 pad_maximum_fusion.1.marks
  2.6 1.0 reshape.43
  3.7 2.0 pad_maximum_fusion.pack_one
  5.6 0.7 convert_bitcast_fusion.4
  6.3 0.7 broadcast_in_dim.21.lengths
  6.9 1.3 fusion.6.own_gains
  8.2 218.8 %shard_map.240 = (bf16[4,512,640]{2,1,0:T(8,128)(2,1)}, bf16[4,512,512]{2,1,0:T(8,128)(2,1)}, bf16[2,8,128,1024]{3,2,1,0:T(8,128)(2,1)}, f32[2,2048]{1,0:T(2,128...) custom-call(bf16[128,2048]{1,0:T(8,128)(2,1)} %bitcast.46, ...), custom_call_target="tpu_custom_call" | custom-call | tf_op jit(solution)/shard_map/pallas_call | solution.py:1228
  227.0 154.0 %shard_map.241 = (bf16[128,2048]{1,0:T(8,128)(2,1)}, f32[128,2048]{1,0:T(8,128)}, f32[2,128]{1,0:T(2,128)}, bf16[8,64,1152]{2,1,0:T(8,128)(2,1)}, f32[512,1408]{...) custom-call(bf16[2,2,8,48,512]{4,3,2,1,0:T(8,128)(2,1)} %get-tuple-e, ...), custom_call_target="tpu_custom_call" | custom-call | tf_op jit(solution)/shard_map/pallas_call | solution.py:1228
  381.1 0.0 copy-start.3
  381.1 2.8 convert_bitcast_fusion
  383.9 0.0 copy-start.2
  383.9 1.1 slice.15
  385.0 0.2 copy.28
  385.2 0.9 reshape.46
  386.1 0.0 copy-done.3
  386.1 0.1 constant_dynamic-slice_fusion
  386.1 0.5 slice_bitcast_fusion
  386.7 1.9 copy.34
  388.5 2.3 copy.35
  390.8 0.0 copy-done.2
  390.8 0.0 copy-start.1
  390.8 1.6 copy.36
  392.4 1.3 copy-done.1
  393.7 0.0 copy-start
  393.7 1.6 copy.37
  395.3 1.3 copy-done
  396.5 1.6 copy.38
  (2 shorter events, 0.0 us)
Async XLA Ops:
  381.1 5.0 %copy-start.3 = (f32[2,128]{1,0:T(2,128)S(1)}, f32[2,128]{1,0:T(2,128)}, u32[]{:S(2)}) copy-start(f32[2,128]{1,0:T(2,128)} %get-tuple-element.64) | copy-start | bytes 3076
  383.9 6.9 %copy-start.2 = (f32[512,1408]{1,0:T(8,128)S(1)}, f32[512,1408]{1,0:T(8,128)}, u32[]{:S(2)}) copy-start(f32[512,1408]{1,0:T(8,128)} %get-tuple-element.65) | copy-start | bytes 8650756
  390.8 2.9 copy-start.1
  393.7 2.9 copy-start

commit v6 on v5

--- a/solution.py
+++ b/solution.py
@@ -155,6 +155,7 @@
     marks,
     own_gains,
     pack_one,
+    query_weight,
     pack_two,
     gate_weight,
     up_weight,
@@ -163,9 +164,9 @@
     lengths,
     cos_key,
     sin_key,
-    first_full,
-    out_full,
-    normed,
+    far_first,
+    far_out,
+    far_normed,
     gains,
     inv_one,
     queries,
@@ -185,6 +186,9 @@
     sel_ffn,
     sel_att,
     gate_columns,
+    first_full,
+    out_full,
+    normed,
     pick_ffn,
     features,
     expert_in,
@@ -267,8 +271,21 @@
         device = {"expert": to, "tensor": share}
         return remote(src(to), dst, sends.at[step], recvs.at[step], device)
 
+    key_cut, query_cut = pl.ds(0, HD), pl.ds(HD, first_full.shape[2] - HD)
+
     def pack_copy(step):
-        return to_owner(pack_one.at.__getitem__, first_full.at[dp, own_rows], pack_send, pack_recv, step)
+        target = first_full.at[dp, own_rows, key_cut]
+        return to_owner(pack_one.at.__getitem__, target, pack_send, pack_recv, step)
+
+    def query_part_copy(step):
+        to = lax.rem(own + step, owners)
+        return remote(
+            query_weight.at[to],
+            first_full.at[dp, own_rows, query_cut],
+            pack_send.at[2 * owners + step],
+            pack_recv.at[2 * owners + step],
+            {"expert": to, "tensor": share},
+        )
 
     def second_copy(step):
         to = lax.rem(own + step, owners)
@@ -293,6 +310,7 @@
     def mark_copy(step):
         return to_owner(lambda to: marks, routes.at[own], mark_send, mark_recv, step)
 
+    each(owners, lambda step: query_part_copy(step).start())
     each(owners, lambda step: pack_copy(step).start())
     each(owners, lambda step: mark_copy(step).start())
 
@@ -314,7 +332,7 @@
     each(owners, lambda step: gain_copy(step).start())
     low_ring.start(gate_weight.at[low])
     own_copies = [
-        pltpu.make_async_copy(pack_one.at[own], first_full.at[dp, own_rows], local.at[0]),
+        pltpu.make_async_copy(pack_one.at[own], first_full.at[dp, own_rows, key_cut], local.at[0]),
         pltpu.make_async_copy(pack_two.at[own], out_full.at[dp, own_rows], local.at[1]),
         pltpu.make_async_copy(gate_weight, gate_up.at[0, dp], local.at[2]),
         pltpu.make_async_copy(up_weight, gate_up.at[1, dp], local.at[3]),
@@ -325,7 +343,13 @@
     routes[own] = marks[...]
     normed[core, own] = tokens[:, pl.ds(pl.multiple_of(core * wide, wide), wide)]
 
+    own_query = pltpu.make_async_copy(
+        query_weight.at[own], first_full.at[dp, own_rows, query_cut], local.at[8]
+    )
+    own_query.start()
     own_copies[0].wait()
+    own_query.wait()
+    each(owners, lambda step: query_part_copy(step).wait())
     each(owners, lambda step: pack_copy(step).wait())
     one_ring.start()
     high_ring.start(gate_weight.at[high])
@@ -433,6 +457,8 @@
     lax.fori_loop(0, owners, squares, 0)
     inv_one[...] = inv_all[own]
     one_ring.finish()
+    kept = [pltpu.make_async_copy(first_full, far_first, local.at[5])]
+    kept[0].start()
 
     each(dps, lambda step: far_gain_copy(step).wait())
     left = lax.broadcasted_iota(jnp.int32, (8, HD), 1) < HD // 2
@@ -458,6 +484,8 @@
         return carry
 
     lax.fori_loop(0, owners, norm_block, 0)
+    kept.append(pltpu.make_async_copy(normed, far_normed, local.at[6]))
+    kept[1].start()
     query = jnp.zeros((rows, columns * HD), F32)
     for index in range(dps):
         cut = slice((index % 2) * piece, (index % 2 + 1) * piece)
@@ -530,6 +558,8 @@
     high_ring.forward()
     down_ring.start(down_weight)
     two_ring.finish()
+    kept.append(pltpu.make_async_copy(out_full, far_out, local.at[7]))
+    kept[2].start()
     each(owners, lambda step: back_copy(step).wait())
     for column in range(columns):
         for side in range(2):
@@ -537,7 +567,7 @@
                 side * head_rows : (side + 1) * head_rows, column * HD : (column + 1) * HD
             ] = mixed_in[2 * column + side]
 
-    def chip_sum(product, far, near, sibling, base):
+    def chip_start(product, base):
         def across(side):
             place = base + side
             return remote(far.at[side], sibling.at[side], one_send.at[place], one_recv.at[place], other)
@@ -547,9 +577,13 @@
             across(side).start()
         for side in range(2):
             near[side] = product(2 * side + core)
-        for side in range(2):
-            across(side).wait()
-            near[side] = (near[side].astype(F32) + sibling[side].astype(F32)).astype(BF)
+
+        def finish():
+            for side in range(2):
+                across(side).wait()
+                near[side] = (near[side].astype(F32) + sibling[side].astype(F32)).astype(BF)
+
+        return finish
 
     def at_tokens(pick, gate, landing):
         total = jnp.zeros((group, piece), F32)
@@ -563,7 +597,7 @@
     def map_product(index):
         return mm(mixed[...], out_full[index], 1, 1).astype(BF).reshape(owners, slots, piece)
 
-    chip_sum(map_product, far, near, sibling, 1)
+    chip_start(map_product, 1)()
     outgoing = send_home(near, landing, home_send, home_recv, own, half, core, owners)
     up_ring.forward()
     wait_home(outgoing, owners)
@@ -665,10 +699,7 @@
     unit_tiles(up_tile)
     down_ring.finish()
     each(dps, lambda step: feature_copy(step).start())
-    chip_sum(lambda index: loose(mm(hidden[...], down[index])), far, near, sibling, 7)
-    outgoing_two = send_home(
-        near, landing_two, home_two_send, home_two_recv, own, half, core, owners
-    )
+    finish_sum = chip_start(lambda index: loose(mm(hidden[...], down[index])), 7)
 
     def grad_tile(cut):
         grad = mm(features[1, 0], down[0, cut, :], 1, 1)
@@ -680,6 +711,10 @@
         d_both[1, :, cut] = (grad * gate * sigma).astype(BF)
 
     unit_tiles(grad_tile)
+    finish_sum()
+    outgoing_two = send_home(
+        near, landing_two, home_two_send, home_two_recv, own, half, core, owners
+    )
     for index in range(dps):
         total = mm(d_both[0], gate_up[0, index], 1, 1) + mm(d_both[1], gate_up[1, index], 1, 1)
         d_parts[index % 2, index // 2] = loose(total)
@@ -694,6 +729,8 @@
     span = pl.ds(pl.multiple_of(share * piece, piece), piece)
     output_part[...] = (state[:, span] + rest).astype(BF)
     across.wait()
+    for copy in kept:
+        copy.wait()
     one_ring.drain()
     two_ring.drain()
     low_ring.drain(gate_weight.at[low])
@@ -835,6 +872,9 @@
     for side in range(2):
         return_out[side] = (parts[core, side].astype(F32) + return_near[side].astype(F32)).astype(BF)
     outgoing = send_home(return_out, return_in, return_send, return_recv, own, half, core, owners)
+    loads[3].wait()
+    for index in range(dps):
+        features_turned[index] = jnp.transpose(acts[index, :, :piece].astype(F32)).astype(BF)
     wait_home(outgoing, owners)
     total = mm(sel_ffn[...], return_in[0].reshape(rows, piece), 0, 0)
     total = total + mm(sel_ffn[...], return_in[1].reshape(rows, piece), 0, 0)
@@ -904,6 +944,11 @@
 
     each(owners, lambda step: head_copy(step).start())
     heads_in[own] = heads_out[own]
+    middle = columns * HD + HD
+    for index in range(dps):
+        cut = slice((index % 2) * piece, (index % 2 + 1) * piece)
+        outs = d_rows[index // 2, :, :, cut].reshape(rows, piece)
+        map_grads[index, :, middle:] = mm(outs, mixed[...], 0, 0).astype(BF)
 
     scale = HD ** (-0.5)
     key_pos = lax.broadcasted_iota(jnp.int32, (1, pairs.shape[1]), 1).astype(F32)
@@ -975,10 +1020,8 @@
     used, units = acts.shape[1], acts.shape[2]
     after, before = lax.rem(dp + 1, dps), lax.rem(dp + dps - 1, dps)
     facing = lax.rem(dp + 2, dps)
-    for copy in loads:
+    for copy in loads[:3]:
         copy.wait()
-    for index in range(dps):
-        features_turned[index] = jnp.transpose(acts[index, :, :piece].astype(F32)).astype(BF)
 
     class load:
         def __init__(self, side):
@@ -1004,15 +1047,10 @@
     def map_grad(index):
         cut = pl.ds(pl.multiple_of(lax.rem(index, 2) * piece, piece), piece)
         inputs = normed[lax.div(index, 2), :, :, cut].reshape(owners * group, piece)
-        outs = d_rows[lax.div(index, 2), :, :, cut].reshape(-1, piece)
-        return mm(inputs, d_proj[...], 0, 0), mm(outs, mixed[...], 0, 0)
-
-    middle = head_width + HD
+        return mm(inputs, d_proj[...], 0, 0)
 
     def keep_grad(index):
-        ins, outs = map_grad(index)
-        map_grads[index, :, :middle] = ins.astype(BF)
-        map_grads[index, :, middle:] = outs.astype(BF)
+        map_grads[index, :, :middle] = map_grad(index).astype(BF)
 
     cut = piece // 2
 
@@ -1058,9 +1096,9 @@
     step_copy(2).start()
     step_copy(3).start()
     hidden_ring.forward()
-    keep_grad(dp)
     both_ring.finish()
     load(0).start()
+    keep_grad(dp)
 
     tile = 2 * HD
     whole, rest = units // tile, units % tile
@@ -1076,9 +1114,9 @@
 
         def put(slot, value, size):
             if rows_first:
-                tall_tiles[slot, :size] = value
+                tall_tiles[slot, :size] = value.astype(BF)
             else:
-                wide_tiles[slot, :, :size] = value
+                wide_tiles[slot, :, :size] = value.astype(BF)
 
         def pair(index, carry):
             for slot in range(2):
@@ -1120,6 +1158,10 @@
             total = total + mm(acts[index, :, span], features[index], 0, 0)
         return total
 
+    load(0).wait()
+    unit_tiles(wide_product, gate_grad, False)
+    load(1).start()
+
     wait_home(outgoing, owners)
     total = jnp.zeros((group, piece), F32)
     for side in range(2):
@@ -1128,9 +1170,6 @@
     slices[share, 0] = total.astype(BF)
     slices[share, 1] = output_part[...]
     joining = share_start(slices, slice_send, slice_recv, own, share, shares)
-    load(0).wait()
-    unit_tiles(wide_product, gate_grad, False)
-    load(1).start()
 
     step_copy(2).wait()
     step_copy(3).wait()
@@ -1153,6 +1192,9 @@
 
     each(owners, lambda step: map_copy(step).start())
     maps_in[own] = map_grads[dp, home_rows(own), :]
+
+    load(1).wait()
+    unit_tiles(wide_product, up_grad, False)
 
     each(shares, lambda step: joining(step).wait())
     inv = inv_one[...]
@@ -1197,8 +1239,8 @@
         grad = gains[0:1, span] * slices[index, 0].astype(F32)
         value = tokens[:, span].astype(F32)
         input_grad[:, span] = input_grad[:, span] + inv * grad - value * mean
-    load(1).wait()
-    unit_tiles(wide_product, up_grad, False)
+    hidden_ring.finish()
+    load(2).start()
     each(owners, lambda step: gain_copy(step).wait())
     total = gain_in[0]
     for index in range(1, owners):
@@ -1206,8 +1248,6 @@
     gain_mid[...] = total
     each(dps, lambda step: far_gain_copy(step).start())
     gain_last[dp] = gain_mid[dp]
-    hidden_ring.finish()
-    load(2).start()
     load(2).wait()
     unit_tiles(tall_product, down_grad, True)
     each(dps, lambda step: far_gain_copy(step).wait())
@@ -1272,7 +1312,7 @@
     head_width = kv_weight.shape[2]
 
     kv_parts = jnp.transpose(kv_weight.reshape(local, 2, columns, HD), (2, 1, 0, 3))
-    pack_one = jnp.concatenate([kv_parts.reshape(owners, local, HD), query_weight], 2)
+    pack_one = kv_parts.reshape(owners, local, HD)
     own_gains = jnp.stack([attn_gain, ffn_gain]).astype(F32)
     own_gains = jnp.pad(own_gains, ((0, 8 - 2), (0, HD - local)))
     pack_two = jnp.swapaxes(out_weight, 1, 2)
@@ -1345,6 +1385,9 @@
             ((group, 8), F32),
         ],
         [
+            ((dps, owners * local, HD + head_width), BF),
+            ((dps, owners * local, head_width), BF),
+            ((2, owners, group, width // 2), BF),
             ((rows, TOPK * group), BF),
             ((2, dps, owners * used, piece), BF),
             ((2, owners, slots, width // 2), BF),
@@ -1366,7 +1409,7 @@
             ((dps, units, piece), BF),
             ((2, owners * used, units), F32),
         ],
-        [24, 24, 5, 2 * owners, 2 * owners]
+        [24, 24, 9, 3 * owners, 3 * owners]
         + [owners] * 4
         + [11, 11]
         + [owners] * 4
@@ -1380,6 +1423,7 @@
             marks,
             own_gains,
             pack_one,
+            query_weight,
             pack_two,
             gate_weight[0],
             up_weight[0],
@@ -1389,8 +1433,8 @@
             cos_key,
             sin_key,
         ],
-        far_args=(3, 4, 5, 6, 7),
-        far_outs=(14,),
+        far_args=(3, 4, 5, 6, 7, 8),
+        far_outs=(0, 1, 2, 14),
     )
 
     grad_width = head_width + HD + head_width
@@ -1411,9 +1455,9 @@
             ((group, width), F32),
             ((2, HD), F32),
             ((owners, local, grad_width), BF),
-            ((piece, units), F32),
-            ((piece, units), F32),
-            ((units, piece), F32),
+            ((piece, units), BF),
+            ((piece, units), BF),
+            ((units, piece), BF),
             ((dps, 2 * owners * used, units), BF),
             ((dps, owners * used, units), BF),
         ],
@@ -1449,8 +1493,8 @@
             ((dps, owners * used, piece), BF),
             ((dps, owners * used, units), BF),
             ((dps, piece, owners * used), BF),
-            ((2, piece, 2 * HD), F32),
-            ((2, 2 * HD, piece), F32),
+            ((2, piece, 2 * HD), BF),
+            ((2, 2 * HD, piece), BF),
         ],
         [
             3,
@@ -1528,9 +1572,9 @@
         out_grad,
         gain_grads[0],
         gain_grads[1],
-        gate_grad[None],
-        up_grad[None],
-        down_grad[None],
+        gate_grad[None].astype(F32),
+        up_grad[None].astype(F32),
+        down_grad[None].astype(F32),
     )
 
 

time: 401 us -> 393 us (0.980)
  the two profiles are of different devices: /device:TPU:1 before, /device:TPU:81 now
where the time goes in v6:
time: 393 us; the launch traced here: 386 us
  Pallas kernels  366 us (93%)
  other arithmetic  12.5 us (3%)
  local copies, waits for them, and re-layouts  5.93 us (2%)
    pallas_call x2, Pallas kernels, call_kernel(): pl.pallas_call(kernel, out_shape=[jax.ShapeDtypeStruct(shape, dtype) for...  366 us

profile of v6, /device:TPU:81, one launch (start us, length us, event | category | flops | bytes accessed | tf_op | source)
XLA Modules:
  0.0 385.8 jit_solution(7352920930003525537)
XLA Ops:
  0.6 0.7 convert_bitcast_fusion.2
  1.3 1.3 pad_maximum_fusion.marks
  2.6 1.0 reshape.49
  3.6 0.7 copy.27
  4.3 0.7 convert_bitcast_fusion.4
  5.0 0.7 broadcast_in_dim.6.lengths
  5.6 1.3 fusion.6.own_gains
  6.9 211.9 %shard_map.240 = (bf16[4,512,640]{2,1,0:T(8,128)(2,1)}, bf16[4,512,512]{2,1,0:T(8,128)(2,1)}, bf16[2,8,128,1024]{3,2,1,0:T(8,128)(2,1)}, f32[2,2048]{1,0:T(2,128...) custom-call(bf16[128,2048]{1,0:T(8,128)(2,1)} %bitcast.49, ...), custom_call_target="tpu_custom_call" | custom-call | tf_op jit(solution)/shard_map/pallas_call | solution.py:1268
  218.8 154.3 %shard_map.241 = (bf16[128,2048]{1,0:T(8,128)(2,1)}, f32[128,2048]{1,0:T(8,128)}, f32[2,128]{1,0:T(2,128)}, bf16[8,64,1152]{2,1,0:T(8,128)(2,1)}, bf16[512,1408]...) custom-call(bf16[2,2,8,48,512]{4,3,2,1,0:T(8,128)(2,1)} %get-tuple-e, ...), custom_call_target="tpu_custom_call" | custom-call | tf_op jit(solution)/shard_map/pallas_call | solution.py:1268
  373.1 0.0 copy-start.1
  373.1 3.5 bitcast_convert_fusion
  376.6 0.0 copy-done.1
  376.6 0.0 copy-start
  376.6 1.8 bitcast_convert_fusion.1
  378.4 0.1 copy-done
  378.5 0.0 copy-start.2
  378.5 1.8 bitcast_convert_fusion.2
  380.3 0.0 copy-done.2
  380.3 0.0 copy-start.5
  380.3 0.0 copy-start.4
  380.3 1.6 convert_bitcast_fusion
  381.9 0.0 copy-start.3
  381.9 0.2 copy.28
  382.1 0.9 reshape.52
  383.0 0.0 copy-done.5
  383.0 0.1 constant_dynamic-slice_fusion
  383.1 0.5 slice_bitcast_fusion
  383.6 0.0 copy-done.4
  383.6 0.8 copy.31
  384.4 0.0 copy-done.3
  384.4 1.0 copy.32
  (2 shorter events, 0.0 us)
Async XLA Ops:
  373.1 3.5 copy-start.1
  376.6 1.9 copy-start
  378.5 1.8 copy-start.2
  380.3 2.7 copy-start.5
  380.3 3.3 copy-start.4
  381.9 2.5 copy-start.3

commit v7 on v6

--- a/solution.py
+++ b/solution.py
@@ -205,6 +205,7 @@
     sibling,
     landing,
     landing_two,
+    sibling_two,
     slices,
     rows_out,
     grads_out,
@@ -567,7 +568,7 @@
                 side * head_rows : (side + 1) * head_rows, column * HD : (column + 1) * HD
             ] = mixed_in[2 * column + side]
 
-    def chip_start(product, base):
+    def chip_start(product, base, near, sibling):
         def across(side):
             place = base + side
             return remote(far.at[side], sibling.at[side], one_send.at[place], one_recv.at[place], other)
@@ -597,7 +598,7 @@
     def map_product(index):
         return mm(mixed[...], out_full[index], 1, 1).astype(BF).reshape(owners, slots, piece)
 
-    chip_start(map_product, 1)()
+    chip_start(map_product, 1, near, sibling)()
     outgoing = send_home(near, landing, home_send, home_recv, own, half, core, owners)
     up_ring.forward()
     wait_home(outgoing, owners)
@@ -699,7 +700,7 @@
     unit_tiles(up_tile)
     down_ring.finish()
     each(dps, lambda step: feature_copy(step).start())
-    finish_sum = chip_start(lambda index: loose(mm(hidden[...], down[index])), 7)
+    finish_sum = chip_start(lambda index: loose(mm(hidden[...], down[index])), 7, near, sibling)
 
     def grad_tile(cut):
         grad = mm(features[1, 0], down[0, cut, :], 1, 1)
@@ -715,9 +716,12 @@
     outgoing_two = send_home(
         near, landing_two, home_two_send, home_two_recv, own, half, core, owners
     )
-    for index in range(dps):
-        total = mm(d_both[0], gate_up[0, index], 1, 1) + mm(d_both[1], gate_up[1, index], 1, 1)
-        d_parts[index % 2, index // 2] = loose(total)
+
+    def input_product(index):
+        total = mm(d_both[0], gate_up[0, index], 1, 1)
+        return loose(total + mm(d_both[1], gate_up[1, index], 1, 1))
+
+    finish_parts = chip_start(input_product, 11, d_parts, sibling_two)
     keep.wait()
     each(dps, lambda step: feature_copy(step).wait())
     across = remote(
@@ -728,6 +732,7 @@
     rest = at_tokens(pick_ffn, 6, landing_two)
     span = pl.ds(pl.multiple_of(share * piece, piece), piece)
     output_part[...] = (state[:, span] + rest).astype(BF)
+    finish_parts()
     across.wait()
     for copy in kept:
         copy.wait()
@@ -864,14 +869,7 @@
     hidden_ring = Ring(hidden_all, ring_send, ring_recv, 4, dp, dps)
     hidden_ring.start(hidden)
 
-    used_slots = pl.ds(0, slots)
-    return_near, return_out = sibling.at[:, :, used_slots], near.at[:, :, used_slots]
-    across = remote(parts.at[1 - core], return_near, first_send.at[0], first_recv.at[0], other)
-    across.start()
-    across.wait()
-    for side in range(2):
-        return_out[side] = (parts[core, side].astype(F32) + return_near[side].astype(F32)).astype(BF)
-    outgoing = send_home(return_out, return_in, return_send, return_recv, own, half, core, owners)
+    outgoing = send_home(parts, return_in, return_send, return_recv, own, half, core, owners)
     loads[3].wait()
     for index in range(dps):
         features_turned[index] = jnp.transpose(acts[index, :, :piece].astype(F32)).astype(BF)
@@ -1378,7 +1376,7 @@
             ((2, dps, owners * used, piece), BF),
             ((owners * used, units), BF),
             ((2, owners * used, units), BF),
-            ((2,) + block, BF),
+            (block, BF),
             ((group, piece), BF),
             ((rows, group), BF),
             ((rows, TOPK * group), BF),
@@ -1400,7 +1398,7 @@
             ((owners, head_rows, HD), BF),
             ((owners, head_rows, HD), BF),
         ]
-        + [(block, BF)] * 5
+        + [(block, BF)] * 6
         + [
             ((shares, group, piece), BF),
             ((owners, slots, width // 2), BF),
@@ -1411,7 +1409,7 @@
         ],
         [24, 24, 9, 3 * owners, 3 * owners]
         + [owners] * 4
-        + [11, 11]
+        + [13, 13]
         + [owners] * 4
         + [2 * owners] * 4
         + [shares, shares]

time: 393 us -> 393 us (level)
  the two profiles are of different devices: /device:TPU:81 before, /device:TPU:68 now
where the time goes in v7:
time: 393 us; the launch traced here: 386 us
  Pallas kernels  366 us (93%)
  other arithmetic  12.5 us (3%)
  local copies, waits for them, and re-layouts  5.93 us (2%)
    pallas_call x2, Pallas kernels, call_kernel(): pl.pallas_call(kernel, out_shape=[jax.ShapeDtypeStruct(shape, dtype) for...  366 us

profile of v7, /device:TPU:68, one launch (start us, length us, event | category | flops | bytes accessed | tf_op | source)
XLA Modules:
  0.0 385.7 jit_solution(14487448005633007583)
XLA Ops:
  0.6 0.7 convert_bitcast_fusion.2
  1.3 1.3 pad_maximum_fusion.marks
  2.6 1.0 reshape.49
  3.6 0.7 copy.27
  4.3 0.7 convert_bitcast_fusion.4
  5.0 0.7 broadcast_in_dim.6.lengths
  5.6 1.3 fusion.6.own_gains
  6.9 211.1 %shard_map.240 = (bf16[4,512,640]{2,1,0:T(8,128)(2,1)}, bf16[4,512,512]{2,1,0:T(8,128)(2,1)}, bf16[2,8,128,1024]{3,2,1,0:T(8,128)(2,1)}, f32[2,2048]{1,0:T(2,128...) custom-call(bf16[128,2048]{1,0:T(8,128)(2,1)} %bitcast.49, ...), custom_call_target="tpu_custom_call" | custom-call | tf_op jit(solution)/shard_map/pallas_call | solution.py:1266
  218.1 155.0 %shard_map.241 = (bf16[128,2048]{1,0:T(8,128)(2,1)}, f32[128,2048]{1,0:T(8,128)}, f32[2,128]{1,0:T(2,128)}, bf16[8,64,1152]{2,1,0:T(8,128)(2,1)}, bf16[512,1408]...) custom-call(bf16[2,8,48,512]{3,2,1,0:T(8,128)(2,1)} %get-tuple-eleme, ...), custom_call_target="tpu_custom_call" | custom-call | tf_op jit(solution)/shard_map/pallas_call | solution.py:1266
  373.0 0.0 copy-start.1
  373.0 3.5 bitcast_convert_fusion
  376.5 0.0 copy-done.1
  376.5 0.0 copy-start
  376.5 1.8 bitcast_convert_fusion.1
  378.3 0.1 copy-done
  378.4 0.0 copy-start.2
  378.4 1.8 bitcast_convert_fusion.2
  380.2 0.0 copy-done.2
  380.2 0.0 copy-start.5
  380.2 0.0 copy-start.4
  380.2 1.6 convert_bitcast_fusion
  381.8 0.0 copy-start.3
  381.8 0.2 copy.28
  382.0 0.9 reshape.52
  382.9 0.0 copy-done.5
  382.9 0.1 constant_dynamic-slice_fusion
  383.0 0.5 slice_bitcast_fusion
  383.5 0.0 copy-done.4
  383.5 0.8 copy.31
  384.3 0.0 copy-done.3
  384.3 1.0 copy.32
  (2 shorter events, 0.0 us)
Async XLA Ops:
  373.0 3.5 copy-start.1
  376.5 1.9 copy-start
  378.4 1.8 copy-start.2
  380.2 2.7 copy-start.5
  380.2 3.3 copy-start.4
  381.8 2.5 copy-start.3
